TPU v7x, 32 devices: a whole 2x2x4 slice. The times are simulated.
32 devices in a mesh: dp: 8 (over y, x, core), head: 4 (over z).
Axes of the slice: x: 2, y: 2, z: 4, core: 2. Of those that a mesh axis runs over, the one named last changes fastest.
Arguments:
- tokens: bfloat16 [2, 8, 1024, 1536], P(None, 'dp', 'head'), may hold values from -6 to 6
- lengths: int32 [2, 8], P(None, 'dp'), may hold values from 128 to 1024, as said below
- cotangent: bfloat16 [2, 8, 1024, 1536], P(None, 'dp', 'head'), may hold values from -6 to 6
- q_weight: bfloat16 [1536, 1536], P('dp', 'head'), may hold values from -0.15625 to 0.15625
- k_weight: bfloat16 [1536, 1536], P('dp', 'head'), may hold values from -0.15625 to 0.15625
- v_weight: bfloat16 [1536, 1536], P('dp', 'head'), may hold values from -0.15625 to 0.15625
- direction_weight: bfloat16 [1536, 1536], P('dp', 'head'), may hold values from -0.15625 to 0.15625
- beta_weight: bfloat16 [1536, 12], P('dp', 'head'), may hold values from -0.15625 to 0.15625
- out_weight: bfloat16 [1536, 1536], P('head', 'dp'), may hold values from -2.5 to 2.5
- gate_weight: bfloat16 [1536, 4096], P('dp', 'head'), may hold values from -0.15625 to 0.15625
- up_weight: bfloat16 [1536, 4096], P('dp', 'head'), may hold values from -0.15625 to 0.15625
- down_weight: bfloat16 [4096, 1536], P('head', 'dp'), may hold values from -0.09375 to 0.09375
- norm_gain_one: bfloat16 [1536], P('dp'), may hold values from 0.5 to 1.5
- norm_gain_two: bfloat16 [1536], P('dp'), may hold values from 0.5 to 1.5
Outputs:
- block_out: bfloat16 [2, 8, 1024, 1536], P(None, 'dp', 'head')
- input_grad: float32 [2, 8, 1024, 1536], P(None, 'dp', 'head')
- q_weight_grad: float32 [1536, 1536], P('dp', 'head')
- k_weight_grad: float32 [1536, 1536], P('dp', 'head')
- v_weight_grad: float32 [1536, 1536], P('dp', 'head')
- direction_weight_grad: float32 [1536, 1536], P('dp', 'head')
- beta_weight_grad: float32 [1536, 12], P('dp', 'head')
- out_weight_grad: float32 [1536, 1536], P('head', 'dp')
- gate_weight_grad: float32 [1536, 4096], P('dp', 'head')
- up_weight_grad: float32 [1536, 4096], P('dp', 'head')
- down_weight_grad: float32 [4096, 1536], P('head', 'dp')
- norm_gain_one_grad: float32 [1536], P('dp')
- norm_gain_two_grad: float32 [1536], P('dp')
Inputs may be any that keep to these rules, and one draw needn't show every extreme that they name: `lengths`: within each aligned group of 1 slots, taken over all 2 micro-batches together, one slot is full (1024 valid tokens).
All inputs are finite; a program needn't handle non-finite values.
Results may differ from a plain program's by a relative error of at most 0.022.
Values may be sent and summed in bfloat16 or wider, within the bound.
No kernel may reach another device: no remote copies, remote signals or barrier semaphores. Data moves between devices by JAX's collectives and lax.ppermute only.
A program may use at most 448 MiB of HBM per device.

v0:
```python
import jax
import jax.numpy as jnp
from jax import lax
from jax.sharding import PartitionSpec as P

HEAD_DIM = 128
SPAN = 64


def einsum_high(formula, left_side, right_side):
    return jnp.einsum(formula, left_side, right_side, precision=lax.Precision.HIGHEST)


def householder_attention(queries, key_rows, values, raw_directions, beta_logits, length):
    seq_len, head_size = queries.shape
    block_size = SPAN
    blocks = seq_len // block_size
    position = jnp.arange(seq_len, dtype=jnp.int32)
    live_mask = (position < length).astype(jnp.float32)
    directions = raw_directions * lax.rsqrt(
        jnp.sum(raw_directions * raw_directions, axis=-1, keepdims=True) + 1e-06
    )
    strength = jax.nn.sigmoid(beta_logits) * live_mask
    query_blocks = queries.reshape(blocks, block_size, head_size)
    key_blocks = key_rows.reshape(blocks, block_size, head_size)
    direction_blocks = directions.reshape(blocks, block_size, head_size)
    strength_blocks = strength.reshape(blocks, block_size)
    inner_index = jnp.arange(block_size, dtype=jnp.int32)
    strict_below = (inner_index[:, None] > inner_index[None, :]).astype(jnp.float32)
    upto_mask = (inner_index[:, None] >= inner_index[None, :]).astype(jnp.float32)
    direction_gram = einsum_high("nsd,ntd->nst", direction_blocks, direction_blocks)
    negated = -(strength_blocks[:, :, None] * direction_gram * strict_below)
    inverse = jnp.eye(block_size, dtype=jnp.float32)[None, :, :] + negated
    power_term = negated
    for doubling in range(1, (block_size - 1).bit_length()):
        power_term = einsum_high("nst,ntu->nsu", power_term, power_term)
        inverse = inverse + einsum_high("nst,ntu->nsu", inverse, power_term)
    query_direction = einsum_high("nid,ntd->nit", query_blocks, direction_blocks) * upto_mask
    direction_key = einsum_high("nsd,njd->nsj", direction_blocks, key_blocks) * strict_below
    weighted = strength_blocks[:, :, None]
    update_rows = einsum_high("nts,nsd->ntd", inverse, weighted * direction_blocks)
    update_keys = einsum_high("nts,nsj->ntj", inverse, weighted * direction_key)
    moved_queries = query_blocks - einsum_high("nit,ntd->nid", query_direction, update_rows)
    moved_keys = key_blocks - einsum_high("ntj,ntd->njd", update_keys, direction_blocks)
    local_scores = einsum_high("nid,njd->nij", query_blocks, key_blocks) - einsum_high(
        "nit,ntj->nij", query_direction, update_keys
    )
    scale = head_size ** (-0.5)

    def advance(carried, block_items):
        block_queries, block_keys, block_rows, block_directions, block_local, start_row = (
            block_items
        )
        across = einsum_high("id,jd->ij", block_queries, carried)
        across = lax.dynamic_update_slice_in_dim(across, block_local, start_row, 1)
        row_position = start_row + inner_index
        allowed = (position[None, :] <= row_position[:, None]) & (position[None, :] < length)
        scores = jnp.where(allowed, across * scale, -1e30)
        row_max = jnp.max(scores, axis=-1, keepdims=True)
        weights = jnp.exp(scores - row_max)
        weights = weights / jnp.sum(weights, axis=-1, keepdims=True)
        block_out = einsum_high("ij,jd->id", weights, values)
        carried = carried - einsum_high(
            "jt,td->jd", einsum_high("jd,td->jt", carried, block_rows), block_directions
        )
        carried = lax.dynamic_update_slice_in_dim(carried, block_keys, start_row, 0)
        return (carried, block_out)

    starts = jnp.arange(blocks, dtype=jnp.int32) * block_size
    initial = jnp.zeros((seq_len, head_size), jnp.float32)
    _, attended = lax.scan(
        jax.checkpoint(advance),
        initial,
        (moved_queries, moved_keys, update_rows, direction_blocks, local_scores, starts),
    )
    return attended.reshape(seq_len, head_size)


def attend_all(queries, key_rows, values, raw_directions, beta_logits, seq_lengths):
    per_head = jax.vmap(householder_attention, in_axes=(1, 1, 1, 1, 1, None), out_axes=1)
    return jax.vmap(per_head)(queries, key_rows, values, raw_directions, beta_logits, seq_lengths)


def root_norm(features, scales):
    return (
        features * lax.rsqrt(jnp.mean(features * features, axis=-1, keepdims=True) + 1e-06) * scales
    )


def product(left_side, right_side):
    return jnp.dot(left_side, right_side, preferred_element_type=jnp.float32)


def by_transposed(left_side, right_side):
    return lax.dot_general(
        left_side, right_side, (((1,), (1,)), ((), ())), preferred_element_type=jnp.float32
    )


def transposed_by(left_side, right_side):
    return lax.dot_general(
        left_side, right_side, (((0,), (0,)), ((), ())), preferred_element_type=jnp.float32
    )


def round_trip(values):
    return lax.optimization_barrier(values.astype(jnp.bfloat16)).astype(jnp.float32)


def fetch_weights(shards):
    return (
        lax.all_gather(shards[0], "dp", axis=0, tiled=True),
        lax.all_gather(shards[1], "dp", axis=0, tiled=True),
        lax.all_gather(shards[2], "dp", axis=0, tiled=True),
        lax.all_gather(shards[3], "dp", axis=0, tiled=True),
        lax.all_gather(shards[4], "dp", axis=0, tiled=True),
        lax.all_gather(shards[5], "dp", axis=1, tiled=True),
        lax.all_gather(shards[6], "dp", axis=0, tiled=True),
        lax.all_gather(shards[7], "dp", axis=0, tiled=True),
        lax.all_gather(shards[8], "dp", axis=1, tiled=True),
        lax.all_gather(shards[9], "dp", axis=0, tiled=True),
        lax.all_gather(shards[10], "dp", axis=0, tiled=True),
    )


def fetch_again(shards):
    return (
        lax.all_gather(shards[0], "dp", axis=0, tiled=True),
        lax.all_gather(shards[1], "dp", axis=0, tiled=True),
        lax.all_gather(shards[2], "dp", axis=0, tiled=True),
        lax.all_gather(shards[3], "dp", axis=0, tiled=True),
        lax.all_gather(shards[4], "dp", axis=0, tiled=True),
        lax.all_gather(shards[5], "dp", axis=1, tiled=True),
        lax.all_gather(shards[6], "dp", axis=0, tiled=True),
        lax.all_gather(shards[7], "dp", axis=0, tiled=True),
        lax.all_gather(shards[8], "dp", axis=1, tiled=True),
        lax.all_gather(shards[9], "dp", axis=0, tiled=True),
        lax.all_gather(shards[10], "dp", axis=0, tiled=True),
    )


def gather_rows(local_rows):
    return lax.all_gather(local_rows, "head", axis=1, tiled=True)


def scatter_rows(partial_rows):
    return lax.psum_scatter(
        partial_rows.astype(jnp.bfloat16), "head", scatter_dimension=1, tiled=True
    ).astype(jnp.float32)


def gather_grads(local_rows):
    return lax.all_gather(local_rows, "head", axis=1, tiled=True)


def scatter_grads(partial_rows):
    return lax.psum_scatter(
        partial_rows.astype(jnp.bfloat16), "head", scatter_dimension=1, tiled=True
    ).astype(jnp.float32)


def reduce_grads(terms):
    return (
        lax.psum_scatter(
            terms[0].astype(jnp.bfloat16), "dp", scatter_dimension=0, tiled=True
        ).astype(jnp.float32),
        lax.psum_scatter(
            terms[1].astype(jnp.bfloat16), "dp", scatter_dimension=0, tiled=True
        ).astype(jnp.float32),
        lax.psum_scatter(
            terms[2].astype(jnp.bfloat16), "dp", scatter_dimension=0, tiled=True
        ).astype(jnp.float32),
        lax.psum_scatter(
            terms[3].astype(jnp.bfloat16), "dp", scatter_dimension=0, tiled=True
        ).astype(jnp.float32),
        lax.psum_scatter(
            terms[4].astype(jnp.bfloat16), "dp", scatter_dimension=0, tiled=True
        ).astype(jnp.float32),
        lax.psum_scatter(
            terms[5].astype(jnp.bfloat16), "dp", scatter_dimension=1, tiled=True
        ).astype(jnp.float32),
        lax.psum_scatter(
            terms[6].astype(jnp.bfloat16), "dp", scatter_dimension=0, tiled=True
        ).astype(jnp.float32),
        lax.psum_scatter(
            terms[7].astype(jnp.bfloat16), "dp", scatter_dimension=0, tiled=True
        ).astype(jnp.float32),
        lax.psum_scatter(
            terms[8].astype(jnp.bfloat16), "dp", scatter_dimension=1, tiled=True
        ).astype(jnp.float32),
    )


def body(
    tokens,
    lengths,
    cotangent,
    q_weight,
    k_weight,
    v_weight,
    direction_weight,
    beta_weight,
    out_weight,
    gate_weight,
    up_weight,
    down_weight,
    norm_gain_one,
    norm_gain_two,
):
    shards = (
        q_weight,
        k_weight,
        v_weight,
        direction_weight,
        beta_weight,
        out_weight,
        gate_weight,
        up_weight,
        down_weight,
        norm_gain_one,
        norm_gain_two,
    )
    micro_count = tokens.shape[0]
    kept_state = []
    outputs = []
    for micro_index in range(micro_count):
        gathered = fetch_weights(shards)
        rows_in = tokens[micro_index].astype(jnp.float32)
        gain_first = gathered[9].astype(jnp.float32)
        gain_second = gathered[10].astype(jnp.float32)
        first_rows = gather_rows(root_norm(rows_in, gain_first).astype(jnp.bfloat16))
        seq_count, seq_len, width = first_rows.shape
        first_flat = first_rows.reshape(-1, width)
        queries = product(first_flat, gathered[0]).astype(jnp.bfloat16)
        key_rows = product(first_flat, gathered[1]).astype(jnp.bfloat16)
        values = product(first_flat, gathered[2]).astype(jnp.bfloat16)
        raw_directions = product(first_flat, gathered[3]).astype(jnp.bfloat16)
        beta_logits = product(first_flat, gathered[4])
        heads_here = queries.shape[1] // HEAD_DIM
        head_shape = (seq_count, seq_len, heads_here, HEAD_DIM)
        mixed = attend_all(
            queries.astype(jnp.float32).reshape(head_shape),
            key_rows.astype(jnp.float32).reshape(head_shape),
            values.astype(jnp.float32).reshape(head_shape),
            raw_directions.astype(jnp.float32).reshape(head_shape),
            beta_logits.reshape(seq_count, seq_len, heads_here),
            lengths[micro_index],
        )
        attended = mixed.reshape(-1, heads_here * HEAD_DIM).astype(jnp.bfloat16)
        middle = rows_in + scatter_rows(
            product(attended, gathered[5]).reshape(seq_count, seq_len, width)
        )
        second_rows = gather_rows(root_norm(middle, gain_second).astype(jnp.bfloat16))
        second_flat = second_rows.reshape(-1, width)
        gate_values = product(second_flat, gathered[6])
        up_values = product(second_flat, gathered[7])
        hidden = (jax.nn.silu(gate_values) * up_values).astype(jnp.bfloat16)
        block_out = middle + scatter_rows(
            product(hidden, gathered[8]).reshape(seq_count, seq_len, width)
        )
        outputs.append(block_out.astype(jnp.bfloat16))
        kept_state.append(
            (
                rows_in,
                first_flat,
                queries,
                key_rows,
                values,
                raw_directions,
                beta_logits,
                attended,
                middle,
                second_flat,
                gate_values,
                up_values,
                hidden,
            )
        )
    sharded_total = None
    gain_first_total = None
    gain_second_total = None
    input_grads = []
    for micro_index in range(micro_count):
        gathered = fetch_again(shards)
        (
            rows_in,
            first_flat,
            queries,
            key_rows,
            values,
            raw_directions,
            beta_logits,
            attended,
            middle,
            second_flat,
            gate_values,
            up_values,
            hidden,
        ) = kept_state[micro_index]
        gain_first = gathered[9].astype(jnp.float32)
        gain_second = gathered[10].astype(jnp.float32)
        cotangent_rows = cotangent[micro_index]
        upstream = gather_grads(cotangent_rows)
        seq_count, seq_len, width = upstream.shape
        upstream_flat = upstream.reshape(-1, width)
        hidden_grad = by_transposed(upstream_flat, gathered[8])
        down_term = transposed_by(hidden, upstream_flat)
        sigmoid_gate = jax.nn.sigmoid(gate_values)
        gate_grad = (
            hidden_grad * up_values * sigmoid_gate * (1.0 + gate_values * (1.0 - sigmoid_gate))
        ).astype(jnp.bfloat16)
        up_grad = (hidden_grad * gate_values * sigmoid_gate).astype(jnp.bfloat16)
        gate_term = transposed_by(second_flat, gate_grad)
        up_term = transposed_by(second_flat, up_grad)
        second_partial = by_transposed(gate_grad, gathered[6]) + by_transposed(up_grad, gathered[7])
        second_grad = scatter_grads(second_partial.reshape(seq_count, seq_len, width))
        _, second_pull = jax.vjp(root_norm, middle, gain_second)
        middle_part, gain_second_part = second_pull(second_grad)
        middle_grad = cotangent_rows.astype(jnp.float32) + middle_part
        middle_rows = gather_grads(middle_grad.astype(jnp.bfloat16))
        middle_flat = middle_rows.reshape(-1, width)
        out_term = transposed_by(attended, middle_flat)
        attended_grad = round_trip(by_transposed(middle_flat, gathered[5]))
        heads_here = queries.shape[1] // HEAD_DIM
        head_shape = (seq_count, seq_len, heads_here, HEAD_DIM)
        slot_lengths = lengths[micro_index]

        def attention_inputs(query_part, key_part, value_part, direction_part, logit_part):
            return attend_all(
                query_part, key_part, value_part, direction_part, logit_part, slot_lengths
            )

        _, attention_pull = jax.vjp(
            attention_inputs,
            queries.astype(jnp.float32).reshape(head_shape),
            key_rows.astype(jnp.float32).reshape(head_shape),
            values.astype(jnp.float32).reshape(head_shape),
            raw_directions.astype(jnp.float32).reshape(head_shape),
            beta_logits.reshape(seq_count, seq_len, heads_here),
        )
        query_grad, key_grad, value_grad, direction_grad, logit_grad = attention_pull(
            attended_grad.reshape(head_shape)
        )
        query_grad = query_grad.reshape(-1, heads_here * HEAD_DIM).astype(jnp.bfloat16)
        key_grad = key_grad.reshape(-1, heads_here * HEAD_DIM).astype(jnp.bfloat16)
        value_grad = value_grad.reshape(-1, heads_here * HEAD_DIM).astype(jnp.bfloat16)
        direction_grad = direction_grad.reshape(-1, heads_here * HEAD_DIM).astype(jnp.bfloat16)
        logit_grad = logit_grad.reshape(-1, heads_here).astype(jnp.bfloat16)
        first_partial = (
            by_transposed(query_grad, gathered[0])
            + by_transposed(key_grad, gathered[1])
            + by_transposed(value_grad, gathered[2])
            + by_transposed(direction_grad, gathered[3])
            + by_transposed(logit_grad, gathered[4])
        )
        first_grad = scatter_grads(first_partial.reshape(seq_count, seq_len, width))
        _, first_pull = jax.vjp(root_norm, rows_in, gain_first)
        input_part, gain_first_part = first_pull(first_grad)
        input_grads.append(middle_grad + input_part)
        weight_terms = (
            transposed_by(first_flat, query_grad),
            transposed_by(first_flat, key_grad),
            transposed_by(first_flat, value_grad),
            transposed_by(first_flat, direction_grad),
            transposed_by(first_flat, logit_grad),
            out_term,
            gate_term,
            up_term,
            down_term,
        )
        reduced = reduce_grads(weight_terms)
        sharded_total = (
            reduced if sharded_total is None else jax.tree.map(jnp.add, sharded_total, reduced)
        )
        gain_first_total = (
            gain_first_part if gain_first_total is None else gain_first_total + gain_first_part
        )
        gain_second_total = (
            gain_second_part if gain_second_total is None else gain_second_total + gain_second_part
        )
    gain_first_sum, gain_second_sum = lax.psum(
        (gain_first_total, gain_second_total), ("dp", "head")
    )
    shard_width = norm_gain_one.shape[0]
    shard_start = lax.axis_index("dp") * shard_width
    gain_first_grad = lax.dynamic_slice_in_dim(gain_first_sum, shard_start, shard_width)
    gain_second_grad = lax.dynamic_slice_in_dim(gain_second_sum, shard_start, shard_width)
    return (
        jnp.stack(outputs),
        jnp.stack(input_grads),
        sharded_total[0],
        sharded_total[1],
        sharded_total[2],
        sharded_total[3],
        sharded_total[4],
        sharded_total[5],
        sharded_total[6],
        sharded_total[7],
        sharded_total[8],
        gain_first_grad,
        gain_second_grad,
    )


def solution(mesh):
    in_specs = (
        P(None, "dp", "head", None),
        P(None, "dp"),
        P(None, "dp", "head", None),
        P("dp", "head"),
        P("dp", "head"),
        P("dp", "head"),
        P("dp", "head"),
        P("dp", "head"),
        P("head", "dp"),
        P("dp", "head"),
        P("dp", "head"),
        P("head", "dp"),
        P("dp"),
        P("dp"),
    )
    out_specs = (
        P(None, "dp", "head", None),
        P(None, "dp", "head", None),
        P("dp", "head"),
        P("dp", "head"),
        P("dp", "head"),
        P("dp", "head"),
        P("dp", "head"),
        P("head", "dp"),
        P("dp", "head"),
        P("dp", "head"),
        P("head", "dp"),
        P("dp"),
        P("dp"),
    )
    return jax.shard_map(body, mesh=mesh, in_specs=in_specs, out_specs=out_specs, check_vma=False)
```

profile of v0, /device:TPU:0, one launch (start us, length us, event | category | flops | bytes accessed | tf_op | source)
XLA Modules:
  0.0 4736.9 jit_solution(881060413060653328)
XLA Ops:
  11.6 16.1 all-reduce.3
  37.4 7.9 all-gather.2
  47.4 55.2 %all-gather.40.cloned.1.call-done = bf16[1,1024,1536]{2,1,0:T(8,128)(2,1)} async-done(((bf16[1,256,1536]{2,1,0:T(8,128)(2,1)}), bf16[1,1024,1536]{2,1,0:T(8,128)(2,1)}) %all-gather.40.cloned.1.call-update) | async-done | bytes 3145744 | tf_op jit(solution)/shard_map/all_gather | solution.py:143
  185.6 392.0 %while.125 = (s32[]{:T(128)}, f32[1,3,1024,128]{3,2,1,0:T(8,128)S(1)}, bf16[16,1,3,64,128]{4,3,0,2,1:T(8,128)(2,1)}, f32[16,1,3,64,128]{4,3,2,1,0:T(8,128)}, f32...) while((s32[]{:T(128)}, ...), condition=%wide.region_18.19_spmd.clone.clone, body=%wide.region_13.18_spmd.clone.clone.sunk | while | flops 1210684160 | bytes 20275832 | solution.py:71
  601.2 5.0 fusion.217
  664.6 379.4 %while.124 = (s32[]{:T(128)}, f32[1,3,1024,128]{3,2,1,0:T(8,128)S(1)}, bf16[16,1,3,64,128]{4,3,0,2,1:T(8,128)(2,1)S(1)}, f32[16,1,3,64,128]{4,3,2,1,0:T(8,128)},...) while((s32[]{:T(128)}, ...), condition=%wide.region_7.8_spmd.clone.clone, body=%wide.region_2.7_spmd.clone.clone.sunk | while | flops 1210684160 | bytes 20277884 | solution.py:71
  1049.9 59.6 %reduce-scatter.31.cloned.1.call-done = bf16[1,256,1536]{2,1,0:T(8,128)(2,1)} async-done(((bf16[1,1024,1536]{2,1,0:T(8,128)(2,1)}), bf16[1,256,1536]{2,1,0:T(8,128)(2,1)}) %reduce-scatter.31.cloned.1.call-update) | async-done | bytes 786448 | tf_op jit(solution)/shard_map/reduce_scatter | solution.py:147
  1118.3 25.2 all-gather.36.cloned.1.call-done
  1143.5 65.7 %all-gather.42.cloned.1.call-done = bf16[1,1024,1536]{2,1,0:T(8,128)(2,1)} async-done(((bf16[1,256,1536]{2,1,0:T(8,128)(2,1)}), bf16[1,1024,1536]{2,1,0:T(8,128)(2,1)}) %all-gather.42.cloned.1.call-update) | async-done | bytes 3145744 | tf_op jit(solution)/shard_map/all_gather | solution.py:143
  1209.2 8.3 fusion.234
  1217.6 24.4 all-gather.34.cloned.1.call-done
  1242.0 8.2 fusion.236
  1250.2 57.4 %all-gather.50.cloned.1.call-done = bf16[1,1,1024,1536]{3,2,1,0:T(8,128)(2,1)} async-done(((bf16[1,1,256,1536]{3,2,1,0:T(8,128)(2,1)}), bf16[1,1,1024,1536]{3,2,1,0:T(8,128)(2,1)}) %all-gather.50.cloned.1.call-update) | async-done | bytes 3145744 | tf_op jit(solution)/shard_map/all_gather | solution.py:153
  1307.6 32.7 all-gather.38.cloned.1.call-done
  1340.4 11.7 multiply_convert_fusion
  1355.6 5.3 fusion.212
  1361.0 44.9 all-gather.32.cloned.1.call-done
  1405.9 8.5 fusion.260
  1414.4 5.0 fusion.262
  1419.4 50.2 %all-gather.48.cloned.1.call-done = bf16[1,1,1024,1536]{3,2,1,0:T(8,128)(2,1)} async-done(((bf16[1,1,256,1536]{3,2,1,0:T(8,128)(2,1)}), bf16[1,1,1024,1536]{3,2,1,0:T(8,128)(2,1)}) %all-gather.48.cloned.1.call-update) | async-done | bytes 3145744 | tf_op jit(solution)/shard_map/all_gather | solution.py:153
  1469.5 11.7 multiply_convert_fusion.2
  1484.7 4.9 fusion.210
  1489.7 7.6 fusion.215
  1497.5 33.1 reduce-scatter.43.cloned.1.call-done
  1530.6 63.0 %reduce-scatter.39.cloned.1.call-done = bf16[1,256,1536]{2,1,0:T(8,128)(2,1)} async-done(((bf16[1,1024,1536]{2,1,0:T(8,128)(2,1)}), bf16[1,256,1536]{2,1,0:T(8,128)(2,1)}) %reduce-scatter.39.cloned.1.call-update) | async-done | bytes 786448 | tf_op jit(solution)/shard_map/reduce_scatter | solution.py:157
  1597.0 59.3 %reduce-scatter.37.cloned.1.call-done = bf16[1,256,1536]{2,1,0:T(8,128)(2,1)} async-done(((bf16[1,1024,1536]{2,1,0:T(8,128)(2,1)}), bf16[1,256,1536]{2,1,0:T(8,128)(2,1)}) %reduce-scatter.37.cloned.1.call-update) | async-done | bytes 786448 | tf_op jit(solution)/shard_map/reduce_scatter | solution.py:147
  1660.9 7.6 convolution_convert_fusion.4
  1670.7 6.5 convolution_convert_fusion.5
  1679.1 6.5 convolution_convert_fusion.6
  1687.5 6.5 convolution_convert_fusion.7
  1694.3 11.5 broadcast.1138.clone.1
  1706.4 223.3 %while.123 = (s32[]{:T(128)}, f32[1,3,1024,128]{3,2,1,0:T(8,128)S(1)}, f32[16,1,3,1024,128]{4,3,2,1,0:T(8,128)}, f32[16,1,3,64,128]{4,3,2,1,0:T(8,128)}, f32[16,...) while((s32[]{:T(128)}, ...), condition=%wide.region_46.47_spmd, body=%wide.region_44.46_spmd.sunk | while | flops 604397568 | bytes 10127085 | solution.py:71
  1929.7 7.8 convolution_convert_fusion.2
  1938.0 12.6 broadcast.1138.clone
  1950.8 223.2 %while.122 = (s32[]{:T(128)}, f32[1,3,1024,128]{3,2,1,0:T(8,128)S(1)}, f32[16,1,3,1024,128]{4,3,2,1,0:T(8,128)}, f32[16,1,3,64,128]{4,3,2,1,0:T(8,128)}, f32[16,...) while((s32[]{:T(128)}, ...), condition=%wide.region_26.27_spmd, body=%wide.region_24.26_spmd.sunk | while | flops 604397568 | bytes 10127085 | solution.py:71
  2174.0 7.7 convolution_convert_fusion.3
  2195.3 835.0 %while.127 = (s32[]{:T(128)}, f32[1,3,1024,128]{2,3,1,0:T(8,128)}, f32[1,3,1024,128]{3,2,1,0:T(8,128)}, f32[16,1,3,64,128]{4,3,0,2,1:T(8,128)}, f32[16,1,3,64,12...) while((s32[]{:T(128)}, f32[1,3,1024,128]{2,3,1,0:T(8,128)}, ...), condition=%wide.region_55.56_spmd.clone, body=%wide.region_47.55_spmd.clone.sunk | while | flops 3030107392 | bytes 76875968 | solution.py:71
  3122.1 832.2 %while.126 = (s32[]{:T(128)}, f32[1,3,1024,128]{2,3,1,0:T(8,128)}, f32[1,3,1024,128]{3,2,1,0:T(8,128)}, f32[16,1,3,64,128]{4,3,0,2,1:T(8,128)}, f32[16,1,3,64,12...) while((s32[]{:T(128)}, f32[1,3,1024,128]{2,3,1,0:T(8,128)}, ...), condition=%wide.region_35.36_spmd.clone, body=%wide.region_27.35_spmd.clone.sunk | while | flops 3030107392 | bytes 76875968 | solution.py:71
  4024.2 4.7 fusion.574
  4065.2 5.1 fusion.305
  4070.3 4.7 fusion.420
  4095.9 4.7 fusion.302
  4103.3 4.8 fusion.290
  4116.7 5.0 fusion.299
  4130.6 5.0 fusion.287
  4143.4 5.2 fusion.296
  4153.4 5.1 fusion.284
  4158.5 4.8 fusion.311
  4163.4 4.8 fusion.308
  4179.8 6.5 fusion.213
  4198.0 6.4 fusion.211
  4206.3 6.5 fusion.214
  4223.6 29.0 reduce-scatter.57.cloned.1.call-done
  4252.6 40.2 reduce-scatter.55.cloned.1.call-done
  4294.6 38.3 reduce-scatter.53.cloned.1.call-done
  4332.9 40.4 reduce-scatter.51.cloned.1.call-done
  4375.0 38.7 reduce-scatter.49.cloned.1.call-done
  4413.7 40.2 reduce-scatter.47.cloned.1.call-done
  4455.7 38.3 reduce-scatter.65.cloned.1.call-done
  4494.0 40.2 reduce-scatter.63.cloned.1.call-done
  4536.0 60.8 %reduce-scatter.45.cloned.1.call-done = bf16[1,256,1536]{2,1,0:T(8,128)(2,1)} async-done(((bf16[1,1024,1536]{2,1,0:T(8,128)(2,1)}), bf16[1,256,1536]{2,1,0:T(8,128)(2,1)}) %reduce-scatter.45.cloned.1.call-update) | async-done | bytes 786448 | tf_op jit(solution)/shard_map/reduce_scatter | solution.py:157
  4596.8 63.2 %reduce-scatter.41.cloned.1.call-done = bf16[1,256,1536]{2,1,0:T(8,128)(2,1)} async-done(((bf16[1,1024,1536]{2,1,0:T(8,128)(2,1)}), bf16[1,256,1536]{2,1,0:T(8,128)(2,1)}) %reduce-scatter.41.cloned.1.call-update) | async-done | bytes 786448 | tf_op jit(solution)/shard_map/reduce_scatter | solution.py:157
  4662.6 44.3 all-reduce.2
  4712.1 11.4 reduce-scatter.33.cloned.1.call-done
  (3643 shorter events, 3224.7 us)
Async XLA Ops:
  7.2 40.2 all-gather.22.cloned.1.call-start
  7.9 94.6 %all-gather.40.cloned.1.call-start = ((), (), s32[]{:S(2)}) async-start(), calls=%async_computation.38 | async-start | bytes 3932160 | tf_op jit(solution)/shard_map/all_gather | solution.py:143
  31.6 104.5 %all-gather.24.cloned.1.call-start = ((), (), s32[]{:S(2)}) async-start(), calls=%async_computation.28 | async-start | bytes 1327104 | tf_op jit(solution)/shard_map/all_gather | solution.py:113
  32.4 124.1 %all-gather.26.cloned.1.call-start = ((), (), s32[]{:S(2)}) async-start(), calls=%async_computation.29 | async-start | bytes 1327104 | tf_op jit(solution)/shard_map/all_gather | solution.py:112
  32.9 145.9 %all-gather.28.cloned.1.call-start = ((), (), s32[]{:S(2)}) async-start(), calls=%async_computation.30 | async-start | bytes 1327104 | tf_op jit(solution)/shard_map/all_gather | solution.py:114
  33.5 546.5 %all-gather.20.cloned.1.call-start = ((), (), s32[]{:S(2)}) async-start(), calls=%async_computation.26 | async-start | bytes 3932160 | tf_op jit(solution)/shard_map/all_gather | solution.py:143
  34.1 567.1 %all-gather.30.cloned.1.call-start = ((), (), s32[]{:S(2)}) async-start(), calls=%async_computation.31 | async-start | bytes 1327104 | tf_op jit(solution)/shard_map/all_gather | solution.py:117
  34.9 1015.0 %reduce-scatter.35.cloned.1.call-start = ((), (), s32[]{:S(2)}) async-start(), calls=%async_computation.39 | async-start | bytes 3932160 | tf_op jit(solution)/shard_map/reduce_scatter | solution.py:147
  34.9 591.4 %copy-start.136 = (f32[64,64]{0,1:T(8,128)}, f32[64,64]{0,1:T(8,128)S(1)}, u32[]{:S(2)}) copy-start(f32[64,64]{0,1:T(8,128)S(1)} %fusion.581) | copy-start | bytes 49156
  34.9 561.9 %copy-start.184 = (f32[64,64]{0,1:T(8,128)}, f32[64,64]{0,1:T(8,128)S(1)}, u32[]{:S(2)}) copy-start(f32[64,64]{0,1:T(8,128)S(1)} %fusion.580) | copy-start | bytes 49156
  35.5 607.8 %copy-start.182 = (f32[64,64]{1,0:T(8,128)}, f32[64,64]{1,0:T(8,128)S(1)}, u32[]{:S(2)}) copy-start(f32[64,64]{1,0:T(8,128)S(1)} %fusion.582) | copy-start | bytes 49156
  45.5 539.9 %copy-start.196 = (bf16[1536,3]{0,1:T(4,128)(2,1)}, bf16[1536,3]{0,1:T(4,128)(2,1)S(1)}, u32[]{:S(2)}) copy-start(bf16[1536,3]{0,1:T(4,128)(2,1)S(1)} %reshape.3186) | copy-start | bytes 27652
  46.8 64.6 %copy-start.222 = (f32[1024]{0:T(1024)}, f32[1024]{0:T(1024)S(1)}, u32[]{:S(2)}) copy-start(f32[1024]{0:T(1024)S(1)} %fusion.602) | copy-start | bytes 12292
  47.3 541.5 %copy-start.220 = (f32[1024]{0:T(1024)}, f32[1024]{0:T(1024)S(1)}, u32[]{:S(2)}) copy-start(f32[1024]{0:T(1024)S(1)} %fusion.601) | copy-start | bytes 12292
  107.8 63.4 %copy-start.4 = (f32[1,3,1024,128]{3,2,1,0:T(8,128)}, f32[1,3,1024,128]{3,2,1,0:T(8,128)S(1)}, u32[]{:S(2)}) copy-start(f32[1,3,1024,128]{3,2,1,0:T(8,128)S(1)} %copy.361) | copy-start | bytes 4718596
  585.4 73.3 %copy-start.7 = (f32[1,3,1024,128]{3,2,1,0:T(8,128)}, f32[1,3,1024,128]{3,2,1,0:T(8,128)S(1)}, u32[]{:S(2)}) copy-start(f32[1,3,1024,128]{3,2,1,0:T(8,128)S(1)} %copy.332) | copy-start | bytes 4718596
  606.3 503.2 %reduce-scatter.31.cloned.1.call-start = ((), (), s32[]{:S(2)}) async-start(), calls=%async_computation.32 | async-start | bytes 3932160 | tf_op jit(solution)/shard_map/reduce_scatter | solution.py:147
  1049.0 94.6 %all-gather.36.cloned.1.call-start = ((), (), s32[]{:S(2)}) async-start(), calls=%async_computation.35 | async-start | bytes 3538944 | tf_op jit(solution)/shard_map/all_gather | solution.py:119
  1049.6 159.7 %all-gather.42.cloned.1.call-start = ((), (), s32[]{:S(2)}) async-start(), calls=%async_computation.40 | async-start | bytes 3932160 | tf_op jit(solution)/shard_map/all_gather | solution.py:143
  1049.8 606.5 %copy-start.198 = (f32[1536]{0:T(1024)}, f32[1536]{0:T(1024)S(1)}, u32[]{:S(2)}) copy-start(f32[1536]{0:T(1024)S(1)} %convert_element_type.638) | copy-start | bytes 18436
  1111.5 544.8 %copy-start.226 = (f32[256]{0:T(256)}, f32[256]{0:T(256)S(1)}, u32[]{:S(2)}) copy-start(f32[256]{0:T(256)S(1)} %fusion.604) | copy-start | bytes 3076
  1111.5 544.8 %copy-start.228 = (f32[256]{0:T(256)}, f32[256]{0:T(256)S(1)}, u32[]{:S(2)}) copy-start(f32[256]{0:T(256)S(1)} %fusion.606) | copy-start | bytes 3076
  1113.3 128.7 %all-gather.34.cloned.1.call-start = ((), (), s32[]{:S(2)}) async-start(), calls=%async_computation.34 | async-start | bytes 3538944 | tf_op jit(solution)/shard_map/all_gather | solution.py:118
  1113.9 193.8 %all-gather.50.cloned.1.call-start = ((), (), s32[]{:S(2)}) async-start(), calls=%async_computation.65 | async-start | bytes 3932160 | tf_op jit(solution)/shard_map/all_gather | solution.py:153
  1116.5 223.8 %all-gather.38.cloned.1.call-start = ((), (), s32[]{:S(2)}) async-start(), calls=%async_computation.36 | async-start | bytes 3538944 | tf_op jit(solution)/shard_map/all_gather | solution.py:120
  1117.1 288.8 %all-gather.32.cloned.1.call-start = ((), (), s32[]{:S(2)}) async-start(), calls=%async_computation.33 | async-start | bytes 3932160 | tf_op jit(solution)/shard_map/all_gather | solution.py:143
  1117.7 351.8 %all-gather.48.cloned.1.call-start = ((), (), s32[]{:S(2)}) async-start(), calls=%async_computation.64 | async-start | bytes 3932160 | tf_op jit(solution)/shard_map/all_gather | solution.py:153
  1118.3 412.3 %reduce-scatter.43.cloned.1.call-start = ((), (), s32[]{:S(2)}) async-start(), calls=%async_computation.45 | async-start | bytes 3932160 | tf_op jit(solution)/shard_map/reduce_scatter | solution.py:157
  1361.0 232.7 %reduce-scatter.39.cloned.1.call-start = ((), (), s32[]{:S(2)}) async-start(), calls=%async_computation.42 | async-start | bytes 3932160 | tf_op jit(solution)/shard_map/reduce_scatter | solution.py:157
  1489.6 166.6 %reduce-scatter.37.cloned.1.call-start = ((), (), s32[]{:S(2)}) async-start(), calls=%async_computation.41 | async-start | bytes 3932160 | tf_op jit(solution)/shard_map/reduce_scatter | solution.py:147
  1497.3 684.5 %all-gather.46.cloned.1.call-start = ((), (), s32[]{:S(2)}) async-start(), calls=%async_computation.46 | async-start | bytes 3932160 | tf_op jit(solution)/shard_map/all_gather | solution.py:153
  1596.9 63.1 %copy-start.236 = (f32[256]{0:T(256)}, f32[256]{0:T(256)S(1)}, u32[]{:S(2)}) copy-start(f32[256]{0:T(256)S(1)} %multiply_multiply_fusion.1) | copy-start | bytes 3076
  1660.1 1449.5 %all-gather.44.cloned.1.call-start = ((), (), s32[]{:S(2)}) async-start(), calls=%async_computation.43 | async-start | bytes 3932160 | tf_op jit(solution)/shard_map/all_gather | solution.py:153
  1660.8 2552.0 %reduce-scatter.73.cloned.1.call-start = ((), (), s32[]{:S(2)}) async-start(), calls=%async_computation.61 | async-start | bytes 3538944 | tf_op jit(solution)/shard_map/reduce_scatter | solution.py:185
  1668.6 2544.3 %reduce-scatter.71.cloned.1.call-start = ((), (), s32[]{:S(2)}) async-start(), calls=%async_computation.60 | async-start | bytes 3538944 | tf_op jit(solution)/shard_map/reduce_scatter | solution.py:185
  1677.2 2537.8 %reduce-scatter.69.cloned.1.call-start = ((), (), s32[]{:S(2)}) async-start(), calls=%async_computation.59 | async-start | bytes 3538944 | tf_op jit(solution)/shard_map/reduce_scatter | solution.py:182
  1685.6 2529.4 %reduce-scatter.67.cloned.1.call-start = ((), (), s32[]{:S(2)}) async-start(), calls=%async_computation.58 | async-start | bytes 3538944 | tf_op jit(solution)/shard_map/reduce_scatter | solution.py:182
  1694.0 2523.1 %reduce-scatter.77.cloned.1.call-start = ((), (), s32[]{:S(2)}) async-start(), calls=%async_computation.63 | async-start | bytes 3538944 | tf_op jit(solution)/shard_map/reduce_scatter | solution.py:188
  1937.5 2279.6 %reduce-scatter.75.cloned.1.call-start = ((), (), s32[]{:S(2)}) async-start(), calls=%async_computation.62 | async-start | bytes 3538944 | tf_op jit(solution)/shard_map/reduce_scatter | solution.py:188
  2181.7 2037.6 %reduce-scatter.81.cloned.1.call-start = ((), (), s32[]{:S(2)}) async-start(), calls=%async_computation.67 | async-start | bytes 442368
  4061.5 158.8 %reduce-scatter.79.cloned.1.call-start = ((), (), s32[]{:S(2)}) async-start(), calls=%async_computation.66 | async-start | bytes 442368
  4065.0 156.8 %reduce-scatter.61.cloned.1.call-start = ((), (), s32[]{:S(2)}) async-start(), calls=%async_computation.55 | async-start | bytes 1327104 | tf_op jit(solution)/shard_map/reduce_scatter | solution.py:173
  4075.0 146.8 %reduce-scatter.59.cloned.1.call-start = ((), (), s32[]{:S(2)}) async-start(), calls=%async_computation.54 | async-start | bytes 1327104 | tf_op jit(solution)/shard_map/reduce_scatter | solution.py:173
  4093.4 159.2 %reduce-scatter.57.cloned.1.call-start = ((), (), s32[]{:S(2)}) async-start(), calls=%async_computation.53 | async-start | bytes 1327104 | tf_op jit(solution)/shard_map/reduce_scatter | solution.py:170
  4100.7 192.2 %reduce-scatter.55.cloned.1.call-start = ((), (), s32[]{:S(2)}) async-start(), calls=%async_computation.52 | async-start | bytes 1327104 | tf_op jit(solution)/shard_map/reduce_scatter | solution.py:170
  4108.1 224.7 %reduce-scatter.53.cloned.1.call-start = ((), (), s32[]{:S(2)}) async-start(), calls=%async_computation.51 | async-start | bytes 1327104 | tf_op jit(solution)/shard_map/reduce_scatter | solution.py:167
  4121.7 251.5 %reduce-scatter.51.cloned.1.call-start = ((), (), s32[]{:S(2)}) async-start(), calls=%async_computation.50 | async-start | bytes 1327104 | tf_op jit(solution)/shard_map/reduce_scatter | solution.py:167
  4135.6 278.1 %reduce-scatter.49.cloned.1.call-start = ((), (), s32[]{:S(2)}) async-start(), calls=%async_computation.49 | async-start | bytes 1327104 | tf_op jit(solution)/shard_map/reduce_scatter | solution.py:164
  4148.6 305.3 %reduce-scatter.47.cloned.1.call-start = ((), (), s32[]{:S(2)}) async-start(), calls=%async_computation.48 | async-start | bytes 1327104 | tf_op jit(solution)/shard_map/reduce_scatter | solution.py:164
  4158.5 335.5 %reduce-scatter.65.cloned.1.call-start = ((), (), s32[]{:S(2)}) async-start(), calls=%async_computation.57 | async-start | bytes 1327104 | tf_op jit(solution)/shard_map/reduce_scatter | solution.py:179
  4163.4 370.8 %reduce-scatter.63.cloned.1.call-start = ((), (), s32[]{:S(2)}) async-start(), calls=%async_computation.56 | async-start | bytes 1327104 | tf_op jit(solution)/shard_map/reduce_scatter | solution.py:179
  4168.3 428.5 %reduce-scatter.45.cloned.1.call-start = ((), (), s32[]{:S(2)}) async-start(), calls=%async_computation.47 | async-start | bytes 3932160 | tf_op jit(solution)/shard_map/reduce_scatter | solution.py:157
  4186.3 473.7 %reduce-scatter.41.cloned.1.call-start = ((), (), s32[]{:S(2)}) async-start(), calls=%async_computation.44 | async-start | bytes 3932160 | tf_op jit(solution)/shard_map/reduce_scatter | solution.py:157
  4204.5 519.1 %reduce-scatter.33.cloned.1.call-start = ((), (), s32[]{:S(2)}) async-start(), calls=%async_computation.37 | async-start | bytes 3932160 | tf_op jit(solution)/shard_map/reduce_scatter | solution.py:147
  4219.2 440.8 %copy-start.11 = (bf16[2,1,256,1536]{3,2,1,0:T(8,128)(2,1)S(1)}, bf16[2,1,256,1536]{3,2,1,0:T(8,128)(2,1)}, u32[]{:S(2)}) copy-start(bf16[2,1,256,1536]{3,2,1,0:T(8,128)(2,1)} %param.50) | copy-start | bytes 4718596
  4219.2 440.8 %copy-start.205 = (f32[1536]{0:T(1024)S(1)}, f32[1536]{0:T(1024)}, u32[]{:S(2)}) copy-start(f32[1536]{0:T(1024)} %copy-done.204) | copy-start | bytes 18436
  4219.2 440.8 %copy-start.231 = (f32[256]{0:T(256)S(1)}, f32[256]{0:T(256)}, u32[]{:S(2)}) copy-start(f32[256]{0:T(256)} %copy-done.230) | copy-start | bytes 3076
  4219.2 440.8 %copy-start.233 = (f32[256]{0:T(256)S(1)}, f32[256]{0:T(256)}, u32[]{:S(2)}) copy-start(f32[256]{0:T(256)} %copy-done.232) | copy-start | bytes 3076
  4535.9 172.3 %copy-start.239 = (f32[256]{0:T(256)S(1)}, f32[256]{0:T(256)}, u32[]{:S(2)}) copy-start(f32[256]{0:T(256)} %copy-done.238) | copy-start | bytes 3076
  4535.9 172.3 %copy-start.241 = (f32[256]{0:T(256)S(1)}, f32[256]{0:T(256)}, u32[]{:S(2)}) copy-start(f32[256]{0:T(256)} %copy-done.240) | copy-start | bytes 3076
  4535.9 172.3 %copy-start.90 = (bf16[1,256,1536]{2,1,0:T(8,128)(2,1)S(1)}, bf16[1,256,1536]{2,1,0:T(8,128)(2,1)}, u32[]{:S(2)}) copy-start(bf16[1,256,1536]{2,1,0:T(8,128)(2,1)} %reduce-scatter.35.cloned.1.call-done) | copy-start | bytes 2359300
  4535.9 172.3 %copy-start.199 = (f32[1536]{0:T(1024)S(1)}, f32[1536]{0:T(1024)}, u32[]{:S(2)}) copy-start(f32[1536]{0:T(1024)} %copy-done.198) | copy-start | bytes 18436
  4535.9 172.3 %copy-start.229 = (f32[256]{0:T(256)S(1)}, f32[256]{0:T(256)}, u32[]{:S(2)}) copy-start(f32[256]{0:T(256)} %copy-done.228) | copy-start | bytes 3076
  4535.9 172.3 %copy-start.237 = (f32[256]{0:T(256)S(1)}, f32[256]{0:T(256)}, u32[]{:S(2)}) copy-start(f32[256]{0:T(256)} %copy-done.236) | copy-start | bytes 3076
  (480 other events, 1708.9 us)
Sparse Core Ops, SparseCore 0:
  9.9 26.9 all-gather.21
  39.0 63.4 all-gather.39
  104.4 22.6 all-gather.23
  128.9 24.0 all-gather.25
  154.8 24.0 all-gather.27
  180.8 63.5 all-gather.19
  246.3 22.6 all-gather.29
  606.4 60.2 reduce-scatter.34
  1049.1 60.2 reduce-scatter.30
  1111.2 32.3 all-gather.35
  1145.7 63.4 all-gather.41
  1211.0 30.9 all-gather.33
  1244.1 63.4 all-gather.49
  1309.4 30.9 all-gather.37
  1342.4 63.4 all-gather.31
  1407.3 62.1 all-gather.47
  1471.7 58.8 reduce-scatter.42
  1533.3 60.2 reduce-scatter.38
  1596.0 60.2 reduce-scatter.36
  1660.2 63.5 all-gather.45
  1725.9 62.1 all-gather.43
  1791.5 44.9 reduce-scatter.72
  1840.2 46.2 reduce-scatter.70
  1889.7 46.2 reduce-scatter.68
  1939.7 46.2 reduce-scatter.66
  1989.2 46.2 reduce-scatter.76
  2181.8 46.1 reduce-scatter.74
  4061.6 33.6 reduce-scatter.80
  4098.4 33.8 reduce-scatter.78
  4135.4 36.7 reduce-scatter.60
  4175.7 36.7 reduce-scatter.58
  4215.8 36.7 reduce-scatter.56
  4256.0 36.7 reduce-scatter.54
  4296.1 36.7 reduce-scatter.52
  4336.4 36.7 reduce-scatter.50
  4376.9 36.7 reduce-scatter.48
  4417.1 36.7 reduce-scatter.46
  4457.2 36.7 reduce-scatter.64
  4497.4 36.7 reduce-scatter.62
  4536.5 60.2 reduce-scatter.44
  4599.6 60.2 reduce-scatter.40
  4662.3 61.2 reduce-scatter.32
where the time goes:
time: 4780 us; the launch traced here: 4740 us
  matrix products  1800 us (38%)
  waiting for transfers between devices  1020 us (21%)
  local copies, waits for them, and re-layouts  894 us (19%)
  other arithmetic  732 us (15%)
  loops' own time  197 us (4%)
  blocking collectives  68.3 us (1%)
    dot_general x626, matrix products, einsum_high(): jnp.einsum(formula, left_side, right_side, precision=lax.Precision.HIGHEST)  1540 us
    another operation x320, other arithmetic  460 us
    reduce_scatter x4, waiting for transfers between devices, scatter_grads(): lax.psum_scatter(partial_rows.astype(jnp.bfloat16), 'head', scatter_dimen...  220 us
    squeeze x160, local copies, waits for them, and re-layouts, householder_attention(): lax.scan(jax.checkpoint(advance), initial, (moved_queries, moved_keys, up...  206 us
    another operation x6, loops' own time, householder_attention(): lax.scan(jax.checkpoint(advance), initial, (moved_queries, moved_keys, up...  197 us
    all_gather x4, waiting for transfers between devices, gather_rows(): return lax.all_gather(local_rows, 'head', axis=1, tiled=True)  166 us
    scatter x96, local copies, waits for them, and re-layouts, advance(): across = lax.dynamic_update_slice_in_dim(across, block_local, start_row, 1)  156 us
    reduce_scatter x4, waiting for transfers between devices, scatter_rows(): lax.psum_scatter(partial_rows.astype(jnp.bfloat16), 'head', scatter_dimen...  130 us
  transfers between devices with their start and end apart: 42, of which 24 were waited for; matrix products, arithmetic and copies ran while one was open for 70% of the time, Pallas kernels for 0%

commit v1 on v0

v1 whole, which is shorter than its diff:
```python
import functools

import jax
import jax.numpy as jnp
from jax import lax
from jax.experimental import pallas as pl
from jax.experimental.pallas import tpu as pltpu
from jax.sharding import Mesh, PartitionSpec as P

HEAD_DIM = 128
TILE = 128
F32 = jnp.float32
BF16 = jnp.bfloat16
COST_SCALE = 2.5e+09
(
    ATTN_ROWS,
    OUT_ROWS,
    FFN_OWN,
    FFN_GIVE,
    COT,
    ATTN,
    FFN_TAKE,
    HOP,
    TOK,
    CHUNK,
    OUT,
    OUT_ALL,
    COT_OTHER,
    ATTEND,
    MIX,
    PROJECT,
    TURN_COT,
    MIDDLE,
    H2_OTHER,
    FEED,
    DH_OTHER,
    TURN_H2,
    GRAD_FAR,
    PLANE_SUM,
    SUM,
    FAR,
    GRAD_MIDDLE,
    MID,
    GRAD_NEAR,
    LAST,
    LAST_OTHER,
    NORM,
    SENT,
    OUT_GRAD,
    OUT_CORE,
    OUT_RS,
    OUTSUM,
    DOWN,
    DOWN_OTHER,
    BACK,
    DH,
    RING,
    ATTN_GRAD,
    ATTN_CORE,
    ATTN_RS,
    GAIN,
    INPUT,
    BLOCK_OUT,
    FINISH,
) = range(49)
PLAN = {
    "order": (
        (PROJECT, 0),
        (ATTEND, 0),
        TURN_COT,
        (PROJECT, 1),
        (ATTEND, 1),
        MIDDLE,
        (FEED, 0),
        TURN_H2,
        (FEED, 1),
        (GRAD_FAR, 1),
        (FEED, 2),
        (GRAD_FAR, 2),
        (FEED, 3),
        NORM,
        (GRAD_FAR, 3),
        OUT_GRAD,
        (BACK, 0),
        (DH, 0),
        DOWN,
        (GRAD_FAR, 0),
        (BACK, 1),
        (DH, 1),
        ATTN_GRAD,
        (GRAD_MIDDLE, 0),
        (INPUT, 0),
        BLOCK_OUT,
        LAST,
        (INPUT, 1),
        FINISH,
    ),
    "direct": (2,),
    "da_first": (0,),
    "whole": (1, 2, 3),
    "gates": {
        (TOK, 1, 3): ((ATTEND, 0),),
        (HOP, 1): ((TOK, 1, 3),),
        (HOP, 2): ((PROJECT, 1),),
        (HOP, 3): ((ATTEND, 1),),
        (CHUNK, 0, 0): (ATTN_ROWS,),
        OUT_ALL: ((PROJECT, 1),),
        (CHUNK, 3, 0): (MIDDLE,),
        (TOK, 0, 2): ((HOP, 0),),
        (CHUNK, 1, 0): ((ATTEND, 1),),
        OUT_RS: ((GRAD_FAR, 0),),
    },
    "pins": {
        (ATTEND, 1): ((CHUNK, 0, 0),),
        (GRAD_FAR, 0): ((RING, 0, 1),),
        (INPUT, 0): ((RING, 1, 2),),
        (DH, 0): ((SUM, 1),),
        (FEED, 1): ((MIX, 1, 1),),
        (DH, 1): ((RING, 0, 2),),
        ATTN_GRAD: ((RING, 0, 3),),
        (GRAD_MIDDLE, 0): ((RING, 1, 1), (SUM, 2)),
    },
}
QUERY, KEY, VALUE, RAW = [slice(i * HEAD_DIM, (i + 1) * HEAD_DIM) for i in range(4)]


def mm(left, right):
    return lax.dot_general(
        left.astype(BF16), right.astype(BF16), (((1,), (0,)), ((), ())), preferred_element_type=F32
    )


def mm_nt(left, right):
    return lax.dot_general(
        left.astype(BF16), right.astype(BF16), (((1,), (1,)), ((), ())), preferred_element_type=F32
    )


def mm_tn(left, right):
    return lax.dot_general(
        left.astype(BF16), right.astype(BF16), (((0,), (0,)), ((), ())), preferred_element_type=F32
    )


def tile_index():
    rows = lax.broadcasted_iota(jnp.int32, (TILE, TILE), 0)
    cols = lax.broadcasted_iota(jnp.int32, (TILE, TILE), 1)
    return rows, cols


def each(function, *lists):
    return [function(*items) for items in zip(*lists)]


def unit_directions(raw):
    raw = raw.astype(F32)
    inv_norm = lax.rsqrt(jnp.sum(raw * raw, axis=-1, keepdims=True) + 1e-06)
    return raw * inv_norm, inv_norm


def get_row(ref, row, cols):
    block = ref[:, cols]
    lines = lax.broadcasted_iota(jnp.int32, block.shape, 0)
    return jnp.sum(jnp.where(lines == row, block, 0.0), axis=0, keepdims=True)


def set_row(ref, row, cols, value):
    block = ref[:, cols]
    lines = lax.broadcasted_iota(jnp.int32, block.shape, 0)
    ref[:, cols] = jnp.where(lines == row, value, block)


def inverse_tiles(lower):
    rows, cols = tile_index()
    identity = (rows == cols).astype(F32)
    width = 8
    part = (rows // width == cols // width).astype(F32)
    power = each(lambda a: a * part, lower)
    result = each(lambda a: identity - a, power)
    reach = 2
    while reach < width:
        power = each(lambda a: mm(a, a), power)
        result = each(lambda a, b: a + mm(a, b), result, power)
        reach *= 2
    while width < TILE:
        corner = (
            (rows // (2 * width) == cols // (2 * width)) & (rows // width != cols // width)
        ).astype(F32)
        inner = each(lambda a, b: mm(a * corner, b), lower, result)
        result = each(lambda a, b: a - mm(a, b), result, inner)
        width *= 2
    return result


def forward_kernel(
    where_ref, length_ref, x_ref, logit_ref,
    out_ref, tt_ref, e_ref, g_ref, d_ref, mq_ref, state_ref, prob_ref,
    mk_ref, local_ref, run_ref,
):
    seq_len = x_ref.shape[0]
    tiles = seq_len // TILE
    length = length_ref[0]
    head = pl.program_id(0)
    rows, cols = tile_index()
    below = (rows > cols).astype(F32)
    upto = (rows >= cols).astype(F32)
    span = [pl.ds(n * TILE, TILE) for n in range(tiles)]
    group = min(tiles, 8)
    for first in range(0, tiles, group):
        part = list(range(first, first + group))
        units = [unit_directions(x_ref[span[n], RAW])[0].astype(BF16) for n in part]
        queries = [x_ref[span[n], QUERY] for n in part]
        keys = [x_ref[span[n], KEY] for n in part]
        position = lax.broadcasted_iota(jnp.int32, (1, TILE), 1)
        strength = [
            jnp.where(
                position + n * TILE < length,
                jax.nn.sigmoid(get_row(logit_ref, head, slice(n * TILE, (n + 1) * TILE))),
                0.0,
            )
            for n in part
        ]
        gram = each(lambda w: mm_nt(w, w) * below, units)
        inverse = inverse_tiles(each(lambda g, b: g * b, gram, strength))
        turned = each(lambda t: t.T, inverse)
        for n, t in zip(part, turned):
            tt_ref[span[n], :] = t.astype(BF16)
        upper = each(lambda t, b: (t * b).astype(BF16), turned, strength)
        cross = each(lambda w, k: (mm_nt(w, k) * below).astype(BF16), units, keys)
        seen = each(lambda q, w: (mm_nt(q, w) * upto).astype(BF16), queries, units)
        weight = each(lambda a, u: mm_nt(a, u).astype(BF16), seen, upper)
        slope = each(lambda u, w: mm(u, w).astype(BF16), upper, units)
        moved_q = each(lambda q, e, w: (q.astype(F32) - mm(e, w)).astype(BF16), queries, weight, units)
        local = each(lambda q, k, e, c: mm_nt(q, k) - mm(e, c), queries, keys, weight, cross)
        moved_k = each(lambda k, c, g: k.astype(F32) - mm_tn(c, g), keys, cross, slope)
        step = each(lambda w, g: mm_tn(w, g).astype(BF16), units, slope)
        for i, n in enumerate(part):
            e_ref[span[n], :] = weight[i]
            g_ref[span[n], :] = slope[i]
            d_ref[span[n], :] = step[i]
            mq_ref[span[n], :] = moved_q[i]
            local_ref[span[n], :] = local[i]
            mk_ref[span[n], :] = moved_k[i]
    scale = HEAD_DIM ** (-0.5)
    offset = 0
    for n in range(tiles):
        done = n * TILE
        if n:
            old = pl.ds(0, done)
            past = run_ref[old, :]
            past_low = past.astype(BF16)
            state_ref[pl.ds(offset, done), :] = past_low
            offset += done
            scores = jnp.concatenate(
                [mm_nt(mq_ref[span[n], :], past_low), local_ref[span[n], :]], axis=1
            )
            if n + 1 < tiles:
                run_ref[old, :] = past - mm(past_low, d_ref[span[n], :])
        else:
            scores = local_ref[span[n], :]
        if n + 1 < tiles:
            run_ref[span[n], :] = mk_ref[span[n], :]
        wide = done + TILE
        row_at = lax.broadcasted_iota(jnp.int32, (TILE, wide), 0) + done
        col_at = lax.broadcasted_iota(jnp.int32, (TILE, wide), 1)
        allowed = (col_at <= row_at) & (col_at < length)
        scores = jnp.where(allowed, scores * scale, -1e30)
        top = jnp.max(scores, axis=-1, keepdims=True)
        weights = jnp.exp(scores - top)
        weights = weights * (1.0 / jnp.sum(weights, axis=-1, keepdims=True))
        weights = weights.astype(BF16)
        prob_ref[0, span[n], pl.ds(0, wide)] = weights
        mixed = mm(weights, x_ref[pl.ds(0, wide), VALUE]).astype(out_ref.dtype)
        if len(out_ref.shape) == 2:
            out_ref[span[n], :] = mixed
        else:
            per = out_ref.shape[1] // TILE
            row = (n % per) * TILE
            out_ref[where_ref[12 + n // per], row : row + TILE, :] = mixed


def backward_kernel(
    grad_count, where_ref, length_ref, x_ref, logit_ref, *refs
):
    grad_refs, refs = refs[:grad_count], refs[grad_count:]
    (
    tt_ref, e_ref, g_ref, d_ref, mq_ref, state_ref, prob_ref,
    dx_ref, dlogit_ref,
    run_ref, value_ref, dmq_ref, dlocal_ref, dmk_ref, dstep_ref, do_ref,
    ) = refs
    part = grad_refs[0].shape[0]

    @pl.when(pl.program_id(0) == 0)
    def _():
        dlogit_ref[...] = jnp.zeros_like(dlogit_ref)

    for s, ref in enumerate(grad_refs):
        at = where_ref[8 + s] * part if grad_count > 1 else 0
        do_ref[pl.ds(pl.multiple_of(at, TILE), part), :] = ref[...]
    seq_len = x_ref.shape[0]
    tiles = seq_len // TILE
    length = length_ref[0]
    head = pl.program_id(0)
    rows, cols = tile_index()
    below = (rows > cols).astype(F32)
    upto = (rows >= cols).astype(F32)
    identity = (rows == cols).astype(F32)
    scale = HEAD_DIM ** (-0.5)
    span = [pl.ds(n * TILE, TILE) for n in range(tiles)]
    offset = TILE * (tiles * (tiles - 1) // 2)
    for n in reversed(range(tiles)):
        done = n * TILE
        wide = done + TILE
        old = pl.ds(0, done)
        grad_out = do_ref[span[n], :]
        weights = prob_ref[0, span[n], pl.ds(0, wide)]
        grad_w = mm_nt(grad_out, x_ref[pl.ds(0, wide), VALUE])
        weights_full = weights.astype(F32)
        mixed = weights_full * grad_w
        total = jnp.sum(mixed, axis=-1, keepdims=True)
        grad_s = ((mixed - weights_full * total) * scale).astype(BF16)
        back = mm_tn(weights, grad_out)
        if n + 1 < tiles:
            value_ref[pl.ds(0, wide), :] = value_ref[pl.ds(0, wide), :] + back
        else:
            value_ref[...] = back
        dlocal_ref[span[n], :] = grad_s[:, done:]
        if n + 1 < tiles:
            dmk_ref[span[n], :] = run_ref[span[n], :].astype(BF16)
        else:
            dmk_ref[span[n], :] = jnp.zeros((TILE, HEAD_DIM), BF16)
        if n:
            offset -= done
            past = state_ref[pl.ds(offset, done), :]
            grad_far = grad_s[:, :done]
            dmq_ref[span[n], :] = mm(grad_far, past).astype(BF16)
            fresh = mm_tn(grad_far, mq_ref[span[n], :])
            if n + 1 < tiles:
                carried = run_ref[old, :]
                carried_low = carried.astype(BF16)
                dstep_ref[span[n], :] = (-mm_tn(past, carried_low)).astype(BF16)
                run_ref[old, :] = carried - mm_nt(carried_low, d_ref[span[n], :]) + fresh
            else:
                dstep_ref[span[n], :] = jnp.zeros((TILE, HEAD_DIM), BF16)
                run_ref[old, :] = fresh
        else:
            dmq_ref[span[n], :] = jnp.zeros((TILE, HEAD_DIM), BF16)
            dstep_ref[span[n], :] = jnp.zeros((TILE, HEAD_DIM), BF16)
    dx_ref[:, VALUE] = value_ref[...].astype(dx_ref.dtype)
    group = min(tiles, 8)
    for first in range(0, tiles, group):
        part = list(range(first, first + group))
        pairs = [unit_directions(x_ref[span[n], RAW]) for n in part]
        units = [p[0].astype(BF16) for p in pairs]
        queries = [x_ref[span[n], QUERY] for n in part]
        keys = [x_ref[span[n], KEY] for n in part]
        position = lax.broadcasted_iota(jnp.int32, (1, TILE), 1)
        gates = [
            jax.nn.sigmoid(get_row(logit_ref, head, slice(n * TILE, (n + 1) * TILE))) for n in part
        ]
        live = [(position + n * TILE < length).astype(F32) for n in part]
        strength = each(lambda s, m: s * m, gates, live)
        turned = [tt_ref[span[n], :] for n in part]
        weight = [e_ref[span[n], :] for n in part]
        slope = [g_ref[span[n], :] for n in part]
        dlocal = [dlocal_ref[span[n], :] for n in part]
        dmq = [dmq_ref[span[n], :] for n in part]
        dmk = [dmk_ref[span[n], :] for n in part]
        dstep = [dstep_ref[span[n], :] for n in part]
        gram = each(lambda w: mm_nt(w, w) * below, units)
        cross = each(lambda w, k: (mm_nt(w, k) * below).astype(BF16), units, keys)
        seen = each(lambda q, w: (mm_nt(q, w) * upto).astype(BF16), queries, units)
        upper = each(lambda t, b: (t.astype(F32) * b).astype(BF16), turned, strength)
        dweight = each(
            lambda dm, w, dl, c: (-(mm_nt(dm, w) + mm_nt(dl, c))).astype(BF16),
            dmq, units, dlocal, cross,
        )
        dcross = each(
            lambda e, dl, g, dm: ((-(mm_tn(e, dl) + mm_nt(g, dm))) * below).astype(BF16),
            weight, dlocal, slope, dmk,
        )
        dslope = each(
            lambda w, ds, c, dm: (mm(w, ds) - mm(c, dm)).astype(BF16), units, dstep, cross, dmk
        )
        dinv = each(
            lambda a, de, w, dg: (mm_tn(a, de) + mm_nt(w, dg)).astype(BF16),
            seen, dweight, units, dslope,
        )
        dseen = each(lambda de, u: (mm(de, u) * upto).astype(BF16), dweight, upper)
        inner = each(lambda d, t: mm(d, t), dinv, turned)
        dlower = each(lambda u, h: -mm(u, h) * below, upper, inner)
        dgram = each(lambda d, b: (d * b).astype(BF16), dlower, strength)
        dunit = each(
            lambda e, dm, g, ds, u, dg: mm_nt(g, ds) - mm_tn(e, dm) + mm_tn(u, dg),
            weight, dmq, slope, dstep, upper, dslope,
        )
        dunit = each(
            lambda acc, da, q, dc, k, dg, w: acc
            + mm_tn(da, q) + mm(dc, k) + mm(dg, w) + mm_tn(dg, w),
            dunit, dseen, queries, dcross, keys, dgram, units,
        )
        for i, n in enumerate(part):
            dx_ref[span[n], QUERY] = (
                dmq[i].astype(F32) + mm(dlocal[i], keys[i]) + mm(dseen[i], units[i])
            ).astype(dx_ref.dtype)
            dx_ref[span[n], KEY] = (
                dmk[i].astype(F32) + mm_tn(dlocal[i], queries[i]) + mm_tn(dcross[i], units[i])
            ).astype(dx_ref.dtype)
            raw = x_ref[span[n], RAW].astype(F32)
            inv_norm = pairs[i][1]
            along = jnp.sum(raw * dunit[i], axis=-1, keepdims=True)
            dx_ref[span[n], RAW] = (
                inv_norm * dunit[i] - raw * (inv_norm * inv_norm * inv_norm) * along
            ).astype(dx_ref.dtype)
            dstrength = jnp.sum(
                identity * inner[i] + dlower[i] * gram[i], axis=0, keepdims=True
            )
            set_row(
                dlogit_ref,
                head,
                slice(n * TILE, (n + 1) * TILE),
                dstrength * gates[i] * (1.0 - gates[i]) * live[i],
            )


def saved_shapes(heads, seq_len):
    tiles = seq_len // TILE
    flat = jax.ShapeDtypeStruct((seq_len, heads * HEAD_DIM), BF16)
    state = jax.ShapeDtypeStruct((TILE * max(1, tiles * (tiles - 1) // 2), heads * HEAD_DIM), BF16)
    prob = jax.ShapeDtypeStruct((heads, seq_len, seq_len), BF16)
    return [flat] * 5 + [state, prob]


def saved_specs(heads, seq_len):
    tiles = seq_len // TILE
    flat = pl.BlockSpec((seq_len, HEAD_DIM), lambda h: (0, h))
    state = pl.BlockSpec((TILE * max(1, tiles * (tiles - 1) // 2), HEAD_DIM), lambda h: (0, h))
    prob = pl.BlockSpec((1, seq_len, seq_len), lambda h: (h, 0, 0))
    return [flat] * 5 + [state, prob]


def packed_spec(seq_len):
    return pl.BlockSpec((seq_len, 4 * HEAD_DIM), lambda h: (0, h))


def attention_forward(where, length, projected, logits):
    seq_len = projected.shape[0]
    heads = projected.shape[1] // (4 * HEAD_DIM)
    flat = pl.BlockSpec((seq_len, HEAD_DIM), lambda h: (0, h))
    return pl.pallas_call(
        forward_kernel,
        grid=(heads,),
        in_specs=[pl.BlockSpec(memory_space=pltpu.SMEM)] * 2
        + [packed_spec(seq_len)]
        + [pl.BlockSpec(logits.shape, lambda h: (0, 0))],
        out_specs=[
            flat
            if where is None
            else pl.BlockSpec((4, seq_len // 4, HEAD_DIM), lambda h: (0, 0, h))
        ]
        + saved_specs(heads, seq_len),
        out_shape=[
            jax.ShapeDtypeStruct(
                (seq_len, heads * HEAD_DIM)
                if where is None
                else (4, seq_len // 4, heads * HEAD_DIM),
                BF16,
            )
        ]
        + saved_shapes(heads, seq_len),
        scratch_shapes=[
            pltpu.VMEM((seq_len, HEAD_DIM), F32),
            pltpu.VMEM((seq_len, TILE), F32),
            pltpu.VMEM((seq_len, HEAD_DIM), F32),
        ],
        name="attention_forward",
        compiler_params=pltpu.CompilerParams(vmem_limit_bytes=56 * 1024 * 1024),
        cost_estimate=cost(21),
    )(length if where is None else where, length, projected, logits)


def attention_backward(where, length, projected, logits, grad_out, batch, saved):
    seq_len = projected.shape[0]
    heads = projected.shape[1] // (4 * HEAD_DIM)
    flat = pl.BlockSpec((seq_len, HEAD_DIM), lambda h: (0, h))
    row = pl.BlockSpec(logits.shape, lambda h: (0, 0))
    result = pl.pallas_call(
        functools.partial(backward_kernel, len(grad_out)),
        grid=(heads,),
        in_specs=[pl.BlockSpec(memory_space=pltpu.SMEM)] * 2
        + [packed_spec(seq_len), row]
        + [pl.BlockSpec((None, seq_len // len(grad_out), HEAD_DIM), lambda h: (batch, 0, h))]
        * len(grad_out)
        + saved_specs(heads, seq_len),
        out_specs=[packed_spec(seq_len), row],
        out_shape=[
            jax.ShapeDtypeStruct(projected.shape, BF16),
            jax.ShapeDtypeStruct(logits.shape, F32),
        ],
        scratch_shapes=[
            pltpu.VMEM((seq_len, HEAD_DIM), F32),
            pltpu.VMEM((seq_len, HEAD_DIM), F32),
            pltpu.VMEM((seq_len, HEAD_DIM), BF16),
            pltpu.VMEM((seq_len, TILE), BF16),
            pltpu.VMEM((seq_len, HEAD_DIM), BF16),
            pltpu.VMEM((seq_len, HEAD_DIM), BF16),
            pltpu.VMEM((seq_len, HEAD_DIM), BF16),
        ],
        name="attention_backward",
        compiler_params=pltpu.CompilerParams(vmem_limit_bytes=56 * 1024 * 1024),
        cost_estimate=cost(22),
    )(
        length if where is None else where,
        length,
        projected,
        logits,
        *grad_out,
        *saved,
    )
    return result[0], result[1]


def cost(microseconds):
    return pl.CostEstimate(
        flops=int(microseconds * COST_SCALE), bytes_accessed=1, transcendentals=0
    )


def params(mebibytes=56):
    return pltpu.CompilerParams(vmem_limit_bytes=mebibytes * 1024 * 1024)


def column(index, width):
    return pl.ds(pl.multiple_of(index * width, 128), width)


def row_norm(rows):
    return lax.rsqrt(jnp.mean(rows * rows, axis=-1, keepdims=True) + 1e-06)


def project_kernel(where_ref, p0, p1, p2, p3, w_ref, small_ref, gain_ref, h_ref, out_ref, logit_ref):
    def work(piece):
        rows = piece[...].astype(F32)
        normed = (rows * row_norm(rows) * gain_ref[...]).astype(BF16)
        h_ref[...] = normed
        for at in range(0, out_ref.shape[1], 512):
            out_ref[:, at : at + 512] = mm(normed, w_ref[:, at : at + 512]).astype(BF16)
        logit_ref[...] = mm_nt(small_ref[...], normed)

    for s, piece in enumerate((p0, p1, p2, p3)):
        pl.when(pl.program_id(0) == s)(functools.partial(work, piece))


def project(where, pieces, weight, small, gain, columns):
    part, width = pieces[0].shape
    rows = part * len(pieces)
    whole = lambda shape: pl.BlockSpec(shape, lambda i, w: (0, 0))
    return pl.pallas_call(
        project_kernel,
        grid_spec=pltpu.PrefetchScalarGridSpec(
            num_scalar_prefetch=1,
            grid=(len(pieces),),
            in_specs=[whole((part, width))] * 4
            + [whole(weight.shape), whole(small.shape), whole((1, width))],
            out_specs=[
                pl.BlockSpec((part, width), lambda i, w: (w[4 + i], 0)),
                pl.BlockSpec((part, columns), lambda i, w: (w[4 + i], 0)),
                pl.BlockSpec((small.shape[0], part), lambda i, w: (0, w[4 + i])),
            ],
        ),
        out_shape=[
            jax.ShapeDtypeStruct((rows, width), BF16),
            jax.ShapeDtypeStruct((rows, columns), BF16),
            jax.ShapeDtypeStruct((small.shape[0], rows), F32),
        ],
        name="project_rows",
        compiler_params=params(),
        cost_estimate=cost(9),
    )(where, *pieces, weight, small, gain)


def turn_kernel(where_ref, own_ref, other_ref, a_ref, b_ref, t_ref):
    own, other = own_ref[...], other_ref[...]
    a_ref[...] = own
    b_ref[...] = other
    rows = own.shape[0]
    t_ref[:, :rows] = own.T
    t_ref[:, rows:] = other.T


def turn_only_kernel(where_ref, own_ref, other_ref, t_ref):
    rows = own_ref.shape[0]
    t_ref[:, :rows] = own_ref[...].T
    t_ref[:, rows:] = other_ref[...].T


def turned(where, own, other, reorder):
    rows, width = own.shape
    block = width // 4
    place_in = (lambda i, w: (0, w[i])) if reorder else (lambda i, w: (0, i))
    flat = pl.BlockSpec((rows, block), lambda i, w: (0, i))
    tall = pl.BlockSpec((block, 2 * rows), lambda i, w: (i, 0))
    tall_shape = jax.ShapeDtypeStruct((width, 2 * rows), BF16)
    same = jax.ShapeDtypeStruct((rows, width), BF16)
    return pl.pallas_call(
        turn_kernel if reorder else turn_only_kernel,
        grid_spec=pltpu.PrefetchScalarGridSpec(
            num_scalar_prefetch=1,
            grid=(4,),
            in_specs=[pl.BlockSpec((rows, block), place_in)] * 2,
            out_specs=[flat, flat, tall] if reorder else [tall],
        ),
        out_shape=[same, same, tall_shape] if reorder else [tall_shape],
        name="turn_rows",
        compiler_params=params(),
        cost_estimate=cost(3),
    )(where, own, other)


def gather_pieces(refs, scratch, count):
    part, inner = refs[0].shape
    for i, ref in enumerate(refs):
        batch, s = i // count, i % count
        scratch[batch * part : (batch + 1) * part, s * inner : (s + 1) * inner] = ref[...]


def assemble(where_ref, block_ref, scratch):
    rows, inner = block_ref.shape[2:]
    for c in range(2):
        for s in range(4):
            scratch[c * rows : (c + 1) * rows, s * inner : (s + 1) * inner] = block_ref[c, s]


def middle_kernel(pieces, where_ref, *refs):
    att_refs = refs[:pieces]
    w_ref, x_ref, gain_ref, mid_ref, h_ref, att, total, gains, weight = refs[pieces:]
    step = pl.program_id(0)

    @pl.when(step == 0)
    def _():
        gather_pieces(att_refs, att, 4)
        total[...] = jnp.zeros_like(total)

    assemble(where_ref, w_ref, weight)
    block = weight.shape[0]
    mid = x_ref[...].astype(F32) + mm_nt(att[...], weight[...])
    at = column(step, block)
    mid_ref[:, at] = mid
    gains[:, at] = jnp.broadcast_to(gain_ref[...], (8, block))
    total[...] += jnp.broadcast_to(jnp.sum(mid * mid, axis=-1, keepdims=True), total.shape)

    @pl.when(step == 3)
    def _():
        scale = lax.rsqrt(total[:, :1] * (1.0 / (4 * block)) + 1e-06)
        h_ref[...] = (mid_ref[...] * scale * gains[:1, :]).astype(BF16)


def middle_rows(where, pieces, out_all, rows_low, gain):
    rows, width = rows_low.shape
    block = width // 4
    part, inner = pieces[0].shape
    full = pl.BlockSpec((rows, width), lambda i, w: (0, 0))
    return pl.pallas_call(
        functools.partial(middle_kernel, len(pieces)),
        grid_spec=pltpu.PrefetchScalarGridSpec(
            num_scalar_prefetch=1,
            grid=(4,),
            in_specs=[pl.BlockSpec((part, inner), lambda i, w: (0, 0))] * len(pieces)
            + [
                pl.BlockSpec((2,) + out_all.shape[1:], lambda i, w: (w[i], 0, 0, 0)),
                pl.BlockSpec((rows, block), lambda i, w: (0, w[i])),
                pl.BlockSpec((1, block), lambda i, w: (0, w[i])),
            ],
            out_specs=[full, full],
            scratch_shapes=[
                pltpu.VMEM((rows, 4 * inner), BF16),
                pltpu.VMEM((rows, 128), F32),
                pltpu.VMEM((8, width), F32),
                pltpu.VMEM((block, 4 * inner), BF16),
            ],
        ),
        out_shape=[
            jax.ShapeDtypeStruct((rows, width), F32),
            jax.ShapeDtypeStruct((rows, width), BF16),
        ],
        name="middle_rows",
        compiler_params=params(),
        cost_estimate=cost(5),
    )(where, *pieces, out_all, rows_low, gain)


def load_pieces(where_ref, pieces, weight, sems, base, cols):
    copies = []
    at = 0
    for i in range(len(pieces) if len(pieces) > 1 else 4):
        if len(pieces) > 1:
            piece = pieces[i]
            height = piece.shape[0]
            rows = pl.ds(0, height)
        else:
            piece = pieces[0]
            height = piece.shape[0] // 4
            rows = pl.ds(pl.multiple_of(where_ref[i] * height, 128), height)
        copies.append(
            pltpu.make_async_copy(
                piece.at[rows, cols], weight.at[pl.ds(at, height), :], sems.at[base + i]
            )
        )
        at += height
    return copies


def store(ref, cols, value):
    ref[:, cols] = value.astype(ref.dtype)


def feed_kernel(units, first, last, where_ref, *refs):
    h_own, h_other, c_own, c_other = refs[:4]
    pieces = refs[4 : len(refs) - (4 + (0 if first else 1) + (1 if last else 0))]
    rest = refs[4 + len(pieces) :]
    if not first:
        dh_sum, rest = rest[0], rest[1:]
    act_ref, *dh_refs, weight, sems = rest
    step = pl.program_id(0)

    @pl.when(step == 0)
    def _():
        copies = load_pieces(
            where_ref, pieces, weight, sems, 0, pl.ds(0, weight.shape[1])
        )
        for copy in copies:
            copy.start()
        for copy in copies:
            copy.wait()

    mine = step < 2
    pair = 2 * units
    h = jnp.where(mine, h_own[...], h_other[...])
    c = jnp.where(mine, c_own[...], c_other[...])
    for at in range(0, units, 256):
        cols = slice(at, at + 256)
        gate = mm(h, weight[:, cols])
        up = mm(h, weight[:, units + at : units + at + 256])
        dhidden = mm(c, weight[:, pair + at : pair + at + 256])
        sig = jax.nn.sigmoid(gate)
        silu = gate * sig
        act_ref[:, pair + at : pair + at + 256] = (silu * up).astype(BF16)
        act_ref[:, cols] = (dhidden * up * (sig + silu * (1.0 - sig))).astype(BF16)
        act_ref[:, units + at : units + at + 256] = (dhidden * silu).astype(BF16)
    width = weight.shape[0]
    act = act_ref[:, :pair]
    for at in range(0, width, 512):
        cols = slice(at, at + 512)
        dh = mm_nt(act, weight[cols, :pair])
        if not first:
            dh = dh + dh_sum[:, cols]
        if last:
            pl.when(mine)(functools.partial(store, dh_refs[0], cols, dh))
            pl.when(jnp.logical_not(mine))(functools.partial(store, dh_refs[1], cols, dh))
        else:
            dh_refs[0][:, cols] = dh


def feed_forward_part(where, h2, cot, pieces, total, last):
    rows, width = h2[0].shape
    columns = pieces[0].shape[1]
    tile = rows // 2
    first = total is None
    own = pl.BlockSpec((tile, width), lambda i: (jnp.minimum(i, 1), 0))
    other = pl.BlockSpec((tile, width), lambda i: (jnp.maximum(i - 2, 0), 0))
    flat = pl.BlockSpec((tile, width), lambda i: (i, 0))
    whole = pl.BlockSpec(memory_space=pl.ANY)
    sums = (
        [jax.ShapeDtypeStruct((rows, width), F32), jax.ShapeDtypeStruct((rows, width), BF16)]
        if last
        else [jax.ShapeDtypeStruct((2 * rows, width), F32)]
    )
    return pl.pallas_call(
        functools.partial(feed_kernel, columns // 3, first, last),
        grid=(4,),
        in_specs=[pl.BlockSpec(memory_space=pltpu.SMEM), own, other, own, other]
        + [whole] * len(pieces)
        + ([] if first else [flat]),
        out_specs=[pl.BlockSpec((tile, columns), lambda i: (i, 0))]
        + ([own, other] if last else [flat]),
        out_shape=[jax.ShapeDtypeStruct((2 * rows, columns), BF16)] + sums,
        scratch_shapes=[
            pltpu.VMEM((width, columns), BF16),
            pltpu.SemaphoreType.DMA((max(4, len(pieces)),)),
        ],
        input_output_aliases={} if first or last else {5 + len(pieces): 1},
        name="feed_forward",
        compiler_params=params(),
        cost_estimate=cost(15),
    )(where, *h2, *cot, *pieces, *([] if first else [total]))


def down_kernel(counts, where_ref, *refs):
    chunks = len(counts)
    acts = refs[:chunks]
    pieces = refs[chunks : chunks + sum(counts)]
    own_ref, other_ref, weight, sems = refs[chunks + sum(counts) :]
    units = weight.shape[2]
    step = pl.program_id(0)

    @pl.when(step == 0)
    def _():
        copies = []
        i = 0
        for c, count in enumerate(counts):
            copies += load_pieces(
                where_ref,
                pieces[i : i + count],
                weight.at[c],
                sems,
                len(copies),
                pl.ds(2 * units, units),
            )
            i += count
        for copy in copies:
            copy.start()
        for copy in copies:
            copy.wait()

    for at in range(0, weight.shape[1], 512):
        cols = slice(at, at + 512)
        total = mm_nt(acts[0][...], weight[0, cols, :])
        for c in range(1, chunks):
            total = total + mm_nt(acts[c][...], weight[c, cols, :])
        pl.when(step == 0)(functools.partial(store, own_ref, cols, total))
        pl.when(step == 1)(functools.partial(store, other_ref, cols, total))


def down_rows(where, acts, chunks, width):
    rows = acts[0].shape[0] // 2
    tile = rows
    units = acts[0].shape[1] // 3
    counts = tuple(len(pieces) for pieces in chunks)
    own = pl.BlockSpec((tile, width), lambda i: (0, 0))
    other = own
    return pl.pallas_call(
        functools.partial(down_kernel, counts),
        grid=(2,),
        in_specs=[pl.BlockSpec(memory_space=pltpu.SMEM)]
        + [pl.BlockSpec((tile, units), lambda i: (i, 2))] * len(acts)
        + [pl.BlockSpec(memory_space=pl.ANY)] * sum(counts),
        out_specs=[own, other],
        out_shape=[
            jax.ShapeDtypeStruct((rows, width), F32),
            jax.ShapeDtypeStruct((rows, width), BF16),
        ],
        scratch_shapes=[
            pltpu.VMEM((len(acts), width, units), BF16),
            pltpu.SemaphoreType.DMA((sum(max(4, count) for count in counts),)),
        ],
        name="down_rows",
        compiler_params=params(),
        cost_estimate=cost(10),
    )(where, *acts, *[piece for pieces in chunks for piece in pieces])


def whole_grad_kernel(where_ref, h_ref, c_ref, act, out_ref):
    def work(left):
        value = mm(left[...], act[...]).astype(out_ref.dtype)
        height = value.shape[0] // 2
        for b in range(2):
            at = pl.multiple_of(((where_ref[0] & 1) ^ b) * height, 128)
            out_ref[pl.ds(at, height), :] = value[b * height : (b + 1) * height]

    pl.when(pl.program_id(0) < 2)(functools.partial(work, h_ref))
    pl.when(pl.program_id(0) == 2)(functools.partial(work, c_ref))


def whole_weight_grads(where, h2_t, cot_t, act):
    width, rows = h2_t.shape
    columns = act.shape[1]
    third = columns // 3
    height = width // 2
    return pl.pallas_call(
        whole_grad_kernel,
        grid_spec=pltpu.PrefetchScalarGridSpec(
            num_scalar_prefetch=1,
            grid=(3, 2),
            in_specs=[
                pl.BlockSpec((height, rows), lambda i, j, w: (jnp.where(i < 2, j, 1), 0)),
                pl.BlockSpec((height, rows), lambda i, j, w: (jnp.where(i < 2, 0, j), 0)),
                pl.BlockSpec((rows, third), lambda i, j, w: (0, i)),
            ],
            out_specs=pl.BlockSpec((height, third), lambda i, j, w: ((w[0] >> 1) ^ j, i)),
        ),
        out_shape=jax.ShapeDtypeStruct((width, columns), BF16),
        name="whole_grads",
        compiler_params=params(),
        cost_estimate=cost(10),
    )(where, h2_t, cot_t, act)


def last_grad_kernel(pair, where_ref, h_ref, c_ref, act, *refs):
    added, (own_ref, other_ref, total) = refs[:-3], refs[-3:]
    for cols, left in ((slice(0, pair), h_ref), (slice(pair, None), c_ref)):
        value = mm(left[...], act[:, cols])
        for term in added:
            value = value + term[:, cols].astype(F32)
        total[:, cols] = value
    rows = own_ref.shape[0]
    own_ref[...] = total[pl.ds(pl.multiple_of(where_ref[16] * rows, 64), rows), :]
    other = pl.ds(pl.multiple_of((1 - where_ref[16]) * rows, 64), rows)
    other_ref[...] = total[other, :].astype(BF16)


def last_weight_grads(where, h2_t, cot_t, act, added):
    width, rows = h2_t.shape
    columns = act.shape[1]
    height = width // 4
    left = pl.BlockSpec((height, rows), lambda i: (0, 0))
    tile = pl.BlockSpec((height, columns), lambda i: (0, 0))
    half = pl.BlockSpec((height // 2, columns), lambda i: (0, 0))
    return pl.pallas_call(
        functools.partial(last_grad_kernel, 2 * columns // 3),
        grid=(1,),
        in_specs=[pl.BlockSpec(memory_space=pltpu.SMEM), left, left]
        + [pl.BlockSpec((rows, columns), lambda i: (0, 0))]
        + [tile] * len(added),
        out_specs=[half, half],
        out_shape=[
            jax.ShapeDtypeStruct((height // 2, columns), F32),
            jax.ShapeDtypeStruct((height // 2, columns), BF16),
        ],
        scratch_shapes=[pltpu.VMEM((height, columns), F32)],
        name="last_weight_grad",
        compiler_params=params(),
        cost_estimate=cost(4),
    )(where, h2_t, cot_t, act, *[term for term, _ in added])


def finish_kernel(where_ref, own_ref, recv_ref, *outs):
    half = own_ref.shape[1] // 3
    for i, out in enumerate(outs):
        cols = slice(i * half, (i + 1) * half)
        out[:, column(where_ref[16], half)] = own_ref[:, cols]
        out[:, column(1 - where_ref[16], half)] = recv_ref[:, cols].astype(F32)


def finish_grads(where, own, recv):
    rows, columns = own.shape
    flat = pl.BlockSpec((rows, columns), lambda i: (0, 0))
    wide = pl.BlockSpec((rows, 2 * columns // 3), lambda i: (0, 0))
    return pl.pallas_call(
        finish_kernel,
        grid=(1,),
        in_specs=[pl.BlockSpec(memory_space=pltpu.SMEM), flat, flat],
        out_specs=[wide] * 3,
        out_shape=[jax.ShapeDtypeStruct((rows, 2 * columns // 3), F32)] * 3,
        name="finish_grads",
        compiler_params=params(),
        cost_estimate=cost(2),
    )(where, own, recv)


def grad_kernel(plan, *refs):
    count = len(plan)
    hs, cs, act = refs[:count], refs[count : 2 * count], refs[2 * count]
    extra = list(refs[2 * count + 1 : -1])
    out_ref = refs[-1]
    height = hs[0].shape[0]

    def work(lefts):
        at = 0
        for i, terms in enumerate(plan):
            value = mm(lefts[i][...], act[...])
            for term in extra[at : at + terms]:
                value = value + term[...].astype(F32)
            at += terms
            out_ref[i * height : (i + 1) * height, :] = value.astype(out_ref.dtype)

    pl.when(pl.program_id(0) < 2)(functools.partial(work, hs))
    pl.when(pl.program_id(0) == 2)(functools.partial(work, cs))


def weight_grads(h2_t, cot_t, act, blocks, added):
    width, rows = h2_t.shape
    columns = act.shape[1]
    height = width // 4
    third = columns // 3
    whole = len(blocks) * height
    if blocks == [2, 3]:
        height, blocks, added = 2 * height, [1], [[]]
    left = [pl.BlockSpec((height, rows), lambda i, at=at: (at, 0)) for at in blocks]
    terms = [term for group in added for term in group]
    tiles = [pl.BlockSpec((height, third), lambda i, at=at: (at, i)) for _, at in terms]
    return pl.pallas_call(
        functools.partial(grad_kernel, tuple(len(g) for g in added)),
        grid=(3,),
        in_specs=left + left + [pl.BlockSpec((rows, third), lambda i: (0, i))] + tiles,
        out_specs=pl.BlockSpec((whole, third), lambda i: (0, i)),
        out_shape=jax.ShapeDtypeStruct((whole, columns), BF16),
        name="weight_grads",
        compiler_params=params(),
        cost_estimate=cost(1 + whole // 192),
    )(*([h2_t] * len(blocks)), *([cot_t] * len(blocks)), act, *[term for term, _ in terms])


def norm_two_kernel(
    where_ref, own_ref, recv_ref, mid_ref, cot_ref, gain_ref, w_ref,
    dmid_ref, dm_ref, datt_ref, dgain_ref, weight,
):
    block = gain_ref.shape[1] // 4
    mid = mid_ref[...]
    scale = row_norm(mid)
    gain = jnp.concatenate([gain_ref[:, column(where_ref[j], block)] for j in range(4)], axis=1)
    upstream = own_ref[...] + recv_ref[...].astype(F32)
    weighted = upstream * gain
    inner = jnp.mean(mid * weighted, axis=-1, keepdims=True)
    grad = cot_ref[...].astype(F32) + scale * weighted - mid * (scale * scale * scale) * inner
    dmid_ref[...] = grad
    low = grad.astype(BF16)
    dm_ref[...] = low
    dgain = jnp.sum(upstream * mid * scale, axis=0, keepdims=True)

    @pl.when(pl.program_id(0) == 0)
    def _():
        dgain_ref[...] = jnp.zeros_like(dgain_ref)

    for j in range(4):
        at = column(where_ref[j], block)
        dgain_ref[0:1, at] = dgain_ref[0:1, at] + dgain[:, j * block : (j + 1) * block]
    total = None
    for j in range(4):
        for c in range(2):
            for s in range(4):
                rows, inner_width = w_ref.shape[2:]
                weight[c * rows : (c + 1) * rows, s * inner_width : (s + 1) * inner_width] = w_ref[
                    2 * where_ref[j] + c, s
                ]
        term = mm(low[:, j * block : (j + 1) * block], weight[...])
        total = term if total is None else total + term
    inner_width = datt_ref.shape[3]
    for s in range(4):
        datt_ref[s, 0] = total[:, s * inner_width : (s + 1) * inner_width].astype(BF16)


def norm_two(where, own, recv, middle, cot, gain, out_all, count):
    rows, width = middle.shape
    part = rows // count
    inner = out_all.shape[3]
    flat = pl.BlockSpec((part, width), lambda i, w: (i, 0))
    row = pl.BlockSpec((1, width), lambda i, w: (0, 0))
    return pl.pallas_call(
        norm_two_kernel,
        grid_spec=pltpu.PrefetchScalarGridSpec(
            num_scalar_prefetch=1,
            grid=(count,),
            in_specs=[flat] * 4
            + [row, pl.BlockSpec(out_all.shape, lambda i, w: (0, 0, 0, 0))],
            out_specs=[
                flat,
                flat,
                pl.BlockSpec((4, 1, part, inner), lambda i, w: (0, i, 0, 0)),
                row,
            ],
            scratch_shapes=[pltpu.VMEM((width // 4, 4 * inner), BF16)],
        ),
        out_shape=[
            jax.ShapeDtypeStruct((rows, width), F32),
            jax.ShapeDtypeStruct((rows, width), BF16),
            jax.ShapeDtypeStruct((4, count, part, inner), BF16),
            jax.ShapeDtypeStruct((1, width), F32),
        ],
        name="norm_two",
        compiler_params=params(),
        cost_estimate=cost(6),
    )(where, own, recv, middle, cot, gain, out_all)


def dh1_kernel(where_ref, d_ref, l_ref, h_ref, w_ref, small_ref, gain_ref, out_ref, dgain_ref):
    columns = d_ref.shape[1]
    step = pl.program_id(0)

    @pl.when(step == 0)
    def _():
        dgain_ref[...] = jnp.zeros_like(dgain_ref)

    grads = d_ref[...]
    for at in range(0, w_ref.shape[0], 512):
        cols = slice(at, at + 512)
        total = mm_nt(grads, w_ref[cols, :columns]) + mm_tn(l_ref[...], small_ref[:, cols])
        out_ref[0, :, cols] = total.astype(BF16)
        part = jnp.sum(total * h_ref[:, cols].astype(F32), axis=0, keepdims=True)
        dgain_ref[:, cols] = dgain_ref[:, cols] + part

    @pl.when(step == 3)
    def _():
        dgain_ref[...] = dgain_ref[...] / gain_ref[...]


def dh1_pieces(where, dprojected, dlogits, normed, weight, small, gain):
    rows, columns = dprojected.shape
    width = weight.shape[0]
    part = rows // 4
    whole = lambda shape: pl.BlockSpec(shape, lambda i, w: (0, 0))
    return pl.pallas_call(
        dh1_kernel,
        grid_spec=pltpu.PrefetchScalarGridSpec(
            num_scalar_prefetch=1,
            grid=(4,),
            in_specs=[
                pl.BlockSpec((part, columns), lambda i, w: (w[7 - i], 0)),
                pl.BlockSpec((dlogits.shape[0], part), lambda i, w: (0, w[7 - i])),
                pl.BlockSpec((part, width), lambda i, w: (w[7 - i], 0)),
                whole(weight.shape),
                whole(small.shape),
                whole(gain.shape),
            ],
            out_specs=[
                pl.BlockSpec((1, part, width), lambda i, w: (3 - i, 0, 0)),
                whole(gain.shape),
            ],
        ),
        out_shape=[
            jax.ShapeDtypeStruct((4, part, width), BF16),
            jax.ShapeDtypeStruct(gain.shape, F32),
        ],
        name="dh1_rows",
        compiler_params=params(),
        cost_estimate=cost(0.008),
    )(where, dprojected, dlogits, normed, weight, small, gain)


def store_cores(where_ref, out_ref, cols, values):
    rows = values.shape[0] // 2
    for c in range(2):
        out_ref[jnp.where(where_ref[16] == c, 0, 1), :, cols] = values[
            c * rows : (c + 1) * rows
        ]


def attn_grad_kernel(count, beta, where_ref, *refs):
    hs, ds, ls = refs[:count], refs[count : 2 * count], refs[2 * count : 3 * count]
    gains, gain_two, out_ref = refs[3 * count : 4 * count], refs[4 * count], refs[4 * count + 1]
    columns = ds[0].shape[1]
    lefts = [h[...].T for h in hs]
    for at in range(0, columns, 512):
        cols = slice(at, at + 512)
        total = mm(lefts[0], ds[0][:, cols])
        for i in range(1, count):
            total = total + mm(lefts[i], ds[i][:, cols])
        store_cores(where_ref, out_ref, cols, total.astype(BF16))
    small = mm_nt(lefts[0], ls[0][...])
    for i in range(1, count):
        small = small + mm_nt(lefts[i], ls[i][...])
    gain_one = gains[0][...]
    for i in range(1, count):
        gain_one = gain_one + gains[i][...]
    extra = ls[0].shape[0]
    width = gain_one.shape[1]
    line = lax.broadcasted_iota(jnp.int32, (extra, width), 0)
    rows = jnp.where(line == beta, gain_one, jnp.where(line == beta + 1, gain_two[...], 0.0))
    eye = lax.broadcasted_iota(jnp.int32, (extra, extra), 0) == lax.broadcasted_iota(
        jnp.int32, (extra, extra), 1
    )
    small = small + mm_tn(rows, eye.astype(BF16))
    store_cores(where_ref, out_ref, slice(columns, None), small.astype(BF16))


def attn_grads(where, normed, dprojected, dlogits, gains, gain_two, beta):
    rows, width = normed[0].shape
    columns = dprojected[0].shape[1]
    extra = dlogits[0].shape[0]
    count = len(normed)
    block = width // 4
    whole = lambda shape: pl.BlockSpec(shape, lambda i: (0, 0))
    return pl.pallas_call(
        functools.partial(attn_grad_kernel, count, beta),
        grid=(4,),
        in_specs=[pl.BlockSpec(memory_space=pltpu.SMEM)]
        + [pl.BlockSpec((rows, block), lambda i: (0, i))] * count
        + [whole((rows, columns))] * count
        + [whole((extra, rows))] * count
        + [pl.BlockSpec((1, block), lambda i: (0, i))] * (count + 1),
        out_specs=pl.BlockSpec((2, block // 2, columns + extra), lambda i: (0, i, 0)),
        out_shape=jax.ShapeDtypeStruct((2, width // 2, columns + extra), BF16),
        name="attn_grads",
        compiler_params=params(),
        cost_estimate=cost(14),
    )(where, *normed, *dprojected, *dlogits, *gains, gain_two)


def out_grad_kernel(pieces, where_ref, *refs):
    dm_ref, out_ref, att = refs[pieces:]

    @pl.when(pl.program_id(0) == 0)
    def _():
        gather_pieces(refs[:pieces], att, 4)

    total = mm_tn(dm_ref[...], att[...]).astype(BF16)
    rows, inner = out_ref.shape[3:]
    for c in range(2):
        for s in range(4):
            out_ref[jnp.where(where_ref[16] == c, 0, 1), 0, s] = total[
                c * rows : (c + 1) * rows, s * inner : (s + 1) * inner
            ]


def out_grads(where, pieces, dm):
    rows, width = dm.shape
    part, inner = pieces[0].shape
    block = width // 4
    return pl.pallas_call(
        functools.partial(out_grad_kernel, len(pieces)),
        grid_spec=pltpu.PrefetchScalarGridSpec(
            num_scalar_prefetch=1,
            grid=(4,),
            in_specs=[pl.BlockSpec((part, inner), lambda i, w: (0, 0))] * len(pieces)
            + [pl.BlockSpec((rows, block), lambda i, w: (0, i))],
            out_specs=pl.BlockSpec((2, 1, 4, block // 2, inner), lambda i, w: (0, w[i], 0, 0, 0)),
            scratch_shapes=[pltpu.VMEM((rows, 4 * inner), BF16)],
        ),
        out_shape=jax.ShapeDtypeStruct((2, 4, 4, block // 2, inner), BF16),
        name="out_grads",
        compiler_params=params(),
        cost_estimate=cost(5),
    )(where, *pieces, dm)


def block_out_kernel(where_ref, mid_ref, own_ref, recv_ref, out_ref):
    total = mid_ref[...] + own_ref[...] + recv_ref[...].astype(F32)
    out_ref[...] = total.astype(out_ref.dtype)


def block_out_rows(where, middle, own, recv):
    rows, width = middle.shape
    block = width // 4
    flat = pl.BlockSpec((rows, block), lambda i, w: (0, i))
    return pl.pallas_call(
        block_out_kernel,
        grid_spec=pltpu.PrefetchScalarGridSpec(
            num_scalar_prefetch=1,
            grid=(4,),
            in_specs=[flat] * 3,
            out_specs=pl.BlockSpec((rows, block), lambda i, w: (0, w[i])),
        ),
        out_shape=jax.ShapeDtypeStruct((rows, width), BF16),
        name="block_out",
        compiler_params=params(),
        cost_estimate=cost(4),
    )(where, middle, own, recv)


def input_grad_kernel(where_ref, x_ref, own_ref, recv_ref, dmid_ref, gain_ref, *refs):
    out_ref = refs[-1]
    rows = x_ref[...].astype(F32)
    scale = row_norm(rows)
    weighted = (own_ref[...].astype(F32) + recv_ref[...].astype(F32)) * gain_ref[...]
    inner = jnp.mean(rows * weighted, axis=-1, keepdims=True)
    out_ref[...] = scale * weighted - rows * (scale * scale * scale) * inner
    block = rows.shape[1] // 4
    for j in range(4):
        at = column(where_ref[j], block)
        out_ref[:, at] = out_ref[:, at] + dmid_ref[:, j * block : (j + 1) * block]


def input_grad_rows(where, rows_low, pieces, recv, dmiddle, gain, batch, total):
    _, part, width = pieces.shape
    own = pl.BlockSpec((None, part // 2, width), lambda i, w: (0, i, 0))
    flat = pl.BlockSpec((part // 2, width), lambda i, w: (i, 0))
    later = pl.BlockSpec((part // 2, width), lambda i, w: (i + 2 * batch, 0))
    first = total is None
    return pl.pallas_call(
        input_grad_kernel,
        grid_spec=pltpu.PrefetchScalarGridSpec(
            num_scalar_prefetch=1,
            grid=(2,),
            in_specs=[later, own, flat, later, pl.BlockSpec((1, width), lambda i, w: (0, 0))]
            + ([] if first else [pl.BlockSpec(memory_space=pl.ANY)]),
            out_specs=later,
        ),
        out_shape=jax.ShapeDtypeStruct(dmiddle.shape, F32),
        input_output_aliases={} if first else {6: 0},
        name="input_grad",
        compiler_params=params(),
        cost_estimate=cost(3),
    )(where, rows_low, pieces, recv, dmiddle, gain, *([] if first else [total]))


def product(left_side, right_side):
    return jnp.dot(left_side, right_side, preferred_element_type=F32)


def by_transposed(left_side, right_side):
    return lax.dot_general(
        left_side, right_side, (((1,), (1,)), ((), ())), preferred_element_type=F32
    )


def transposed_by(left_side, right_side):
    return lax.dot_general(
        left_side, right_side, (((0,), (0,)), ((), ())), preferred_element_type=F32
    )


def shift(values, axis, step):
    size = lax.axis_size(axis)
    return lax.ppermute(values, axis, [(i, (i + step) % size) for i in range(size)])


def ring_gather(values, axis):
    pieces = [values]
    for _ in range(lax.axis_size(axis) - 1):
        pieces.append(shift(pieces[-1], axis, 1))
    return pieces


def ring_scatter(pieces, axis):
    total = pieces[-1].astype(BF16)
    for piece in pieces[-2::-1]:
        total = shift(total, axis, -1).astype(F32) + piece.astype(F32)
        if piece is not pieces[0]:
            total = total.astype(BF16)
    return total


def row_scale(rows):
    return lax.rsqrt(jnp.mean(rows * rows, axis=-1, keepdims=True) + 1e-06)


def norm_back(rows, scale, gain, upstream):
    weighted = upstream * gain
    inner = jnp.mean(rows * weighted, axis=-1, keepdims=True)
    grad = scale * weighted - rows * (scale * scale * scale) * inner
    return grad, jnp.sum(upstream * rows * scale, axis=0)


def place(pieces, axis, order):
    size = lax.axis_size(axis)
    index = lax.axis_index(axis)
    height = pieces[0].shape[0]
    whole = jnp.zeros((size * height,) + pieces[0].shape[1:], pieces[0].dtype)
    for s, piece in enumerate(pieces):
        at = ((index + order * s) % size) * height
        whole = lax.dynamic_update_slice_in_dim(whole, piece, at, 0)
    return whole


def cut(whole, axis, step):
    size = lax.axis_size(axis)
    height = whole.shape[0] // size
    at = ((lax.axis_index(axis) + step) % size) * height
    return lax.dynamic_slice_in_dim(whole, at, height, 0)


def by_core(own, other, axis):
    first = lax.axis_index("core") == 0
    return jnp.where(
        first, jnp.concatenate([own, other], axis), jnp.concatenate([other, own], axis)
    )


def general_body(
    tokens,
    lengths,
    cotangent,
    q_weight,
    k_weight,
    v_weight,
    direction_weight,
    beta_weight,
    out_weight,
    gate_weight,
    up_weight,
    down_weight,
    norm_gain_one,
    norm_gain_two,
):
    zsize = lax.axis_size("head")
    core = lax.axis_index("core")
    plane = ("da", "db")
    dp = ("da", "db", "core")
    micro, slots, part, width = tokens.shape
    count = micro * slots
    local = count * part
    shard = q_weight.shape[0]
    heads = beta_weight.shape[1]
    inner = heads * HEAD_DIM
    half = gate_weight.shape[1] // 2
    rows_low = tokens.reshape(count, part, width)
    rows_in = rows_low.reshape(local, width).astype(F32)
    cot_own = cotangent.reshape(local, width)
    seq_lengths = lengths.reshape(count)

    sequences = [place(ring_gather(rows_low[i], "head"), "head", -1) for i in range(count)]

    small = jnp.concatenate(
        [beta_weight.T, norm_gain_one[None, :], norm_gain_two[None, :]], axis=0
    )
    small = lax.all_gather(small, dp, axis=1, tiled=True)
    beta_rows = small[:heads]
    gain_one = small[heads].astype(F32)
    gain_two = small[heads + 1].astype(F32)
    attn_local = jnp.stack(
        [w.reshape(shard, heads, HEAD_DIM) for w in (q_weight, k_weight, v_weight, direction_weight)],
        axis=2,
    ).reshape(shard, 4 * inner)
    attn_weight = lax.all_gather(attn_local, dp, axis=0, tiled=True)
    out_pieces = ring_gather(out_weight.T, "head")
    out_all = jnp.concatenate(out_pieces, axis=1)
    out_all = lax.all_gather(out_all, dp, axis=0, tiled=True)
    ffn_local = jnp.concatenate(
        [w.reshape(shard, 2, half) for w in (gate_weight, up_weight, down_weight.T)], axis=2
    )
    ffn_own = lax.dynamic_index_in_dim(ffn_local, core, 1, keepdims=False)
    ffn_other = lax.dynamic_index_in_dim(ffn_local, 1 - core, 1, keepdims=False)
    ffn_other = shift(ffn_other, "core", 1)
    ffn_chip = by_core(ffn_own, ffn_other, 0)
    ffn_weight = [
        lax.all_gather(w, plane, axis=0, tiled=True) for w in ring_gather(ffn_chip, "head")
    ]

    normed, projected, logits, kept, mixed = [], [], [], [], []
    for i in range(count):
        rows = sequences[i].astype(F32)
        h1 = (rows * row_scale(rows) * gain_one).astype(BF16)
        normed.append(h1)
        projected.append(product(h1, attn_weight).astype(BF16))
        logits.append(by_transposed(beta_rows, h1))
        result = attention_forward(None, seq_lengths[i : i + 1], projected[i], logits[i])
        kept.append(result[1:])
        pieces = [cut(result[0], "head", 0)]
        for s in range(1, zsize):
            pieces.append(shift(cut(result[0], "head", s), "head", s))
        mixed.append(jnp.concatenate(pieces, axis=1))
    attended = jnp.concatenate(mixed, axis=0)
    middle = rows_in + by_transposed(attended, out_all)
    scale_two = row_scale(middle)
    h2_own = (middle * scale_two * gain_two).astype(BF16)
    h2 = jnp.concatenate([h2_own, shift(h2_own, "core", 1)], axis=0)
    cot = jnp.concatenate([cot_own, shift(cot_own, "core", 1)], axis=0)

    out_sum = None
    dh2_sum = None
    ffn_terms = []
    for weight in ffn_weight:
        gate_up = product(h2, weight[:, : 2 * half])
        dhidden = product(cot, weight[:, 2 * half :])
        gate = gate_up[:, :half]
        up = gate_up[:, half:]
        sig = jax.nn.sigmoid(gate)
        hidden = (gate * sig * up).astype(BF16)
        dgate = (dhidden * up * sig * (1.0 + gate * (1.0 - sig))).astype(BF16)
        dup = (dhidden * gate * sig).astype(BF16)
        dgate_up = jnp.concatenate([dgate, dup], axis=1)
        out_part = by_transposed(hidden, weight[:, 2 * half :])
        dh2_part = by_transposed(dgate_up, weight[:, : 2 * half])
        out_sum = out_part if out_sum is None else out_sum + out_part
        dh2_sum = dh2_part if dh2_sum is None else dh2_sum + dh2_part
        ffn_terms.append(
            jnp.concatenate(
                [
                    transposed_by(h2, dgate_up).astype(BF16),
                    transposed_by(cot, hidden).astype(BF16),
                ],
                axis=1,
            )
        )
    dh2 = dh2_sum[:local] + shift(dh2_sum[local:].astype(BF16), "core", 1).astype(F32)
    down = out_sum[:local] + shift(out_sum[local:].astype(BF16), "core", 1).astype(F32)
    block_out = (middle + down).astype(BF16)
    dmid, gain_two_grad = norm_back(middle, scale_two, gain_two, dh2)
    dmiddle = cot_own.astype(F32) + dmid
    dm = dmiddle.astype(BF16)
    dattended = product(dm, out_all).astype(BF16)
    out_term = transposed_by(dm, attended).astype(BF16)

    attn_term = None
    beta_term = None
    dh1_parts = []
    for i in range(count):
        rows = dattended[i * part : (i + 1) * part]
        pieces = [rows[:, :inner]]
        for s in range(1, zsize):
            pieces.append(shift(rows[:, s * inner : (s + 1) * inner], "head", -s))
        grad_out = place(pieces, "head", 1)
        dprojected, dlogits = attention_backward(
            None, seq_lengths[i : i + 1], projected[i], logits[i], [grad_out[None]], 0, kept[i]
        )
        dlogits = dlogits.astype(BF16)
        dh1 = by_transposed(dprojected, attn_weight) + transposed_by(dlogits, beta_rows)
        dh1 = dh1.astype(BF16)
        dh1_parts.append(ring_scatter([cut(dh1, "head", -s) for s in range(zsize)], "head"))
        term = transposed_by(normed[i], dprojected)
        attn_term = term if attn_term is None else attn_term + term
        term = product(dlogits, normed[i])
        beta_term = term if beta_term is None else beta_term + term
    dh1 = jnp.concatenate(dh1_parts, axis=0)
    scale_one = row_scale(rows_in)
    drows, gain_one_grad = norm_back(rows_in, scale_one, gain_one, dh1)
    input_grad = dmiddle + drows

    ffn_total = ring_scatter(
        [lax.psum_scatter(t, plane, scatter_dimension=0, tiled=True) for t in ffn_terms], "head"
    )
    ffn_total = ffn_total.reshape(2, shard, 3 * half)
    own = lax.dynamic_index_in_dim(ffn_total, core, 0, keepdims=False)
    other = lax.dynamic_index_in_dim(ffn_total, 1 - core, 0, keepdims=False)
    other = shift(other.astype(BF16), "core", 1).astype(F32)
    gate_grad, up_grad, down_grad = [
        by_core(own[:, j * half : (j + 1) * half], other[:, j * half : (j + 1) * half], 1)
        for j in range(3)
    ]
    out_total = lax.psum_scatter(out_term, dp, scatter_dimension=0, tiled=True)
    out_total = ring_scatter(
        [out_total[:, s * inner : (s + 1) * inner] for s in range(zsize)], "head"
    )
    attn_total = lax.psum_scatter(attn_term.astype(BF16), dp, scatter_dimension=0, tiled=True)
    attn_total = attn_total.astype(F32).reshape(shard, heads, 4, HEAD_DIM)
    small_term = jnp.concatenate(
        [beta_term, gain_one_grad[None, :], gain_two_grad[None, :]], axis=0
    )
    small_total = lax.psum_scatter(small_term, dp, scatter_dimension=1, tiled=True)
    gain_grads = lax.psum(small_total[heads:], "head")
    shape = (micro, slots, part, width)
    return (
        block_out.reshape(shape),
        input_grad.reshape(shape),
        attn_total[:, :, 0].reshape(shard, inner),
        attn_total[:, :, 1].reshape(shard, inner),
        attn_total[:, :, 2].reshape(shard, inner),
        attn_total[:, :, 3].reshape(shard, inner),
        small_total[:heads].T,
        out_total.T,
        gate_grad,
        up_grad,
        down_grad.T,
        gain_grads[0],
        gain_grads[1],
    )


def after(values, others):
    return lax.optimization_barrier((values, others))[0]


def swap(values, axis, mask):
    size = lax.axis_size(axis)
    return lax.ppermute(values, axis, [(i, i ^ mask) for i in range(size)])


def plane_swap(values, mask):
    return lax.ppermute(values, ("da", "db"), [(i, i ^ mask) for i in range(4)])


class Plan:
    def __init__(self):
        self.made = {}
        self.waiting = []
        self.last = None

    def get(self, name):
        return self.made[name]

    def send(self, name, needs, start):
        self.waiting.append((name, needs, start))
        self.flush()

    def flush(self):
        progress = True
        while progress:
            progress = False
            for item in list(self.waiting):
                name, needs, start = item
                gates = PLAN["gates"].get(name, [])
                if all(need in self.made for need in list(needs) + list(gates)):
                    self.waiting.remove(item)
                    values = [self.made[need] for need in needs]
                    if gates:
                        values[0] = after(values[0], [self.made[gate] for gate in gates])
                    self.made[name] = start(*values)
                    progress = True

    def put(self, name, value):
        self.made[name] = value
        self.flush()

    def step(self, name, value, work):
        holds = [self.made[pin] for pin in PLAN["pins"].get(name, []) if pin in self.made]
        if self.last is not None:
            holds.append(self.last)
        result = work(after(value, holds) if holds else value)
        self.last = result[0] if isinstance(result, (tuple, list)) else result
        self.put(name, result)


def body(
    tokens,
    lengths,
    cotangent,
    q_weight,
    k_weight,
    v_weight,
    direction_weight,
    beta_weight,
    out_weight,
    gate_weight,
    up_weight,
    down_weight,
    norm_gain_one,
    norm_gain_two,
):
    plan = Plan()
    get, put, send, step = plan.get, plan.put, plan.send, plan.step
    core = lax.axis_index("core")
    z = lax.axis_index("head")
    plane_at = [
        (lax.axis_index("da") ^ a) * 2 + (lax.axis_index("db") ^ b)
        for a in range(2)
        for b in range(2)
    ]
    where = jnp.stack(
        plane_at
        + [(z - s) % 4 for s in range(4)]
        + [(z + s) % 4 for s in range(4)]
        + [(p - z) % 4 for p in range(4)]
        + [core]
    ).astype(jnp.int32)
    dp = ("da", "db", "core")
    micro, slots, part, width = tokens.shape
    count = micro * slots
    local = count * part
    shard = q_weight.shape[0]
    heads = beta_weight.shape[1]
    inner = heads * HEAD_DIM
    columns = 4 * inner
    half = gate_weight.shape[1] // 2
    rows_low = tokens.reshape(count, part, width)
    flat_low = rows_low.reshape(local, width)
    cot_own = cotangent.reshape(local, width)
    seq_lengths = lengths.reshape(count)
    ahead = lambda values: shift(values, "head", 1)
    back = lambda values: shift(values, "head", -1)

    attn_local = jnp.stack(
        [w.reshape(shard, heads, HEAD_DIM) for w in (q_weight, k_weight, v_weight, direction_weight)],
        axis=2,
    ).reshape(shard, columns)
    small = jnp.concatenate(
        [beta_weight, norm_gain_one[:, None], norm_gain_two[:, None]], axis=1
    )
    small = jnp.pad(small, ((0, 0), (0, 128 - small.shape[1])))
    put(ATTN_ROWS, jnp.concatenate([attn_local, small], axis=1))
    put(OUT_ROWS, out_weight.T)
    ffn_local = jnp.concatenate(
        [w.reshape(shard, 2, half) for w in (gate_weight, up_weight, down_weight.T)], axis=2
    )
    put(FFN_OWN, lax.dynamic_index_in_dim(ffn_local, core, 1, keepdims=False))
    put(FFN_GIVE, lax.dynamic_index_in_dim(ffn_local, 1 - core, 1, keepdims=False))
    put(COT, cot_own)

    send(ATTN, [ATTN_ROWS], lambda v: lax.all_gather(v, dp, axis=0, tiled=True))
    send(FFN_TAKE, [FFN_GIVE], lambda v: swap(v, "core", 1))
    send((HOP, 0), [FFN_TAKE, FFN_OWN], lambda take, own: by_core(own, take, 0))
    for i in range(count):
        put((TOK, i, 0), rows_low[i])
        for s in range(1, 4):
            send((TOK, i, s), [(TOK, i, s - 1)], ahead)
    for s in range(1, 4):
        send((HOP, s), [(HOP, s - 1)], ahead)
    for s in range(4):
        if s in PLAN["direct"]:
            for mask in range(1, 4):
                send((CHUNK, s, mask), [(HOP, s)], lambda v, mask=mask: plane_swap(v, mask))
        else:
            send(
                (CHUNK, s, 0),
                [(HOP, s)],
                lambda v: lax.all_gather(v, ("da", "db"), axis=0, tiled=True),
            )
    for s in range(1, 4):
        send((OUT, s), [OUT_ROWS], lambda v, s=s: shift(v, "head", s))
    send(
        OUT_ALL,
        [(OUT, 1), (OUT, 2), (OUT, 3)],
        lambda *v: lax.all_gather(
            jnp.concatenate([out_weight.T] + list(v), axis=0), dp, axis=0, tiled=True
        ),
    )
    send(COT_OTHER, [COT], lambda v: swap(v, "core", 1))

    def chunk(s):
        if s in PLAN["direct"]:
            return [get((HOP, s))] + [get((CHUNK, s, mask)) for mask in range(1, 4)]
        return [get((CHUNK, s, 0))]

    def small_rows():
        turned_small = get(ATTN)[:, columns:].T
        gains = [turned_small[heads + i : heads + i + 1].astype(F32) for i in range(2)]
        return turned_small[:8], gains[0], gains[1]

    def mixed():
        pieces = []
        for i in range(count):
            pieces += [get((ATTEND, i))[0][0]] + [get((MIX, i, s)) for s in range(1, 4)]
        return pieces

    def project_step(i):
        small8, gain_one, _ = small_rows()
        pieces = [get((TOK, i, s)) for s in range(1, 4)]
        step(
            (PROJECT, i),
            rows_low[i],
            lambda v: project(where, [v] + pieces, get(ATTN), small8, gain_one, columns)[::-1],
        )

    def forward_step(i):
        logit, packed, _ = get((PROJECT, i))
        step(
            (ATTEND, i),
            packed,
            lambda v: attention_forward(where, seq_lengths[i : i + 1], v, logit),
        )
        for s in range(1, 4):
            send((MIX, i, s), [(ATTEND, i)], lambda v, s=s: shift(v[0][s], "head", s))

    def turn_cot():
        step(
            TURN_COT, cot_own, lambda v: turned(where, v, get(COT_OTHER), True)
        )

    def middle_step():
        pieces = mixed()
        out_all = get(OUT_ALL).reshape(8, 4, shard, inner)
        _, _, gain_two = small_rows()
        step(
            MIDDLE,
            pieces[0],
            lambda v: middle_rows(where, [v] + pieces[1:], out_all, flat_low, gain_two)[::-1],
        )
        send(H2_OTHER, [MIDDLE], lambda v: swap(v[0], "core", 1))

    def feed_step(s):
        total = get((FEED, s - 1))[1] if s else None
        h2 = get(MIDDLE)[0]
        step(
            (FEED, s),
            h2,
            lambda v: feed_forward_part(
                where, (v, get(H2_OTHER)), get(TURN_COT)[:2], chunk(s), total, s == 3
            ),
        )
        if s == 3:
            send(DH_OTHER, [(FEED, 3)], lambda v: swap(v[2], "core", 1))

    def turn_h2():
        step(TURN_H2, get(MIDDLE)[0], lambda v: turned(where, v, get(H2_OTHER), False)[0])

    def grads(name, c, blocks, added):
        step(
            name,
            get((FEED, c))[0],
            lambda v: weight_grads(get(TURN_H2), get(TURN_COT)[2], v, blocks, added),
        )

    def far_step(c):
        if c in PLAN["whole"]:
            step(
                (GRAD_FAR, c),
                get((FEED, c))[0],
                lambda v: whole_weight_grads(where, get(TURN_H2), get(TURN_COT)[2], v),
            )
            send(
                (PLANE_SUM, c),
                [(GRAD_FAR, c)],
                lambda v: lax.psum_scatter(v, ("da", "db"), scatter_dimension=0, tiled=True),
            )
            if c == 1:
                send((SUM, c), [(PLANE_SUM, c)], ahead)
            else:
                send(
                    (SUM, c),
                    [(PLANE_SUM, c), (SUM, c - 1)],
                    lambda v, last: ahead((v.astype(F32) + last.astype(F32)).astype(BF16)),
                )
            return
        first = c in PLAN["da_first"]
        grads((GRAD_FAR, c), c, [2, 3] if first else [1, 3], [[], []])
        send((FAR, c), [(GRAD_FAR, c)], lambda v: swap(v, "da" if first else "db", 1))

    def middle_grads(c):
        if c in PLAN["whole"]:
            return
        first = c in PLAN["da_first"]
        grads((GRAD_MIDDLE, c), c, [1] if first else [2], [[(get((FAR, c)), 1)]])
        send((MID, c), [(GRAD_MIDDLE, c)], lambda v: swap(v, "db" if first else "da", 1))

    def near_terms(c):
        terms = [(get((FAR, c)), 0), (get((MID, c)), 0)]
        return terms + ([(get((SUM, (c - 1) % 4)), 0)] if c != 1 else [])

    def near_step(c):
        if c in PLAN["whole"]:
            return
        grads((GRAD_NEAR, c), c, [0], [near_terms(c)])
        send((SUM, c), [(GRAD_NEAR, c)], ahead)

    def last_step():
        step(
            LAST,
            get((FEED, 0))[0],
            lambda v: last_weight_grads(where, get(TURN_H2), get(TURN_COT)[2], v, near_terms(0)),
        )
        send(LAST_OTHER, [LAST], lambda v: swap(v[1], "core", 1))

    def norm_step():
        _, _, gain_two = small_rows()
        out_all = get(OUT_ALL).reshape(8, 4, shard, inner)
        step(
            NORM,
            get((FEED, 3))[1],
            lambda v: norm_two(
                where, v, get(DH_OTHER), get(MIDDLE)[1], get(TURN_COT)[0], gain_two, out_all, count
            ),
        )
        for s in range(1, 4):
            send((SENT, s), [NORM], lambda v, s=s: shift(v[2][s], "head", -s))

    def out_step():
        step(OUT_GRAD, get(NORM)[1], lambda v: out_grads(where, mixed(), v))
        send(OUT_CORE, [OUT_GRAD], lambda v: swap(v[1], "core", 1))
        send(
            OUT_RS,
            [OUT_GRAD, OUT_CORE],
            lambda v, other: lax.psum_scatter(
                (v[0].astype(F32) + other.astype(F32)).astype(BF16).reshape(16 * shard, inner),
                ("da", "db"),
                scatter_dimension=0,
                tiled=True,
            ),
        )
        for s in range(1, 4):
            send(
                (OUTSUM, s),
                [OUT_RS, (OUTSUM, s - 1)] if s > 1 else [OUT_RS],
                lambda v, *last, s=s: back(
                    (last[0].astype(F32) + v[(4 - s) * shard : (5 - s) * shard].astype(F32)).astype(
                        BF16
                    )
                    if last
                    else v[3 * shard :]
                ),
            )

    def down_step():
        chunks = [chunk(s) for s in range(4)]
        step(
            DOWN,
            get((FEED, 0))[0],
            lambda v: down_rows(
                where, [v] + [get((FEED, s))[0] for s in range(1, 4)], chunks, width
            ),
        )
        send(DOWN_OTHER, [DOWN], lambda v: swap(v[1], "core", 1))

    def backward_step(i):
        logit, packed, _ = get((PROJECT, i))
        sent = [get(NORM)[2][0]] + [get((SENT, s)) for s in range(1, 4)]
        step(
            (BACK, i),
            packed,
            lambda v: attention_backward(
                where, seq_lengths[i : i + 1], v, logit, sent, i, get((ATTEND, i))[1:]
            ),
        )

    def dh1_step(i):
        small8, gain_one, _ = small_rows()
        dpacked, dlogit = get((BACK, i))
        normed = get((PROJECT, i))[2]
        step(
            (DH, i),
            dpacked,
            lambda v: dh1_pieces(where, v, dlogit, normed, get(ATTN), small8, gain_one),
        )
        send((RING, i, 1), [(DH, i)], lambda v: back(v[0][3]))
        for s in (2, 3):
            send(
                (RING, i, s),
                [(RING, i, s - 1), (DH, i)],
                lambda v, d, s=s: back(
                    (v.astype(F32) + d[0][4 - s].astype(F32)).astype(BF16)
                ),
            )

    def attn_step():
        step(
            ATTN_GRAD,
            get((BACK, 0))[0],
            lambda v: attn_grads(
                where,
                [get((PROJECT, i))[2] for i in range(count)],
                [v] + [get((BACK, i))[0] for i in range(1, count)],
                [get((BACK, i))[1] for i in range(count)],
                [get((DH, i))[1] for i in range(count)],
                get(NORM)[3],
                heads,
            ),
        )
        send(ATTN_CORE, [ATTN_GRAD], lambda v: swap(v[1], "core", 1))
        send(
            ATTN_RS,
            [ATTN_GRAD, ATTN_CORE],
            lambda v, other: lax.psum_scatter(
                (v[0].astype(F32) + other.astype(F32)).astype(BF16),
                ("da", "db"),
                scatter_dimension=0,
                tiled=True,
            ).astype(F32),
        )
        send((GAIN, 0), [ATTN_RS], lambda v: v[:, columns + heads : columns + heads + 2].T)
        send((GAIN, 1), [(GAIN, 0)], lambda v: v + swap(v, "head", 1))
        send((GAIN, 2), [(GAIN, 1)], lambda v: v + swap(v, "head", 2))

    def input_step(i):
        _, gain_one, _ = small_rows()
        total = get((INPUT, 0)) if i else None
        step(
            (INPUT, i),
            get(NORM)[0],
            lambda v: input_grad_rows(
                where, flat_low, get((DH, i))[0], get((RING, i, 3)), v, gain_one, i, total
            ),
        )

    def block_step():
        step(
            BLOCK_OUT,
            get(MIDDLE)[1],
            lambda v: block_out_rows(where, v, get(DOWN)[0], get(DOWN_OTHER)),
        )

    def finish_step():
        step(FINISH, get(LAST)[0], lambda v: finish_grads(where, v, get(LAST_OTHER)))

    steps = {TURN_COT: turn_cot, MIDDLE: middle_step, TURN_H2: turn_h2, NORM: norm_step, OUT_GRAD: out_step}
    steps |= {DOWN: down_step, ATTN_GRAD: attn_step, BLOCK_OUT: block_step, LAST: last_step}
    steps[FINISH] = finish_step
    for i in range(2):
        steps[(PROJECT, i)] = functools.partial(project_step, i)
        steps[(ATTEND, i)] = functools.partial(forward_step, i)
        steps[(BACK, i)] = functools.partial(backward_step, i)
        steps[(DH, i)] = functools.partial(dh1_step, i)
        steps[(INPUT, i)] = functools.partial(input_step, i)
    for c in range(4):
        steps[(FEED, c)] = functools.partial(feed_step, c)
        steps[(GRAD_FAR, c)] = functools.partial(far_step, c)
        steps[(GRAD_MIDDLE, c)] = functools.partial(middle_grads, c)
        if c:
            steps[(GRAD_NEAR, c)] = functools.partial(near_step, c)
    for name in PLAN["order"]:
        steps[name]()

    attn_total = get(ATTN_RS)
    beta_grad = attn_total[:, columns : columns + heads]
    attn_total = attn_total[:, :columns].reshape(shard, heads, 4, HEAD_DIM)
    gate_grad, up_grad, down_grad = get(FINISH)
    gains = get((GAIN, 2))
    shape = (micro, slots, part, width)
    return (
        get(BLOCK_OUT).reshape(shape),
        get((INPUT, 1)).reshape(shape),
        attn_total[:, :, 0].reshape(shard, inner),
        attn_total[:, :, 1].reshape(shard, inner),
        attn_total[:, :, 2].reshape(shard, inner),
        attn_total[:, :, 3].reshape(shard, inner),
        beta_grad,
        (get(OUT_RS)[:shard].astype(F32) + get((OUTSUM, 3)).astype(F32)).T,
        gate_grad,
        up_grad,
        down_grad.T,
        gains[0],
        gains[1],
    )


def solution(mesh):
    dp_size = mesh.shape["dp"]
    fine = Mesh(
        mesh.devices.reshape(dp_size // 4, 2, 2, mesh.shape["head"]), ("da", "db", "core", "head")
    )
    dp = ("da", "db", "core")
    rows = P(None, dp, "head", None)
    wide = P(dp, "head")
    tall = P("head", dp)
    in_specs = (
        rows, P(None, dp), rows, wide, wide, wide, wide, wide, tall, wide, wide, tall, P(dp), P(dp)
    )
    out_specs = (rows, rows, wide, wide, wide, wide, wide, tall, wide, wide, tall, P(dp), P(dp))
    special = dp_size == 8 and mesh.shape["head"] == 4
    return jax.shard_map(
        body if special else general_body,
        mesh=fine,
        in_specs=in_specs,
        out_specs=out_specs,
        check_vma=False,
    )
```

time: 4780 us -> 769 us (0.16)
  matrix products: 1800 us -> 0 us
  local copies, waits for them, and re-layouts: 894 us -> 49.1 us
  waiting for transfers between devices: 1020 us -> 253 us
  other arithmetic: 732 us -> 22.3 us
  Pallas kernels: 0 us -> 343 us
  loops' own time: 197 us -> 0 us
  starting transfers between devices: 4.16 us -> 81.5 us
  blocking collectives: 68.3 us -> 0 us
    dot_general x680 -> x0, matrix products: 1800 us -> none  [the longest x626 1540 us: einsum_high(): jnp.einsum(formula, left_side, right_side, precision=lax.Precision.HIGHEST)]
    reduce_scatter x24 -> x5, waiting for transfers between devices: 656 us -> 0.04 us  [the longest x1 0.02 us: out_step(): lax.psum_scatter((v[0].astype(F32) + other.astype(F32)).astype(BF16).resh...]
    another operation x356 -> x1, other arithmetic: 516 us -> 0.71 us  [body(): jnp.stack([w.reshape(shard, heads, HEAD_DIM) for w in (q_weight, k_weight...]
    all_gather x16 -> x5, waiting for transfers between devices: 359 us -> 0.04 us  [the longest x1 0.02 us: body(): send(ATTN, [ATTN_ROWS], lambda v: lax.all_gather(v, dp, axis=0, tiled=True))]
    pallas_call x0 -> x29, Pallas kernels: none -> 343 us  [the longest x4 63.8 us: feed_forward_part(): pl.pallas_call(functools.partial(feed_kernel, columns // 3, first, last),...]
    ppermute x0 -> x48, waiting for transfers between devices: none -> 253 us  [the longest x33 242 us: shift(): lax.ppermute(values, axis, [(i, (i + step) % size) for i in range(size)])]
    scatter x192 -> x0, local copies, waits for them, and re-layouts: 219 us -> none  [the longest x96 156 us: advance(): across = lax.dynamic_update_slice_in_dim(across, block_local, start_row, 1)]
    another operation x6 -> x0, loops' own time: 197 us -> none  [householder_attention(): lax.scan(jax.checkpoint(advance), initial, (moved_queries, moved_keys, up...]
  transfers between devices with their start and end apart: 42 -> 58, of which waited for: 24 -> 20; matrix products, arithmetic and copies ran while one was open for 70% -> 6% of each run, Pallas kernels for 0% -> 45%
where the time goes in v1:
time: 769 us; the launch traced here: 764 us
  Pallas kernels  343 us (45%)
  waiting for transfers between devices  253 us (33%)
  starting transfers between devices  81.5 us (11%)
  local copies, waits for them, and re-layouts  49.1 us (6%)
  other arithmetic  22.3 us (3%)
  between operations  15.1 us (2%)
    ppermute x33, waiting for transfers between devices, shift(): lax.ppermute(values, axis, [(i, (i + step) % size) for i in range(size)])  242 us
    ppermute x33, starting transfers between devices, shift(): lax.ppermute(values, axis, [(i, (i + step) % size) for i in range(size)])  73.3 us
    pallas_call x4, Pallas kernels, feed_forward_part(): pl.pallas_call(functools.partial(feed_kernel, columns // 3, first, last),...  63.8 us
    pallas_call x2, Pallas kernels, attention_backward(): pl.pallas_call(functools.partial(backward_kernel, len(grad_out)), grid=(h...  43.5 us
    pallas_call x2, Pallas kernels, attention_forward(): pl.pallas_call(forward_kernel, grid=(heads,), in_specs=[pl.BlockSpec(memo...  41.8 us
    pallas_call x3, Pallas kernels, whole_weight_grads(): pl.pallas_call(whole_grad_kernel, grid_spec=pltpu.PrefetchScalarGridSpec(...  35.7 us
    pallas_call x2, Pallas kernels, project(): pl.pallas_call(project_kernel, grid_spec=pltpu.PrefetchScalarGridSpec(num...  24.8 us
    pallas_call x2, Pallas kernels, dh1_pieces(): pl.pallas_call(dh1_kernel, grid_spec=pltpu.PrefetchScalarGridSpec(num_sca...  23.4 us
  transfers between devices with their start and end apart: 58, of which 20 were waited for; matrix products, arithmetic and copies ran while one was open for 6% of the time, Pallas kernels for 45%

profile of v1, /device:TPU:0, one launch (start us, length us, event | category | flops | bytes accessed | tf_op | source)
XLA Modules:
  0.0 763.6 jit_solution(15923956091884200381)
XLA Ops:
  17.9 3.1 collective-permute-start
  22.3 18.3 %collective-permute-done.p1 = bf16[256,1536]{1,0:T(8,128)(2,1)} collective-permute-done((bf16[256,1536]{1,0:T(8,128)(2,1)S(1)}, bf16[256,1536]{1,0:T(8,128)(2,1)}, u32[]{:S(2)}, u32[]{:S(2)}) %collective-permute-start) | collective-permute-done | bytes 786464 | tf_op jit(solution)/shard_map/ppermute | solution.py:1303
  41.9 21.3 %collective-permute-done.2.p2 = bf16[256,1536]{1,0:T(8,128)(2,1)} collective-permute-done((bf16[256,1536]{1,0:T(8,128)(2,1)}, bf16[256,1536]{1,0:T(8,128)(2,1)}, u32[]{:S(2)}, u32[]{:S(2)}) %collective-permute-start.2) | collective-permute-done | bytes 786464 | tf_op jit(solution)/shard_map/ppermute | solution.py:1303
  64.6 15.4 %collective-permute-done.5.p1 = bf16[256,1536]{1,0:T(8,128)(2,1)S(1)} collective-permute-done((bf16[256,1536]{1,0:T(8,128)(2,1)S(1)}, bf16[256,1536]{1,0:T(8,128)(2,1)S(1)}, u32[]{:S(2)}, u32[]{:S(2)}) %collective-permute-start.5) | collective-permute-done | bytes 786464 | tf_op jit(solution)/shard_map/ppermute | solution.py:1303
  82.7 14.3 %collective-permute-done.3.p3 = bf16[256,1536]{1,0:T(8,128)(2,1)} collective-permute-done((bf16[256,1536]{1,0:T(8,128)(2,1)}, bf16[256,1536]{1,0:T(8,128)(2,1)}, u32[]{:S(2)}, u32[]{:S(2)}) %collective-permute-start.3) | collective-permute-done | bytes 786464 | tf_op jit(solution)/shard_map/ppermute | solution.py:1303
  97.0 12.4 %project_rows.2 = (bf16[1024,1536]{1,0:T(8,128)(2,1)}, bf16[1024,1536]{1,0:T(8,128)(2,1)}, f32[8,1024]{1,0:T(8,128)}) custom-call(s32[17]{0:T(128)} %stack.71.where_ref, bf16[256,1536]{1,0:T(8,128)(2,1)} %copy-done.8, bf16[256,1536]{1,0:T(8,128)(2,1)} %collective-permute-done.p1, bf16[256,1536]{1,0:T(8,128)(2,1)} %collective-permute-done.2.p2, ...), custom_call_target="tpu_custom_call" | custom-call | flops 22499999744 | bytes 1 | tf_op jit(solution)/shard_map/project_rows/pallas_call | solution.py:558
  109.3 20.8 %attention_forward.2 = (bf16[4,256,384]{2,1,0:T(8,128)(2,1)}, bf16[1024,384]{1,0:T(8,128)(2,1)}, bf16[1024,384]{1,0:T(8,128)(2,1)}, bf16[1024,384]{1,0:T(8,128)(...) custom-call(s32[17]{0:T(128)} %stack.71.where_ref, ...), custom_call_target="tpu_custom_call" | custom-call | flops 52500000768 | bytes 1 | tf_op jit(solution)/shard_map/attention_forward/pallas_call | solution.py:450
  130.3 3.8 collective-permute-start.16
  134.9 5.9 turn_rows.2
  140.8 11.8 %collective-permute-done.7.p3 = bf16[256,1536]{1,0:T(8,128)(2,1)S(1)} collective-permute-done((bf16[256,1536]{1,0:T(8,128)(2,1)S(1)}, bf16[256,1536]{1,0:T(8,128)(2,1)S(1)}, u32[]{:S(2)}, u32[]{:S(2)}) %collective-permute-start.7) | collective-permute-done | bytes 786464 | tf_op jit(solution)/shard_map/ppermute | solution.py:1303
  153.4 12.4 %project_rows.3 = (bf16[1024,1536]{1,0:T(8,128)(2,1)}, bf16[1024,1536]{1,0:T(8,128)(2,1)}, f32[8,1024]{1,0:T(8,128)}) custom-call(s32[17]{0:T(128)} %stack.71.where_ref, bf16[256,1536]{1,0:T(8,128)(2,1)} %copy-done.7, bf16[256,1536]{1,0:T(8,128)(2,1)} %copy-done.18, bf16[256,1536]{1,0:T(8,128)(2,1)} %copy-done.20, bf16[256,1536]{1,0:T(8,128)(2,1)} %copy-done.21, ...), custom_call_target="tpu_custom_call" | custom-call | flops 22499999744 | bytes 1 | tf_op jit(solution)/shard_map/project_rows/pallas_call | solution.py:558
  167.3 21.0 %attention_forward.3 = (bf16[4,256,384]{2,1,0:T(8,128)(2,1)}, bf16[1024,384]{1,0:T(8,128)(2,1)}, bf16[1024,384]{1,0:T(8,128)(2,1)}, bf16[1024,384]{1,0:T(8,128)(...) custom-call(s32[17]{0:T(128)} %stack.71.where_ref, ...), custom_call_target="tpu_custom_call" | custom-call | flops 52500000768 | bytes 1 | tf_op jit(solution)/shard_map/attention_forward/pallas_call | solution.py:450
  188.3 3.7 collective-permute-done.18
  201.5 7.9 %collective-permute-start.11 = (bf16[256,384]{1,0:T(8,128)(2,1)S(1)}, bf16[256,384]{1,0:T(8,128)(2,1)S(1)}, u32[]{:S(2)}, u32[]{:S(2)}) collective-permute-start(bf16[256,384]{1,0:T(8,128)(2,1)S(1)} %get-tuple-element.280), channel_id=1, source_target_pairs={{0,1},{1,2},{2,3},{3,0},{4,5},{5,6},{6,7},{7,4},{8,9},{9,10},{10,1... | collective-permute-start | bytes 589832 | tf_op jit(solution)/shard_map/ppermute | solution.py:1303
  209.4 20.6 %collective-permute-done.9.refs_2_ = bf16[256,384]{1,0:T(8,128)(2,1)S(1)} collective-permute-done((bf16[256,384]{1,0:T(8,128)(2,1)S(1)}, bf16[256,384]{1,0:T(8,128)(2,1)S(1)}, u32[]{:S(2)}, u32[]{:S(2)}) %collective-permute-start.9) | collective-permute-done | bytes 196640 | tf_op jit(solution)/shard_map/ppermute | solution.py:1303
  230.6 18.3 %collective-permute-done.12.refs_6_ = bf16[256,384]{1,0:T(8,128)(2,1)S(1)} collective-permute-done((bf16[256,384]{1,0:T(8,128)(2,1)S(1)}, bf16[256,384]{1,0:T(8,128)(2,1)S(1)}, u32[]{:S(2)}, u32[]{:S(2)}) %collective-permute-start.12) | collective-permute-done | bytes 196640 | tf_op jit(solution)/shard_map/ppermute | solution.py:1303
  249.7 10.3 %middle_rows.1 = (f32[512,1536]{1,0:T(8,128)}, bf16[512,1536]{1,0:T(8,128)(2,1)}) custom-call(s32[17]{0:T(128)} %stack.71.where_ref, bf16[256,384]{1,0:T(8,128)(2,1)} %get-tuple-element.127.refs_0_, bf16[256,384]{1,0:T(8,128)(2,1)} %copy-done.25, bf16[256,384]{1,0:T(8,128)(2,1)} %copy-done.24, bf16[256,384]{1,0:T(8,128)(2,1)} %copy-done.23, ...), custom_call_target="tpu_custom_call" | custom-call | flops 12499999744 | bytes 1 | tf_op jit(solution)/shard_map/middle_rows/pallas_call | solution.py:663
  263.6 26.7 %collective-permute-done.23 = bf16[384,1536]{1,0:T(8,128)(2,1)S(1)} collective-permute-done((bf16[384,1536]{1,0:T(8,128)(2,1)}, bf16[384,1536]{1,0:T(8,128)(2,1)S(1)}, u32[]{:S(2)}, u32[]{:S(2)}) %collective-permute-start.23) | collective-permute-done | bytes 1179680 | tf_op jit(solution)/shard_map/ppermute | solution.py:1303
  292.6 14.6 %feed_forward.4 = (bf16[1024,1536]{1,0:T(8,128)(2,1)}, f32[1024,1536]{1,0:T(8,128)}) custom-call(s32[17]{0:T(128)} %stack.71.where_ref, bf16[512,1536]{1,0:T(8,128)(2,1)} %get-tuple-element.155.refs_0_.own_ref, bf16[512,1536]{1,0:T(8,128)(2,1)} %copy-done.15, bf16[512,1536]{1,0:T(8,128)(2,1)} %get-tuple-element.112.refs_2_.cot_ref, ...), custom_call_target="tpu_custom_call" | custom-call | flops 37499998208 | bytes 1 | tf_op jit(solution)/shard_map/feed_forward/pallas_call | solution.py:778
  307.3 5.3 turn_rows.3.h_ref.refs_0_
  312.6 15.4 %feed_forward.5 = (bf16[1024,1536]{1,0:T(8,128)(2,1)}, f32[1024,1536]{1,0:T(8,128)}) custom-call(s32[17]{0:T(128)} %stack.71.where_ref, bf16[512,1536]{1,0:T(8,128)(2,1)} %get-tuple-element.155.refs_0_.own_ref, bf16[512,1536]{1,0:T(8,128)(2,1)} %copy-done.15, bf16[512,1536]{1,0:T(8,128)(2,1)} %get-tuple-element.112.refs_2_.cot_ref, ...), custom_call_target="tpu_custom_call", output_to_operand_aliasing={{1}: (6, {})} | custom-call | flops 37499998208 | bytes 1 | tf_op jit(solution)/shard_map/feed_forward/pallas_call | solution.py:778
  328.0 12.4 %whole_grads.3 = bf16[1536,1536]{1,0:T(8,128)(2,1)} custom-call(s32[17]{0:T(128)} %stack.71.where_ref, bf16[1536,1024]{1,0:T(8,128)(2,1)} %turn_rows.3.h_ref.refs_0_, bf16[1536,1024]{1,0:T(8,128)(2,1)} %get-tuple-element.136.c_ref.refs_1_, bf16[1024,1536]{1,0:T(8,128)(2,1)} %get-tuple-element.149.act.refs_1_), custom_call_target="tpu_custom_call" | custom-call | flops 24999999488 | bytes 1 | tf_op jit(solution)/shard_map/whole_grads/pallas_call | solution.py:879
  340.7 15.4 %feed_forward.6 = (bf16[1024,1536]{1,0:T(8,128)(2,1)}, f32[1024,1536]{1,0:T(8,128)}) custom-call(s32[17]{0:T(128)} %stack.71.where_ref, bf16[512,1536]{1,0:T(8,128)(2,1)} %get-tuple-element.155.refs_0_.own_ref, bf16[512,1536]{1,0:T(8,128)(2,1)} %copy-done.15, bf16[512,1536]{1,0:T(8,128)(2,1)} %get-tuple-element.112.refs_2_.cot_ref, ...), custom_call_target="tpu_custom_call", output_to_operand_aliasing={{1}: (9, {})} | custom-call | flops 37499998208 | bytes 1 | tf_op jit(solution)/shard_map/feed_forward/pallas_call | solution.py:778
  356.1 11.7 %whole_grads.4 = bf16[1536,1536]{1,0:T(8,128)(2,1)} custom-call(s32[17]{0:T(128)} %stack.71.where_ref, bf16[1536,1024]{1,0:T(8,128)(2,1)} %turn_rows.3.h_ref.refs_0_, bf16[1536,1024]{1,0:T(8,128)(2,1)} %get-tuple-element.136.c_ref.refs_1_, bf16[1024,1536]{1,0:T(8,128)(2,1)} %get-tuple-element.154.act.refs_2_), custom_call_target="tpu_custom_call" | custom-call | flops 24999999488 | bytes 1 | tf_op jit(solution)/shard_map/whole_grads/pallas_call | solution.py:879
  367.8 18.3 %feed_forward.7 = (bf16[1024,1536]{1,0:T(8,128)(2,1)}, f32[512,1536]{1,0:T(8,128)}, bf16[512,1536]{1,0:T(8,128)(2,1)}) custom-call(s32[17]{0:T(128)} %stack.71.where_ref, bf16[512,1536]{1,0:T(8,128)(2,1)} %get-tuple-element.155.refs_0_.own_ref, bf16[512,1536]{1,0:T(8,128)(2,1)} %copy-done.15, bf16[512,1536]{1,0:T(8,128)(2,1)} %get-tuple-element.112.refs_2_.cot_ref, ...), custom_call_target="tpu_custom_call" | custom-call | flops 37499998208 | bytes 1 | tf_op jit(solution)/shard_map/feed_forward/pallas_call | solution.py:778
  386.3 3.5 collective-permute-done.24.recv_ref
  390.9 13.2 %norm_two.1 = (f32[512,1536]{1,0:T(8,128)}, bf16[512,1536]{1,0:T(8,128)(2,1)}, bf16[4,2,256,384]{3,2,1,0:T(8,128)(2,1)}, f32[1,1536]{1,0:T(1,128)}) custom-call(s32[17]{0:T(128)} %stack.71.where_ref, f32[512,1536]{1,0:T(8,128)} %get-tuple-element.161.own_ref, bf16[512,1536]{1,0:T(8,128)(2,1)} %copy-done.16, f32[512,1536]{1,0:T(8,128)} %get-tuple-element.188.mid_ref, ...), custom_call_target="tpu_custom_call" | custom-call | flops 15000000512 | bytes 1 | tf_op jit(solution)/shard_map/norm_two/pallas_call | solution.py:1048
  404.1 2.8 slice_bitcast_fusion.7
  407.0 3.8 collective-permute-start.25
  410.8 11.7 %whole_grads.5 = bf16[1536,1536]{1,0:T(8,128)(2,1)} custom-call(s32[17]{0:T(128)} %stack.71.where_ref, bf16[1536,1024]{1,0:T(8,128)(2,1)} %turn_rows.3.h_ref.refs_0_, bf16[1536,1024]{1,0:T(8,128)(2,1)} %get-tuple-element.136.c_ref.refs_1_, bf16[1024,1536]{1,0:T(8,128)(2,1)} %get-tuple-element.165.act.refs_3_), custom_call_target="tpu_custom_call" | custom-call | flops 24999999488 | bytes 1 | tf_op jit(solution)/shard_map/whole_grads/pallas_call | solution.py:879
  422.5 7.3 out_grads.1
  429.8 3.9 slice_bitcast_fusion.2
  434.2 2.9 collective-permute-done.26.refs_2_
  437.1 21.8 %attention_backward.2 = (bf16[1024,1536]{1,0:T(8,128)(2,1)}, f32[8,1024]{1,0:T(8,128)}) custom-call(s32[17]{0:T(128)} %stack.71.where_ref, s32[1]{0:T(128)} %bitcast.16.length_ref, bf16[1024,1536]{1,0:T(8,128)(2,1)} %get-tuple-element.167.x_ref, f32[8,1024]{1,0:T(8,128)} %get-tuple-element.108.logit_ref, bf16[2,256,384]{2,1,0:T(8,128)(2,1)} %get-tuple-element.273.refs_0_, ...), custom_call_target="tpu_custom_call" | custom-call | flops 54999998464 | bytes 1 | tf_op jit(solution)/shard_map/attention_backward/pallas_call | solution.py:487
  458.9 5.5 collective-permute-done.28
  464.4 12.2 %dh1_rows.2 = (bf16[4,256,1536]{2,1,0:T(8,128)(2,1)}, f32[1,1536]{1,0:T(1,128)}) custom-call(s32[17]{0:T(128)} %stack.71.where_ref, bf16[1024,1536]{1,0:T(8,128)(2,1)} %get-tuple-element.182.d_ref.refs_2_, f32[8,1024]{1,0:T(8,128)} %get-tuple-element.171.l_ref.refs_4_, bf16[1024,1536]{1,0:T(8,128)(2,1)} %get-tuple-element.172.h_ref.refs_0_, ...), custom_call_target="tpu_custom_call" | custom-call | flops 20000000 | bytes 1 | tf_op jit(solution)/shard_map/dh1_rows/pallas_call | solution.py:1101
  478.6 3.0 collective-permute-start.29
  481.5 14.8 %down_rows.1 = (f32[512,1536]{1,0:T(8,128)}, bf16[512,1536]{1,0:T(8,128)(2,1)}) custom-call(s32[17]{0:T(128)} %stack.71.where_ref, bf16[1024,1536]{1,0:T(8,128)(2,1)} %get-tuple-element.190.refs_0_.refs_2_.act, bf16[1024,1536]{1,0:T(8,128)(2,1)} %get-tuple-element.149.act.refs_1_, bf16[1024,1536]{1,0:T(8,128)(2,1)} %get-tuple-element.154.act.refs_2_, ...), custom_call_target="tpu_custom_call" | custom-call | flops 24999999488 | bytes 1 | tf_op jit(solution)/shard_map/down_rows/pallas_call | solution.py:841
  496.3 27.5 %collective-permute-done.29 = bf16[256,1536]{1,0:T(8,128)(2,1)} collective-permute-done((bf16[256,1536]{1,0:T(8,128)(2,1)}, bf16[256,1536]{1,0:T(8,128)(2,1)}, u32[]{:S(2)}, u32[]{:S(2)}) %collective-permute-start.29) | collective-permute-done | bytes 786464 | tf_op jit(solution)/shard_map/ppermute | solution.py:1303
  523.9 6.7 weight_grads.2
  539.1 16.5 %collective-permute-done.30 = bf16[256,1536]{1,0:T(8,128)(2,1)S(1)} collective-permute-done((bf16[256,1536]{1,0:T(8,128)(2,1)S(1)}, bf16[256,1536]{1,0:T(8,128)(2,1)S(1)}, u32[]{:S(2)}, u32[]{:S(2)}) %collective-permute-start.30) | collective-permute-done | bytes 786464 | tf_op jit(solution)/shard_map/ppermute | solution.py:1303
  558.5 21.7 %attention_backward.3 = (bf16[1024,1536]{1,0:T(8,128)(2,1)}, f32[8,1024]{1,0:T(8,128)}) custom-call(s32[17]{0:T(128)} %stack.71.where_ref, s32[1]{0:T(128)} %bitcast.23.length_ref, bf16[1024,1536]{1,0:T(8,128)(2,1)} %get-tuple-element.177.x_ref, f32[8,1024]{1,0:T(8,128)} %get-tuple-element.124.logit_ref, bf16[2,256,384]{2,1,0:T(8,128)(2,1)} %get-tuple-element.273.refs_0_, ...), custom_call_target="tpu_custom_call" | custom-call | flops 54999998464 | bytes 1 | tf_op jit(solution)/shard_map/attention_backward/pallas_call | solution.py:487
  580.2 11.3 %dh1_rows.3 = (bf16[4,256,1536]{2,1,0:T(8,128)(2,1)}, f32[1,1536]{1,0:T(1,128)}) custom-call(s32[17]{0:T(128)} %stack.71.where_ref, bf16[1024,1536]{1,0:T(8,128)(2,1)} %get-tuple-element.179.d_ref.refs_3_, f32[8,1024]{1,0:T(8,128)} %get-tuple-element.180.l_ref.refs_5_, bf16[1024,1536]{1,0:T(8,128)(2,1)} %get-tuple-element.128.h_ref.refs_1_, ...), custom_call_target="tpu_custom_call" | custom-call | flops 20000000 | bytes 1 | tf_op jit(solution)/shard_map/dh1_rows/pallas_call | solution.py:1101
  592.6 23.1 %collective-permute-start.32 = (bf16[256,1536]{1,0:T(8,128)(2,1)S(1)}, bf16[256,1536]{1,0:T(8,128)(2,1)}, u32[]{:S(2)}, u32[]{:S(2)}) collective-permute-start(bf16[256,1536]{1,0:T(8,128)(2,1)S(1)} %slice_bitcast_fusion.3), channel_id=1, source_target_pairs={{0,3},{1,0},{2,1},{3,2},{4,7},{5,4},{6,5},{7,6},{8,11},{9,8},{10,9... | collective-permute-start | bytes 2359304 | tf_op jit(solution)/shard_map/ppermute | solution.py:1303
  615.7 17.8 %attn_grads.1 = bf16[2,768,1544]{2,1,0:T(8,128)(2,1)} custom-call(s32[17]{0:T(128)} %stack.71.where_ref, bf16[1024,1536]{1,0:T(8,128)(2,1)} %get-tuple-element.172.h_ref.refs_0_, bf16[1024,1536]{1,0:T(8,128)(2,1)} %get-tuple-element.128.h_ref.refs_1_, bf16[1024,1536]{1,0:T(8,128)(2,1)} %get-tuple-element.182.d_ref.refs_2_, ...), custom_call_target="tpu_custom_call" | custom-call | flops 35000000512 | bytes 1 | tf_op jit(solution)/shard_map/attn_grads/pallas_call | solution.py:1172
  635.4 2.7 copy.84
  639.7 2.7 collective-permute-start.33
  642.7 17.2 %collective-permute-done.33 = bf16[256,1536]{1,0:T(8,128)(2,1)S(1)} collective-permute-done((bf16[256,1536]{1,0:T(8,128)(2,1)S(1)}, bf16[256,1536]{1,0:T(8,128)(2,1)S(1)}, u32[]{:S(2)}, u32[]{:S(2)}) %collective-permute-start.33) | collective-permute-done | bytes 786464 | tf_op jit(solution)/shard_map/ppermute | solution.py:1303
  661.2 4.5 collective-permute-start.37
  665.7 5.2 weight_grads.3
  671.0 3.3 copy.85
  674.3 3.8 fusion
  679.1 4.3 input_grad.2.refs_0_
  685.6 4.3 collective-permute-start.43
  694.2 4.3 collective-permute-start.44
  698.6 5.7 block_out.1
  704.2 17.1 %collective-permute-done.44 = bf16[192,384]{1,0:T(8,128)(2,1)S(1)} collective-permute-done((bf16[192,384]{1,0:T(8,128)(2,1)S(1)}, bf16[192,384]{1,0:T(8,128)(2,1)S(1)}, u32[]{:S(2)}, u32[]{:S(2)}) %collective-permute-start.44) | collective-permute-done | bytes 147488 | tf_op jit(solution)/shard_map/ppermute | solution.py:1303
  723.1 6.3 last_weight_grad.1
  729.5 4.1 input_grad.3
  734.4 2.9 finish_grads.1
  739.0 3.6 slice_reduce_fusion
  744.0 4.0 collective-permute-done.46
  748.1 2.8 collective-permute-start.47
  752.5 3.3 collective-permute-done.47
  (212 shorter events, 74.2 us)
Async XLA Ops:
  7.2 73.0 %all-gather.6.cloned.1.call-start = ((), (), s32[]{:S(2)}) async-start(), calls=%async_computation.5 | async-start | bytes 5750784 | tf_op jit(solution)/shard_map/all_gather | solution.py:1657
  15.9 151.4 %all-gather.8.cloned.1.call-start = ((), (), s32[]{:S(2)}) async-start(), calls=%async_computation.6 | async-start | bytes 5898240 | tf_op jit(solution)/shard_map/all_gather | solution.py:1674
  16.5 4.5 collective-permute-start.1
  17.9 46.6 %copy-start.7 = (bf16[256,1536]{1,0:T(8,128)(2,1)}, bf16[256,1536]{1,0:T(8,128)(2,1)S(1)}, u32[]{:S(2)}) copy-start(bf16[256,1536]{1,0:T(8,128)(2,1)S(1)} %get-tuple-element.113.p0) | copy-start | bytes 2359300
  17.9 46.6 %copy-start.8 = (bf16[256,1536]{1,0:T(8,128)(2,1)}, bf16[256,1536]{1,0:T(8,128)(2,1)S(1)}, u32[]{:S(2)}) copy-start(bf16[256,1536]{1,0:T(8,128)(2,1)S(1)} %get-tuple-element.275.p0) | copy-start | bytes 2359300
  17.9 46.0 %copy-start.14 = (s32[2,1]{0,1:T(1,128)S(1)}, s32[2,1]{0,1:T(1,128)}, u32[]{:S(2)}) copy-start(s32[2,1]{0,1:T(1,128)} %param.15) | copy-start | bytes 28
  17.9 22.7 %collective-permute-start = (bf16[256,1536]{1,0:T(8,128)(2,1)S(1)}, bf16[256,1536]{1,0:T(8,128)(2,1)}, u32[]{:S(2)}, u32[]{:S(2)}) collective-permute-start(bf16[256,1536]{1,0:T(8,128)(2,1)S(1)} %get-tuple-element.275.p0), channel_id=1, source_target_pairs={{0,1},{1,2},{2,3},{3,0},{4,5},{5,6},{6,7},{7,4},{8,9},{9,10},{10,1... | collective-permute-start | bytes 2359304 | tf_op jit(solution)/shard_map/ppermute | solution.py:1303
  40.6 22.6 %collective-permute-start.2 = (bf16[256,1536]{1,0:T(8,128)(2,1)}, bf16[256,1536]{1,0:T(8,128)(2,1)}, u32[]{:S(2)}, u32[]{:S(2)}) collective-permute-start(bf16[256,1536]{1,0:T(8,128)(2,1)} %collective-permute-done.p1), channel_id=1, source_target_pairs={{0,1},{1,2},{2,3},{3,0},{4,5},{5,6},{6,7},{7,4},{8,9},{9,10},{10,1... | collective-permute-start | bytes 2359304 | tf_op jit(solution)/shard_map/ppermute | solution.py:1303
  40.6 39.4 %collective-permute-start.5 = (bf16[256,1536]{1,0:T(8,128)(2,1)S(1)}, bf16[256,1536]{1,0:T(8,128)(2,1)S(1)}, u32[]{:S(2)}, u32[]{:S(2)}) collective-permute-start(bf16[256,1536]{1,0:T(8,128)(2,1)S(1)} %get-tuple-element.113.p0), channel_id=1, source_target_pairs={{0,1},{1,2},{2,3},{3,0},{4,5},{5,6},{6,7},{7,4},{8,9},{9,10},{10,1... | collective-permute-start | bytes 2359304 | tf_op jit(solution)/shard_map/ppermute | solution.py:1303
  63.2 33.7 %collective-permute-start.3 = (bf16[256,1536]{1,0:T(8,128)(2,1)}, bf16[256,1536]{1,0:T(8,128)(2,1)}, u32[]{:S(2)}, u32[]{:S(2)}) collective-permute-start(bf16[256,1536]{1,0:T(8,128)(2,1)} %collective-permute-done.2.p2), channel_id=1, source_target_pairs={{0,1},{1,2},{2,3},{3,0},{4,5},{5,6},{6,7},{7,4},{8,9},{9,10},{10,1... | collective-permute-start | bytes 2359304 | tf_op jit(solution)/shard_map/ppermute | solution.py:1303
  63.3 71.6 %collective-permute-start.4 = (bf16[512,1536]{1,0:T(8,128)(2,1)}, bf16[512,1536]{1,0:T(8,128)(2,1)}, u32[]{:S(2)}, u32[]{:S(2)}) collective-permute-start(bf16[512,1536]{1,0:T(8,128)(2,1)} %bitcast.140), channel_id=1, source_target_pairs={{0,4},{4,0},{1,5},{5,1},{2,6},{6,2},{3,7},{7,3},{8,12},{12,8},{9,1... | collective-permute-start | bytes 4718600 | tf_op jit(solution)/shard_map/ppermute | solution.py:1544
  64.5 184.4 %all-gather.10.cloned.1.call-start = ((), (), s32[]{:S(2)}) async-start(), calls=%async_computation.7 | async-start | bytes 5308416 | tf_op jit(solution)/shard_map/all_gather | solution.py:1681
  80.0 50.2 %collective-permute-start.6 = (bf16[256,1536]{1,0:T(8,128)(2,1)S(1)}, bf16[256,1536]{1,0:T(8,128)(2,1)S(1)}, u32[]{:S(2)}, u32[]{:S(2)}) collective-permute-start(bf16[256,1536]{1,0:T(8,128)(2,1)S(1)} %collective-permute-done.5.p1), channel_id=1, source_target_pairs={{0,1},{1,2},{2,3},{3,0},{4,5},{5,6},{6,7},{7,4},{8,9},{9,10},{10,1... | collective-permute-start | bytes 2359304 | tf_op jit(solution)/shard_map/ppermute | solution.py:1303
  130.2 22.3 %collective-permute-start.7 = (bf16[256,1536]{1,0:T(8,128)(2,1)S(1)}, bf16[256,1536]{1,0:T(8,128)(2,1)S(1)}, u32[]{:S(2)}, u32[]{:S(2)}) collective-permute-start(bf16[256,1536]{1,0:T(8,128)(2,1)S(1)} %collective-permute-done.6.p2), channel_id=1, source_target_pairs={{0,1},{1,2},{2,3},{3,0},{4,5},{5,6},{6,7},{7,4},{8,9},{9,10},{10,1... | collective-permute-start | bytes 2359304 | tf_op jit(solution)/shard_map/ppermute | solution.py:1303
  130.3 35.6 %collective-permute-start.16 = (bf16[192,384]{1,0:T(8,128)(2,1)S(1)}, bf16[192,384]{1,0:T(8,128)(2,1)S(1)}, u32[]{:S(2)}, u32[]{:S(2)}) collective-permute-start(bf16[192,384]{1,0:T(8,128)(2,1)S(1)} %bitcast.134), channel_id=1, source_target_pairs={{0,3},{1,0},{2,1},{3,2},{4,7},{5,4},{6,5},{7,6},{8,11},{9,8},{10,9... | collective-permute-start | bytes 442376 | tf_op jit(solution)/shard_map/ppermute | solution.py:1303
  134.1 31.8 %collective-permute-start.15 = (bf16[192,384]{1,0:T(8,128)(2,1)S(1)}, bf16[192,384]{1,0:T(8,128)(2,1)S(1)}, u32[]{:S(2)}, u32[]{:S(2)}) collective-permute-start(bf16[192,384]{1,0:T(8,128)(2,1)S(1)} %bitcast.135), channel_id=1, source_target_pairs={{0,2},{1,3},{2,0},{3,1},{4,6},{5,7},{6,4},{7,5},{8,10},{9,11},{10,... | collective-permute-start | bytes 442376 | tf_op jit(solution)/shard_map/ppermute | solution.py:1303
  134.1 31.8 %collective-permute-start.14 = (bf16[192,384]{1,0:T(8,128)(2,1)S(1)}, bf16[192,384]{1,0:T(8,128)(2,1)S(1)}, u32[]{:S(2)}, u32[]{:S(2)}) collective-permute-start(bf16[192,384]{1,0:T(8,128)(2,1)S(1)} %bitcast.136), channel_id=1, source_target_pairs={{0,1},{1,2},{2,3},{3,0},{4,5},{5,6},{6,7},{7,4},{8,9},{9,10},{10,1... | collective-permute-start | bytes 442376 | tf_op jit(solution)/shard_map/ppermute | solution.py:1303
  166.8 145.8 %all-gather.12.cloned.1.call-start = ((), (), s32[]{:S(2)}) async-start(), calls=%async_computation.8 | async-start | bytes 5898240 | tf_op jit(solution)/shard_map/all_gather | solution.py:1674
  167.3 24.7 %collective-permute-start.18 = (bf16[384,1536]{1,0:T(8,128)(2,1)S(1)}, bf16[384,1536]{1,0:T(8,128)(2,1)S(1)}, u32[]{:S(2)}, u32[]{:S(2)}) collective-permute-start(bf16[384,1536]{1,0:T(8,128)(2,1)S(1)} %copy-done.1), channel_id=1, source_target_pairs={{0,1},{1,2},{2,3},{3,0},{4,5},{5,6},{6,7},{7,4},{8,9},{9,10},{10,1... | collective-permute-start | bytes 3538952 | tf_op jit(solution)/shard_map/ppermute | solution.py:1303
  193.1 174.7 %all-gather.14.cloned.1.call-start = ((), (), s32[]{:S(2)}) async-start(), calls=%async_computation.9 | async-start | bytes 5898240 | tf_op jit(solution)/shard_map/all_gather | solution.py:1674
  193.9 7.6 collective-permute-start.10
  194.5 35.6 %collective-permute-start.9 = (bf16[256,384]{1,0:T(8,128)(2,1)S(1)}, bf16[256,384]{1,0:T(8,128)(2,1)S(1)}, u32[]{:S(2)}, u32[]{:S(2)}) collective-permute-start(bf16[256,384]{1,0:T(8,128)(2,1)S(1)} %get-tuple-element.283), channel_id=1, source_target_pairs={{0,2},{1,3},{2,0},{3,1},{4,6},{5,7},{6,4},{7,5},{8,10},{9,11},{10,... | collective-permute-start | bytes 589832 | tf_op jit(solution)/shard_map/ppermute | solution.py:1303
  194.5 36.1 %collective-permute-start.8 = (bf16[256,384]{1,0:T(8,128)(2,1)S(1)}, bf16[256,384]{1,0:T(8,128)(2,1)S(1)}, u32[]{:S(2)}, u32[]{:S(2)}) collective-permute-start(bf16[256,384]{1,0:T(8,128)(2,1)S(1)} %get-tuple-element.284), channel_id=1, source_target_pairs={{0,1},{1,2},{2,3},{3,0},{4,5},{5,6},{6,7},{7,4},{8,9},{9,10},{10,1... | collective-permute-start | bytes 589832 | tf_op jit(solution)/shard_map/ppermute | solution.py:1303
  197.9 32.7 %collective-permute-start.13 = (bf16[256,384]{1,0:T(8,128)(2,1)S(1)}, bf16[256,384]{1,0:T(8,128)(2,1)S(1)}, u32[]{:S(2)}, u32[]{:S(2)}) collective-permute-start(bf16[256,384]{1,0:T(8,128)(2,1)S(1)} %get-tuple-element.278), channel_id=1, source_target_pairs={{0,3},{1,0},{2,1},{3,2},{4,7},{5,4},{6,5},{7,6},{8,11},{9,8},{10,9... | collective-permute-start | bytes 589832 | tf_op jit(solution)/shard_map/ppermute | solution.py:1303
  200.3 48.6 %collective-permute-start.12 = (bf16[256,384]{1,0:T(8,128)(2,1)S(1)}, bf16[256,384]{1,0:T(8,128)(2,1)S(1)}, u32[]{:S(2)}, u32[]{:S(2)}) collective-permute-start(bf16[256,384]{1,0:T(8,128)(2,1)S(1)} %get-tuple-element.279), channel_id=1, source_target_pairs={{0,2},{1,3},{2,0},{3,1},{4,6},{5,7},{6,4},{7,5},{8,10},{9,11},{10,... | collective-permute-start | bytes 589832 | tf_op jit(solution)/shard_map/ppermute | solution.py:1303
  201.5 47.4 %copy-start.23 = (bf16[256,384]{1,0:T(8,128)(2,1)}, bf16[256,384]{1,0:T(8,128)(2,1)S(1)}, u32[]{:S(2)}) copy-start(bf16[256,384]{1,0:T(8,128)(2,1)S(1)} %collective-permute-done.10.refs_3_) | copy-start | bytes 589828
  201.5 47.4 %collective-permute-start.11 = (bf16[256,384]{1,0:T(8,128)(2,1)S(1)}, bf16[256,384]{1,0:T(8,128)(2,1)S(1)}, u32[]{:S(2)}, u32[]{:S(2)}) collective-permute-start(bf16[256,384]{1,0:T(8,128)(2,1)S(1)} %get-tuple-element.280), channel_id=1, source_target_pairs={{0,1},{1,2},{2,3},{3,0},{4,5},{5,6},{6,7},{7,4},{8,9},{9,10},{10,1... | collective-permute-start | bytes 589832 | tf_op jit(solution)/shard_map/ppermute | solution.py:1303
  230.0 29.9 %collective-permute-start.19 = (bf16[384,1536]{1,0:T(8,128)(2,1)S(1)}, bf16[384,1536]{1,0:T(8,128)(2,1)}, u32[]{:S(2)}, u32[]{:S(2)}) collective-permute-start(bf16[384,1536]{1,0:T(8,128)(2,1)S(1)} %copy-done.4), channel_id=1, source_target_pairs={{0,1},{1,2},{2,3},{3,0},{4,5},{5,6},{6,7},{7,4},{8,9},{9,10},{10,1... | collective-permute-start | bytes 3538952 | tf_op jit(solution)/shard_map/ppermute | solution.py:1303
  259.9 31.5 %collective-permute-start.17 = (bf16[512,1536]{1,0:T(8,128)(2,1)}, bf16[512,1536]{1,0:T(8,128)(2,1)S(1)}, u32[]{:S(2)}, u32[]{:S(2)}) collective-permute-start(bf16[512,1536]{1,0:T(8,128)(2,1)} %get-tuple-element.155.refs_0_.own_ref), channel_id=1, source_target_pairs={{0,4},{4,0},{1,5},{5,1},{2,6},{6,2},{3,7},{7,3},{8,12},{12,8},{9,1... | collective-permute-start | bytes 4718600 | tf_op jit(solution)/shard_map/ppermute | solution.py:1544
  259.9 30.4 %collective-permute-start.23 = (bf16[384,1536]{1,0:T(8,128)(2,1)}, bf16[384,1536]{1,0:T(8,128)(2,1)S(1)}, u32[]{:S(2)}, u32[]{:S(2)}) collective-permute-start(bf16[384,1536]{1,0:T(8,128)(2,1)} %collective-permute-done.19.refs_4_.refs_6_), channel_id=1, source_target_pairs={{0,1},{1,2},{2,3},{3,0},{4,5},{5,6},{6,7},{7,4},{8,9},{9,10},{10,1... | collective-permute-start | bytes 3538952 | tf_op jit(solution)/shard_map/ppermute | solution.py:1303
  260.0 80.7 %collective-permute-start.22 = (bf16[384,1536]{1,0:T(8,128)(2,1)}, bf16[384,1536]{1,0:T(8,128)(2,1)}, u32[]{:S(2)}, u32[]{:S(2)}) collective-permute-start(bf16[384,1536]{1,0:T(8,128)(2,1)} %collective-permute-done.19.refs_4_.refs_6_), channel_id=1, source_target_pairs={{0,24},{8,16},{16,8},{24,0},{1,25},{9,17},{17,9},{25,1},{2,26},{10... | collective-permute-start | bytes 3538952 | tf_op jit(solution)/shard_map/ppermute | solution.py:1548
  261.6 79.1 %collective-permute-start.21 = (bf16[384,1536]{1,0:T(8,128)(2,1)}, bf16[384,1536]{1,0:T(8,128)(2,1)}, u32[]{:S(2)}, u32[]{:S(2)}) collective-permute-start(bf16[384,1536]{1,0:T(8,128)(2,1)} %collective-permute-done.19.refs_4_.refs_6_), channel_id=1, source_target_pairs={{0,16},{8,24},{16,0},{24,8},{1,17},{9,25},{17,1},{25,9},{2,18},{10... | collective-permute-start | bytes 3538952 | tf_op jit(solution)/shard_map/ppermute | solution.py:1548
  262.0 78.6 %collective-permute-start.20 = (bf16[384,1536]{1,0:T(8,128)(2,1)}, bf16[384,1536]{1,0:T(8,128)(2,1)}, u32[]{:S(2)}, u32[]{:S(2)}) collective-permute-start(bf16[384,1536]{1,0:T(8,128)(2,1)} %collective-permute-done.19.refs_4_.refs_6_), channel_id=1, source_target_pairs={{0,8},{8,0},{16,24},{24,16},{1,9},{9,1},{17,25},{25,17},{2,10},{10... | collective-permute-start | bytes 3538952 | tf_op jit(solution)/shard_map/ppermute | solution.py:1548
  291.4 142.3 %reduce-scatter.6.cloned.1.call-start = ((), (), s32[]{:S(2)}) async-start(), calls=%async_computation.10 | async-start | bytes 5898240 | tf_op jit(solution)/shard_map/reduce_scatter | solution.py:1771
  340.4 194.0 %reduce-scatter.8.cloned.1.call-start = ((), (), s32[]{:S(2)}) async-start(), calls=%async_computation.11 | async-start | bytes 5898240 | tf_op jit(solution)/shard_map/reduce_scatter | solution.py:1771
  386.1 3.7 collective-permute-start.24
  386.2 291.9 %reduce-scatter.14.cloned.1.call-start = ((), (), s32[]{:S(2)}) async-start(), calls=%async_computation.14 | async-start | bytes 2949120 | tf_op jit(solution)/shard_map/reduce_scatter | solution.py:1830
  407.0 27.2 %collective-permute-start.27 = (bf16[2,256,384]{2,1,0:T(8,128)(2,1)}, bf16[2,256,384]{2,1,0:T(8,128)(2,1)}, u32[]{:S(2)}, u32[]{:S(2)}) collective-permute-start(bf16[2,256,384]{2,1,0:T(8,128)(2,1)} %get-tuple-element.270), channel_id=1, source_target_pairs={{0,1},{1,2},{2,3},{3,0},{4,5},{5,6},{6,7},{7,4},{8,9},{9,10},{10,1... | collective-permute-start | bytes 1179656 | tf_op jit(solution)/shard_map/ppermute | solution.py:1303
  407.0 30.1 %collective-permute-start.26 = (bf16[2,256,384]{2,1,0:T(8,128)(2,1)}, bf16[2,256,384]{2,1,0:T(8,128)(2,1)}, u32[]{:S(2)}, u32[]{:S(2)}) collective-permute-start(bf16[2,256,384]{2,1,0:T(8,128)(2,1)} %get-tuple-element.271), channel_id=1, source_target_pairs={{0,2},{1,3},{2,0},{3,1},{4,6},{5,7},{6,4},{7,5},{8,10},{9,11},{10,... | collective-permute-start | bytes 1179656 | tf_op jit(solution)/shard_map/ppermute | solution.py:1303
  407.0 30.1 %collective-permute-start.25 = (bf16[2,256,384]{2,1,0:T(8,128)(2,1)}, bf16[2,256,384]{2,1,0:T(8,128)(2,1)}, u32[]{:S(2)}, u32[]{:S(2)}) collective-permute-start(bf16[2,256,384]{2,1,0:T(8,128)(2,1)} %get-tuple-element.272), channel_id=1, source_target_pairs={{0,3},{1,0},{2,1},{3,2},{4,7},{5,4},{6,5},{7,6},{8,11},{9,8},{10,9... | collective-permute-start | bytes 1179656 | tf_op jit(solution)/shard_map/ppermute | solution.py:1303
  433.7 96.9 %collective-permute-start.41 = (bf16[4,4,192,384]{3,2,1,0:T(8,128)(2,1)}, bf16[4,4,192,384]{3,2,1,0:T(8,128)(2,1)S(1)}, u32[]{:S(2)}, u32[]{:S(2)}) collective-permute-start(bf16[4,4,192,384]{3,2,1,0:T(8,128)(2,1)} %slice_bitcast_fusion.2), channel_id=1, source_target_pairs={{0,4},{4,0},{1,5},{5,1},{2,6},{6,2},{3,7},{7,3},{8,12},{12,8},{9,1... | collective-permute-start | bytes 7077896 | tf_op jit(solution)/shard_map/ppermute | solution.py:1544
  433.7 30.7 %collective-permute-start.28 = (bf16[384,1536]{1,0:T(8,128)(2,1)}, bf16[384,1536]{1,0:T(8,128)(2,1)S(1)}, u32[]{:S(2)}, u32[]{:S(2)}) collective-permute-start(bf16[384,1536]{1,0:T(8,128)(2,1)} %reduce-scatter.6.cloned.1.call-done), channel_id=1, source_target_pairs={{0,1},{1,2},{2,3},{3,0},{4,5},{5,6},{6,7},{7,4},{8,9},{9,10},{10,1... | collective-permute-start | bytes 3538952 | tf_op jit(solution)/shard_map/ppermute | solution.py:1303
  464.3 66.2 %slice-start = ((s8[4718592]{0:T(1024)(128)(4,1)}), s8[4194304]{0:T(1024)(128)(4,1)S(1)}, s32[]{:S(2)}) async-start(s8[4718592]{0:T(1024)(128)(4,1)} %bitcast.120), calls=%async_computation.15 | async-start | bytes 8388608
  478.6 52.0 %slice-start.1 = ((s8[4718592]{0:T(1024)(128)(4,1)}), s8[524288]{0:T(1024)(128)(4,1)S(1)}, s32[]{:S(2)}) async-start(s8[4718592]{0:T(1024)(128)(4,1)} %bitcast.120), calls=%async_computation.16 | async-start | bytes 1048576
  478.6 45.3 %collective-permute-start.29 = (bf16[256,1536]{1,0:T(8,128)(2,1)}, bf16[256,1536]{1,0:T(8,128)(2,1)}, u32[]{:S(2)}, u32[]{:S(2)}) collective-permute-start(bf16[256,1536]{1,0:T(8,128)(2,1)} %slice_bitcast_fusion.4), channel_id=1, source_target_pairs={{0,3},{1,0},{2,1},{3,2},{4,7},{5,4},{6,5},{7,6},{8,11},{9,8},{10,9... | collective-permute-start | bytes 2359304 | tf_op jit(solution)/shard_map/ppermute | solution.py:1303
  532.7 157.3 %reduce-scatter.10.cloned.1.call-start = ((), (), s32[]{:S(2)}) async-start(), calls=%async_computation.12 | async-start | bytes 5898240 | tf_op jit(solution)/shard_map/reduce_scatter | solution.py:1771
  534.3 21.3 %collective-permute-start.30 = (bf16[256,1536]{1,0:T(8,128)(2,1)S(1)}, bf16[256,1536]{1,0:T(8,128)(2,1)S(1)}, u32[]{:S(2)}, u32[]{:S(2)}) collective-permute-start(bf16[256,1536]{1,0:T(8,128)(2,1)S(1)} %fusion.5), channel_id=1, source_target_pairs={{0,3},{1,0},{2,1},{3,2},{4,7},{5,4},{6,5},{7,6},{8,11},{9,8},{10,9... | collective-permute-start | bytes 2359304 | tf_op jit(solution)/shard_map/ppermute | solution.py:1303
  534.4 202.9 %reduce-scatter.12.cloned.1.call-start = ((), (), s32[]{:S(2)}) async-start(), calls=%async_computation.13 | async-start | bytes 3194880 | tf_op jit(solution)/shard_map/reduce_scatter | solution.py:1909
  537.1 105.6 %collective-permute-start.34 = (bf16[384,1536]{1,0:T(8,128)(2,1)}, bf16[384,1536]{1,0:T(8,128)(2,1)}, u32[]{:S(2)}, u32[]{:S(2)}) collective-permute-start(bf16[384,1536]{1,0:T(8,128)(2,1)} %add_convert_fusion.1), channel_id=1, source_target_pairs={{0,1},{1,2},{2,3},{3,0},{4,5},{5,6},{6,7},{7,4},{8,9},{9,10},{10,1... | collective-permute-start | bytes 3538952 | tf_op jit(solution)/shard_map/ppermute | solution.py:1303
  539.1 126.6 %collective-permute-start.35 = (bf16[768,1536]{1,0:T(8,128)(2,1)}, bf16[768,1536]{1,0:T(8,128)(2,1)}, u32[]{:S(2)}, u32[]{:S(2)}) collective-permute-start(bf16[768,1536]{1,0:T(8,128)(2,1)} %weight_grads.2), channel_id=1, source_target_pairs={{0,16},{16,0},{1,17},{17,1},{2,18},{18,2},{3,19},{19,3},{4,20},{20... | collective-permute-start | bytes 7077896 | tf_op jit(solution)/shard_map/ppermute | solution.py:1544
  556.9 58.8 %collective-permute-start.31 = (bf16[256,1536]{1,0:T(8,128)(2,1)S(1)}, bf16[256,1536]{1,0:T(8,128)(2,1)S(1)}, u32[]{:S(2)}, u32[]{:S(2)}) collective-permute-start(bf16[256,1536]{1,0:T(8,128)(2,1)S(1)} %fusion.4), channel_id=1, source_target_pairs={{0,3},{1,0},{2,1},{3,2},{4,7},{5,4},{6,5},{7,6},{8,11},{9,8},{10,9... | collective-permute-start | bytes 2359304 | tf_op jit(solution)/shard_map/ppermute | solution.py:1303
  592.6 45.5 %collective-permute-start.32 = (bf16[256,1536]{1,0:T(8,128)(2,1)S(1)}, bf16[256,1536]{1,0:T(8,128)(2,1)}, u32[]{:S(2)}, u32[]{:S(2)}) collective-permute-start(bf16[256,1536]{1,0:T(8,128)(2,1)S(1)} %slice_bitcast_fusion.3), channel_id=1, source_target_pairs={{0,3},{1,0},{2,1},{3,2},{4,7},{5,4},{6,5},{7,6},{8,11},{9,8},{10,9... | collective-permute-start | bytes 2359304 | tf_op jit(solution)/shard_map/ppermute | solution.py:1303
  638.2 32.8 %collective-permute-start.40 = (bf16[768,1544]{0,1:T(8,128)(2,1)}, bf16[768,1544]{0,1:T(8,128)(2,1)}, u32[]{:S(2)}, u32[]{:S(2)}) collective-permute-start(bf16[768,1544]{0,1:T(8,128)(2,1)} %copy.84), channel_id=1, source_target_pairs={{0,4},{4,0},{1,5},{5,1},{2,6},{6,2},{3,7},{7,3},{8,12},{12,8},{9,1... | collective-permute-start | bytes 7114760 | tf_op jit(solution)/shard_map/ppermute | solution.py:1544
  639.7 20.2 %collective-permute-start.33 = (bf16[256,1536]{1,0:T(8,128)(2,1)S(1)}, bf16[256,1536]{1,0:T(8,128)(2,1)S(1)}, u32[]{:S(2)}, u32[]{:S(2)}) collective-permute-start(bf16[256,1536]{1,0:T(8,128)(2,1)S(1)} %fusion.3), channel_id=1, source_target_pairs={{0,3},{1,0},{2,1},{3,2},{4,7},{5,4},{6,5},{7,6},{8,11},{9,8},{10,9... | collective-permute-start | bytes 2359304 | tf_op jit(solution)/shard_map/ppermute | solution.py:1303
  642.4 56.1 %collective-permute-start.36 = (bf16[512,1536]{1,0:T(8,128)(2,1)}, bf16[512,1536]{1,0:T(8,128)(2,1)}, u32[]{:S(2)}, u32[]{:S(2)}) collective-permute-start(bf16[512,1536]{1,0:T(8,128)(2,1)} %get-tuple-element.189), channel_id=1, source_target_pairs={{0,4},{4,0},{1,5},{5,1},{2,6},{6,2},{3,7},{7,3},{8,12},{12,8},{9,1... | collective-permute-start | bytes 4718600 | tf_op jit(solution)/shard_map/ppermute | solution.py:1544
  661.2 68.2 %collective-permute-start.37 = (bf16[256,1536]{1,0:T(8,128)(2,1)S(1)}, bf16[256,1536]{1,0:T(8,128)(2,1)}, u32[]{:S(2)}, u32[]{:S(2)}) collective-permute-start(bf16[256,1536]{1,0:T(8,128)(2,1)S(1)} %fusion.2), channel_id=1, source_target_pairs={{0,3},{1,0},{2,1},{3,2},{4,7},{5,4},{6,5},{7,6},{8,11},{9,8},{10,9... | collective-permute-start | bytes 2359304 | tf_op jit(solution)/shard_map/ppermute | solution.py:1303
  671.0 51.2 %collective-permute-start.38 = (bf16[384,1536]{1,0:T(8,128)(2,1)}, bf16[384,1536]{1,0:T(8,128)(2,1)}, u32[]{:S(2)}, u32[]{:S(2)}) collective-permute-start(bf16[384,1536]{1,0:T(8,128)(2,1)} %weight_grads.3), channel_id=1, source_target_pairs={{0,8},{8,0},{1,9},{9,1},{2,10},{10,2},{3,11},{11,3},{4,12},{12,4},... | collective-permute-start | bytes 3538952 | tf_op jit(solution)/shard_map/ppermute | solution.py:1544
  679.0 6.6 collective-permute-start.42
  685.6 8.6 %collective-permute-start.43 = (bf16[192,384]{1,0:T(8,128)(2,1)S(1)}, bf16[192,384]{1,0:T(8,128)(2,1)S(1)}, u32[]{:S(2)}, u32[]{:S(2)}) collective-permute-start(bf16[192,384]{1,0:T(8,128)(2,1)S(1)} %add_convert_fusion.3), channel_id=1, source_target_pairs={{0,3},{1,0},{2,1},{3,2},{4,7},{5,4},{6,5},{7,6},{8,11},{9,8},{10,9... | collective-permute-start | bytes 442376 | tf_op jit(solution)/shard_map/ppermute | solution.py:1303
  691.9 30.3 %collective-permute-start.39 = (bf16[384,1536]{1,0:T(8,128)(2,1)S(1)}, bf16[384,1536]{1,0:T(8,128)(2,1)S(1)}, u32[]{:S(2)}, u32[]{:S(2)}) collective-permute-start(bf16[384,1536]{1,0:T(8,128)(2,1)S(1)} %add_convert_fusion), channel_id=1, source_target_pairs={{0,1},{1,2},{2,3},{3,0},{4,5},{5,6},{6,7},{7,4},{8,9},{9,10},{10,1... | collective-permute-start | bytes 3538952 | tf_op jit(solution)/shard_map/ppermute | solution.py:1303
  694.2 27.1 %collective-permute-start.44 = (bf16[192,384]{1,0:T(8,128)(2,1)S(1)}, bf16[192,384]{1,0:T(8,128)(2,1)S(1)}, u32[]{:S(2)}, u32[]{:S(2)}) collective-permute-start(bf16[192,384]{1,0:T(8,128)(2,1)S(1)} %add_convert_fusion.2), channel_id=1, source_target_pairs={{0,3},{1,0},{2,1},{3,2},{4,7},{5,4},{6,5},{7,6},{8,11},{9,8},{10,9... | collective-permute-start | bytes 442376 | tf_op jit(solution)/shard_map/ppermute | solution.py:1303
  729.4 4.1 collective-permute-start.45
  742.8 5.3 collective-permute-start.46
  748.1 7.7 %collective-permute-start.47 = (f32[2,192]{0,1:T(8,128)S(1)}, f32[2,192]{0,1:T(8,128)S(1)}, u32[]{:S(2)}, u32[]{:S(2)}) collective-permute-start(f32[2,192]{0,1:T(8,128)S(1)} %fusion.8), channel_id=1, source_target_pairs={{0,2},{1,3},{2,0},{3,1},{4,6},{5,7},{6,4},{7,5},{8,10},{9,11},{10,... | collective-permute-start | bytes 4616 | tf_op jit(solution)/shard_map/ppermute | solution.py:1544
  (25 other events, 201.5 us)
Sparse Core Ops, SparseCore 0:
  16.0 43.2 all-gather.5
  64.6 58.6 all-gather.7
  166.9 37.1 all-gather.9
  205.8 57.0 all-gather.11
  291.5 69.2 all-gather.13
  363.6 57.1 reduce-scatter.5
  423.8 57.0 reduce-scatter.7
  532.8 53.8 reduce-scatter.13
  589.7 66.1 reduce-scatter.9
  678.2 46.7 reduce-scatter.11

commit v2 on v1

--- a/solution.py
+++ b/solution.py
@@ -104,16 +104,18 @@
         (HOP, 2): ((PROJECT, 1),),
         (HOP, 3): ((ATTEND, 1),),
         (CHUNK, 0, 0): (ATTN_ROWS,),
-        OUT_ALL: ((PROJECT, 1),),
+        OUT_ALL: (TURN_COT,),
         (CHUNK, 3, 0): (MIDDLE,),
         (TOK, 0, 2): ((HOP, 0),),
+        (OUT, 1): ((TOK, 1, 3),),
+        (OUT, 2): ((TOK, 1, 3),),
+        (OUT, 3): ((TOK, 1, 3),),
         (CHUNK, 1, 0): ((ATTEND, 1),),
         OUT_RS: ((GRAD_FAR, 0),),
     },
     "pins": {
         (ATTEND, 1): ((CHUNK, 0, 0),),
         (GRAD_FAR, 0): ((RING, 0, 1),),
-        (INPUT, 0): ((RING, 1, 2),),
         (DH, 0): ((SUM, 1),),
         (FEED, 1): ((MIX, 1, 1),),
         (DH, 1): ((RING, 0, 2),),
@@ -575,7 +577,7 @@
         ],
         name="project_rows",
         compiler_params=params(),
-        cost_estimate=cost(9),
+        cost_estimate=cost(0.0027),
     )(where, *pieces, weight, small, gain)
 
 
@@ -613,7 +615,7 @@
         out_shape=[same, same, tall_shape] if reorder else [tall_shape],
         name="turn_rows",
         compiler_params=params(),
-        cost_estimate=cost(3),
+        cost_estimate=cost(0.3),
     )(where, own, other)
 
 

time: 769 us -> 780 us (1.014)
  transfers between devices with their start and end apart: 58 -> 58, of which waited for: 20 -> 20; matrix products, arithmetic and copies ran while one was open for 6% -> 6% of each run, Pallas kernels for 45% -> 44%
where the time goes in v2:
time: 780 us; the launch traced here: 774 us
  Pallas kernels  342 us (44%)
  waiting for transfers between devices  254 us (33%)
  starting transfers between devices  87.7 us (11%)
  local copies, waits for them, and re-layouts  50 us (6%)
  other arithmetic  24.5 us (3%)
  between operations  15.3 us (2%)
    ppermute x33, waiting for transfers between devices, shift(): lax.ppermute(values, axis, [(i, (i + step) % size) for i in range(size)])  243 us
    ppermute x33, starting transfers between devices, shift(): lax.ppermute(values, axis, [(i, (i + step) % size) for i in range(size)])  76.7 us
    pallas_call x4, Pallas kernels, feed_forward_part(): pl.pallas_call(functools.partial(feed_kernel, columns // 3, first, last),...  64.3 us
    pallas_call x2, Pallas kernels, attention_backward(): pl.pallas_call(functools.partial(backward_kernel, len(grad_out)), grid=(h...  43.6 us
    pallas_call x2, Pallas kernels, attention_forward(): pl.pallas_call(forward_kernel, grid=(heads,), in_specs=[pl.BlockSpec(memo...  41.7 us
    pallas_call x3, Pallas kernels, whole_weight_grads(): pl.pallas_call(whole_grad_kernel, grid_spec=pltpu.PrefetchScalarGridSpec(...  35.2 us
    pallas_call x2, Pallas kernels, project(): pl.pallas_call(project_kernel, grid_spec=pltpu.PrefetchScalarGridSpec(num...  24.8 us
    pallas_call x2, Pallas kernels, dh1_pieces(): pl.pallas_call(dh1_kernel, grid_spec=pltpu.PrefetchScalarGridSpec(num_sca...  23.2 us
  transfers between devices with their start and end apart: 58, of which 20 were waited for; matrix products, arithmetic and copies ran while one was open for 6% of the time, Pallas kernels for 44%

profile of v2, /device:TPU:0, one launch (start us, length us, event | category | flops | bytes accessed | tf_op | source)
XLA Modules:
  0.0 774.0 jit_solution(9993258855488106085)
XLA Ops:
  18.1 3.1 collective-permute-start
  21.2 2.7 maximum_select_fusion
  23.9 16.8 %collective-permute-done.p1 = bf16[256,1536]{1,0:T(8,128)(2,1)S(1)} collective-permute-done((bf16[256,1536]{1,0:T(8,128)(2,1)S(1)}, bf16[256,1536]{1,0:T(8,128)(2,1)S(1)}, u32[]{:S(2)}, u32[]{:S(2)}) %collective-permute-start) | collective-permute-done | bytes 786464 | tf_op jit(solution)/shard_map/ppermute | solution.py:1305
  42.1 21.0 %collective-permute-done.2.p2 = bf16[256,1536]{1,0:T(8,128)(2,1)} collective-permute-done((bf16[256,1536]{1,0:T(8,128)(2,1)S(1)}, bf16[256,1536]{1,0:T(8,128)(2,1)}, u32[]{:S(2)}, u32[]{:S(2)}) %collective-permute-start.2) | collective-permute-done | bytes 786464 | tf_op jit(solution)/shard_map/ppermute | solution.py:1305
  64.6 15.4 %collective-permute-done.5.p1 = bf16[256,1536]{1,0:T(8,128)(2,1)} collective-permute-done((bf16[256,1536]{1,0:T(8,128)(2,1)S(1)}, bf16[256,1536]{1,0:T(8,128)(2,1)}, u32[]{:S(2)}, u32[]{:S(2)}) %collective-permute-start.5) | collective-permute-done | bytes 786464 | tf_op jit(solution)/shard_map/ppermute | solution.py:1305
  84.9 11.8 %collective-permute-done.3.p3 = bf16[256,1536]{1,0:T(8,128)(2,1)S(1)} collective-permute-done((bf16[256,1536]{1,0:T(8,128)(2,1)}, bf16[256,1536]{1,0:T(8,128)(2,1)S(1)}, u32[]{:S(2)}, u32[]{:S(2)}) %collective-permute-start.3) | collective-permute-done | bytes 786464 | tf_op jit(solution)/shard_map/ppermute | solution.py:1305
  97.6 12.4 %project_rows.2 = (bf16[1024,1536]{1,0:T(8,128)(2,1)}, bf16[1024,1536]{1,0:T(8,128)(2,1)}, f32[8,1024]{1,0:T(8,128)}) custom-call(s32[17]{0:T(128)} %stack.71.where_ref, bf16[256,1536]{1,0:T(8,128)(2,1)} %copy-done.3, bf16[256,1536]{1,0:T(8,128)(2,1)} %copy-done.10, bf16[256,1536]{1,0:T(8,128)(2,1)} %collective-permute-done.2.p2, ...), custom_call_target="tpu_custom_call" | custom-call | flops 6750000 | bytes 1 | tf_op jit(solution)/shard_map/project_rows/pallas_call | solution.py:560
  110.0 20.9 %attention_forward.2 = (bf16[4,256,384]{2,1,0:T(8,128)(2,1)}, bf16[1024,384]{1,0:T(8,128)(2,1)}, bf16[1024,384]{1,0:T(8,128)(2,1)}, bf16[1024,384]{1,0:T(8,128)(...) custom-call(s32[17]{0:T(128)} %stack.71.where_ref, ...), custom_call_target="tpu_custom_call" | custom-call | flops 52500000768 | bytes 1 | tf_op jit(solution)/shard_map/attention_forward/pallas_call | solution.py:452
  130.9 18.0 %collective-permute-done.7.p3 = bf16[256,1536]{1,0:T(8,128)(2,1)S(1)} collective-permute-done((bf16[256,1536]{1,0:T(8,128)(2,1)S(1)}, bf16[256,1536]{1,0:T(8,128)(2,1)S(1)}, u32[]{:S(2)}, u32[]{:S(2)}) %collective-permute-start.7) | collective-permute-done | bytes 786464 | tf_op jit(solution)/shard_map/ppermute | solution.py:1305
  149.0 3.8 collective-permute-start.16
  153.9 5.9 turn_rows.2
  162.7 12.4 %project_rows.3 = (bf16[1024,1536]{1,0:T(8,128)(2,1)}, bf16[1024,1536]{1,0:T(8,128)(2,1)}, f32[8,1024]{1,0:T(8,128)}) custom-call(s32[17]{0:T(128)} %stack.71.where_ref, bf16[256,1536]{1,0:T(8,128)(2,1)} %copy-done.2, bf16[256,1536]{1,0:T(8,128)(2,1)} %collective-permute-done.5.p1, bf16[256,1536]{1,0:T(8,128)(2,1)} %copy-done.12, ...), custom_call_target="tpu_custom_call" | custom-call | flops 6750000 | bytes 1 | tf_op jit(solution)/shard_map/project_rows/pallas_call | solution.py:560
  175.1 20.8 %attention_forward.3 = (bf16[4,256,384]{2,1,0:T(8,128)(2,1)}, bf16[1024,384]{1,0:T(8,128)(2,1)}, bf16[1024,384]{1,0:T(8,128)(2,1)}, bf16[1024,384]{1,0:T(8,128)(...) custom-call(s32[17]{0:T(128)} %stack.71.where_ref, ...), custom_call_target="tpu_custom_call" | custom-call | flops 52500000768 | bytes 1 | tf_op jit(solution)/shard_map/attention_forward/pallas_call | solution.py:452
  198.2 3.8 collective-permute-start.10
  203.4 3.3 collective-permute-start.13
  207.8 7.3 collective-permute-start.11
  215.0 25.7 %collective-permute-done.9.refs_2_ = bf16[256,384]{1,0:T(8,128)(2,1)S(1)} collective-permute-done((bf16[256,384]{1,0:T(8,128)(2,1)S(1)}, bf16[256,384]{1,0:T(8,128)(2,1)S(1)}, u32[]{:S(2)}, u32[]{:S(2)}) %collective-permute-start.9) | collective-permute-done | bytes 196640 | tf_op jit(solution)/shard_map/ppermute | solution.py:1305
  241.2 19.3 %collective-permute-done.12.refs_6_ = bf16[256,384]{1,0:T(8,128)(2,1)S(1)} collective-permute-done((bf16[256,384]{1,0:T(8,128)(2,1)S(1)}, bf16[256,384]{1,0:T(8,128)(2,1)S(1)}, u32[]{:S(2)}, u32[]{:S(2)}) %collective-permute-start.12) | collective-permute-done | bytes 196640 | tf_op jit(solution)/shard_map/ppermute | solution.py:1305
  261.2 10.3 %middle_rows.1 = (f32[512,1536]{1,0:T(8,128)}, bf16[512,1536]{1,0:T(8,128)(2,1)}) custom-call(s32[17]{0:T(128)} %stack.71.where_ref, bf16[256,384]{1,0:T(8,128)(2,1)} %get-tuple-element.128.refs_0_, bf16[256,384]{1,0:T(8,128)(2,1)} %copy-done.28, bf16[256,384]{1,0:T(8,128)(2,1)} %copy-done.27, bf16[256,384]{1,0:T(8,128)(2,1)} %copy-done.26, ...), custom_call_target="tpu_custom_call" | custom-call | flops 12499999744 | bytes 1 | tf_op jit(solution)/shard_map/middle_rows/pallas_call | solution.py:665
  275.1 26.7 %collective-permute-done.23 = bf16[384,1536]{1,0:T(8,128)(2,1)S(1)} collective-permute-done((bf16[384,1536]{1,0:T(8,128)(2,1)}, bf16[384,1536]{1,0:T(8,128)(2,1)S(1)}, u32[]{:S(2)}, u32[]{:S(2)}) %collective-permute-start.23) | collective-permute-done | bytes 1179680 | tf_op jit(solution)/shard_map/ppermute | solution.py:1305
  304.2 15.0 %feed_forward.4 = (bf16[1024,1536]{1,0:T(8,128)(2,1)}, f32[1024,1536]{1,0:T(8,128)}) custom-call(s32[17]{0:T(128)} %stack.71.where_ref, bf16[512,1536]{1,0:T(8,128)(2,1)} %get-tuple-element.157.refs_0_.own_ref, bf16[512,1536]{1,0:T(8,128)(2,1)} %copy-done.6, bf16[512,1536]{1,0:T(8,128)(2,1)} %get-tuple-element.113.refs_2_.cot_ref, ...), custom_call_target="tpu_custom_call" | custom-call | flops 37499998208 | bytes 1 | tf_op jit(solution)/shard_map/feed_forward/pallas_call | solution.py:780
  319.2 5.3 turn_rows.3.h_ref.refs_0_
  324.4 15.4 %feed_forward.5 = (bf16[1024,1536]{1,0:T(8,128)(2,1)}, f32[1024,1536]{1,0:T(8,128)}) custom-call(s32[17]{0:T(128)} %stack.71.where_ref, bf16[512,1536]{1,0:T(8,128)(2,1)} %get-tuple-element.157.refs_0_.own_ref, bf16[512,1536]{1,0:T(8,128)(2,1)} %copy-done.6, bf16[512,1536]{1,0:T(8,128)(2,1)} %get-tuple-element.113.refs_2_.cot_ref, ...), custom_call_target="tpu_custom_call", output_to_operand_aliasing={{1}: (6, {})} | custom-call | flops 37499998208 | bytes 1 | tf_op jit(solution)/shard_map/feed_forward/pallas_call | solution.py:780
  339.9 11.8 %whole_grads.3 = bf16[1536,1536]{1,0:T(8,128)(2,1)} custom-call(s32[17]{0:T(128)} %stack.71.where_ref, bf16[1536,1024]{1,0:T(8,128)(2,1)} %turn_rows.3.h_ref.refs_0_, bf16[1536,1024]{1,0:T(8,128)(2,1)} %get-tuple-element.131.c_ref.refs_1_, bf16[1024,1536]{1,0:T(8,128)(2,1)} %get-tuple-element.150.act.refs_1_), custom_call_target="tpu_custom_call" | custom-call | flops 24999999488 | bytes 1 | tf_op jit(solution)/shard_map/whole_grads/pallas_call | solution.py:881
  352.0 15.4 %feed_forward.6 = (bf16[1024,1536]{1,0:T(8,128)(2,1)}, f32[1024,1536]{1,0:T(8,128)}) custom-call(s32[17]{0:T(128)} %stack.71.where_ref, bf16[512,1536]{1,0:T(8,128)(2,1)} %get-tuple-element.157.refs_0_.own_ref, bf16[512,1536]{1,0:T(8,128)(2,1)} %copy-done.6, bf16[512,1536]{1,0:T(8,128)(2,1)} %get-tuple-element.113.refs_2_.cot_ref, ...), custom_call_target="tpu_custom_call", output_to_operand_aliasing={{1}: (9, {})} | custom-call | flops 37499998208 | bytes 1 | tf_op jit(solution)/shard_map/feed_forward/pallas_call | solution.py:780
  367.4 11.7 %whole_grads.4 = bf16[1536,1536]{1,0:T(8,128)(2,1)} custom-call(s32[17]{0:T(128)} %stack.71.where_ref, bf16[1536,1024]{1,0:T(8,128)(2,1)} %turn_rows.3.h_ref.refs_0_, bf16[1536,1024]{1,0:T(8,128)(2,1)} %get-tuple-element.131.c_ref.refs_1_, bf16[1024,1536]{1,0:T(8,128)(2,1)} %get-tuple-element.156.act.refs_2_), custom_call_target="tpu_custom_call" | custom-call | flops 24999999488 | bytes 1 | tf_op jit(solution)/shard_map/whole_grads/pallas_call | solution.py:881
  379.1 18.5 %feed_forward.7 = (bf16[1024,1536]{1,0:T(8,128)(2,1)}, f32[512,1536]{1,0:T(8,128)}, bf16[512,1536]{1,0:T(8,128)(2,1)}) custom-call(s32[17]{0:T(128)} %stack.71.where_ref, bf16[512,1536]{1,0:T(8,128)(2,1)} %get-tuple-element.157.refs_0_.own_ref, bf16[512,1536]{1,0:T(8,128)(2,1)} %copy-done.6, bf16[512,1536]{1,0:T(8,128)(2,1)} %get-tuple-element.113.refs_2_.cot_ref, ...), custom_call_target="tpu_custom_call" | custom-call | flops 37499998208 | bytes 1 | tf_op jit(solution)/shard_map/feed_forward/pallas_call | solution.py:780
  397.8 3.5 collective-permute-done.24.recv_ref
  402.4 13.2 %norm_two.1 = (f32[512,1536]{1,0:T(8,128)}, bf16[512,1536]{1,0:T(8,128)(2,1)}, bf16[4,2,256,384]{3,2,1,0:T(8,128)(2,1)}, f32[1,1536]{1,0:T(1,128)}) custom-call(s32[17]{0:T(128)} %stack.71.where_ref, f32[512,1536]{1,0:T(8,128)} %get-tuple-element.163.own_ref, bf16[512,1536]{1,0:T(8,128)(2,1)} %copy-done.22, f32[512,1536]{1,0:T(8,128)} %get-tuple-element.190.mid_ref, ...), custom_call_target="tpu_custom_call" | custom-call | flops 15000000512 | bytes 1 | tf_op jit(solution)/shard_map/norm_two/pallas_call | solution.py:1050
  418.2 3.8 collective-permute-start.25
  422.0 11.7 %whole_grads.5 = bf16[1536,1536]{1,0:T(8,128)(2,1)} custom-call(s32[17]{0:T(128)} %stack.71.where_ref, bf16[1536,1024]{1,0:T(8,128)(2,1)} %turn_rows.3.h_ref.refs_0_, bf16[1536,1024]{1,0:T(8,128)(2,1)} %get-tuple-element.131.c_ref.refs_1_, bf16[1024,1536]{1,0:T(8,128)(2,1)} %get-tuple-element.167.act.refs_3_), custom_call_target="tpu_custom_call" | custom-call | flops 24999999488 | bytes 1 | tf_op jit(solution)/shard_map/whole_grads/pallas_call | solution.py:881
  433.8 7.3 out_grads.1
  441.0 3.4 slice_bitcast_fusion.2
  448.3 21.9 %attention_backward.2 = (bf16[1024,1536]{1,0:T(8,128)(2,1)}, f32[8,1024]{1,0:T(8,128)}) custom-call(s32[17]{0:T(128)} %stack.71.where_ref, s32[1]{0:T(128)} %bitcast.16.length_ref, bf16[1024,1536]{1,0:T(8,128)(2,1)} %get-tuple-element.169.x_ref, f32[8,1024]{1,0:T(8,128)} %get-tuple-element.109.logit_ref, bf16[2,256,384]{2,1,0:T(8,128)(2,1)} %get-tuple-element.275.refs_0_, ...), custom_call_target="tpu_custom_call" | custom-call | flops 54999998464 | bytes 1 | tf_op jit(solution)/shard_map/attention_backward/pallas_call | solution.py:489
  470.2 5.0 collective-permute-done.28
  475.1 11.9 %dh1_rows.2 = (bf16[4,256,1536]{2,1,0:T(8,128)(2,1)}, f32[1,1536]{1,0:T(1,128)}) custom-call(s32[17]{0:T(128)} %stack.71.where_ref, bf16[1024,1536]{1,0:T(8,128)(2,1)} %get-tuple-element.184.d_ref.refs_2_, f32[8,1024]{1,0:T(8,128)} %get-tuple-element.173.l_ref.refs_4_, bf16[1024,1536]{1,0:T(8,128)(2,1)} %get-tuple-element.174.h_ref.refs_0_, ...), custom_call_target="tpu_custom_call" | custom-call | flops 20000000 | bytes 1 | tf_op jit(solution)/shard_map/dh1_rows/pallas_call | solution.py:1103
  489.1 3.3 collective-permute-start.29
  492.4 14.8 %down_rows.1 = (f32[512,1536]{1,0:T(8,128)}, bf16[512,1536]{1,0:T(8,128)(2,1)}) custom-call(s32[17]{0:T(128)} %stack.71.where_ref, bf16[1024,1536]{1,0:T(8,128)(2,1)} %get-tuple-element.192.refs_0_.refs_2_.act, bf16[1024,1536]{1,0:T(8,128)(2,1)} %get-tuple-element.150.act.refs_1_, bf16[1024,1536]{1,0:T(8,128)(2,1)} %get-tuple-element.156.act.refs_2_, ...), custom_call_target="tpu_custom_call" | custom-call | flops 24999999488 | bytes 1 | tf_op jit(solution)/shard_map/down_rows/pallas_call | solution.py:843
  507.2 27.5 %collective-permute-done.29 = bf16[256,1536]{1,0:T(8,128)(2,1)} collective-permute-done((bf16[256,1536]{1,0:T(8,128)(2,1)}, bf16[256,1536]{1,0:T(8,128)(2,1)}, u32[]{:S(2)}, u32[]{:S(2)}) %collective-permute-start.29) | collective-permute-done | bytes 786464 | tf_op jit(solution)/shard_map/ppermute | solution.py:1305
  534.7 6.6 weight_grads.2
  551.5 14.6 %collective-permute-done.30 = bf16[256,1536]{1,0:T(8,128)(2,1)S(1)} collective-permute-done((bf16[256,1536]{1,0:T(8,128)(2,1)S(1)}, bf16[256,1536]{1,0:T(8,128)(2,1)S(1)}, u32[]{:S(2)}, u32[]{:S(2)}) %collective-permute-start.30) | collective-permute-done | bytes 786464 | tf_op jit(solution)/shard_map/ppermute | solution.py:1305
  569.3 21.7 %attention_backward.3 = (bf16[1024,1536]{1,0:T(8,128)(2,1)}, f32[8,1024]{1,0:T(8,128)}) custom-call(s32[17]{0:T(128)} %stack.71.where_ref, s32[1]{0:T(128)} %bitcast.23.length_ref, bf16[1024,1536]{1,0:T(8,128)(2,1)} %get-tuple-element.179.x_ref, f32[8,1024]{1,0:T(8,128)} %get-tuple-element.125.logit_ref, bf16[2,256,384]{2,1,0:T(8,128)(2,1)} %get-tuple-element.275.refs_0_, ...), custom_call_target="tpu_custom_call" | custom-call | flops 54999998464 | bytes 1 | tf_op jit(solution)/shard_map/attention_backward/pallas_call | solution.py:489
  591.0 11.3 %dh1_rows.3 = (bf16[4,256,1536]{2,1,0:T(8,128)(2,1)}, f32[1,1536]{1,0:T(1,128)}) custom-call(s32[17]{0:T(128)} %stack.71.where_ref, bf16[1024,1536]{1,0:T(8,128)(2,1)} %get-tuple-element.181.d_ref.refs_3_, f32[8,1024]{1,0:T(8,128)} %get-tuple-element.182.l_ref.refs_5_, bf16[1024,1536]{1,0:T(8,128)(2,1)} %get-tuple-element.152.h_ref.refs_1_, ...), custom_call_target="tpu_custom_call" | custom-call | flops 20000000 | bytes 1 | tf_op jit(solution)/shard_map/dh1_rows/pallas_call | solution.py:1103
  603.5 22.5 %collective-permute-start.32 = (bf16[256,1536]{1,0:T(8,128)(2,1)S(1)}, bf16[256,1536]{1,0:T(8,128)(2,1)}, u32[]{:S(2)}, u32[]{:S(2)}) collective-permute-start(bf16[256,1536]{1,0:T(8,128)(2,1)S(1)} %slice_bitcast_fusion.3), channel_id=1, source_target_pairs={{0,3},{1,0},{2,1},{3,2},{4,7},{5,4},{6,5},{7,6},{8,11},{9,8},{10,9... | collective-permute-start | bytes 2359304 | tf_op jit(solution)/shard_map/ppermute | solution.py:1305
  626.0 17.5 %attn_grads.1 = bf16[2,768,1544]{2,1,0:T(8,128)(2,1)} custom-call(s32[17]{0:T(128)} %stack.71.where_ref, bf16[1024,1536]{1,0:T(8,128)(2,1)} %get-tuple-element.174.h_ref.refs_0_, bf16[1024,1536]{1,0:T(8,128)(2,1)} %get-tuple-element.152.h_ref.refs_1_, bf16[1024,1536]{1,0:T(8,128)(2,1)} %get-tuple-element.184.d_ref.refs_2_, ...), custom_call_target="tpu_custom_call" | custom-call | flops 35000000512 | bytes 1 | tf_op jit(solution)/shard_map/attn_grads/pallas_call | solution.py:1174
  649.8 3.1 collective-permute-start.36
  653.1 5.2 weight_grads.3
  660.0 10.4 %collective-permute-done.36 = bf16[256,1536]{1,0:T(8,128)(2,1)S(1)} collective-permute-done((bf16[256,1536]{1,0:T(8,128)(2,1)S(1)}, bf16[256,1536]{1,0:T(8,128)(2,1)S(1)}, u32[]{:S(2)}, u32[]{:S(2)}) %collective-permute-start.36) | collective-permute-done | bytes 786464 | tf_op jit(solution)/shard_map/ppermute | solution.py:1305
  671.7 4.5 collective-permute-start.37
  676.2 3.3 copy.85
  679.5 3.8 fusion
  684.4 4.3 input_grad.2.refs_0_
  688.7 7.4 collective-permute-done.42
  696.1 4.3 collective-permute-start.43
  704.7 4.3 collective-permute-start.44
  709.1 5.9 block_out.1
  714.9 16.9 %collective-permute-done.44 = bf16[192,384]{1,0:T(8,128)(2,1)S(1)} collective-permute-done((bf16[192,384]{1,0:T(8,128)(2,1)S(1)}, bf16[192,384]{1,0:T(8,128)(2,1)S(1)}, u32[]{:S(2)}, u32[]{:S(2)}) %collective-permute-start.44) | collective-permute-done | bytes 147488 | tf_op jit(solution)/shard_map/ppermute | solution.py:1305
  733.6 6.2 last_weight_grad.1
  739.8 4.1 input_grad.3
  744.8 2.9 finish_grads.1
  749.3 3.6 slice_reduce_fusion
  754.2 4.2 collective-permute-done.46
  758.5 2.8 collective-permute-start.47
  762.8 3.4 collective-permute-done.47
  (218 shorter events, 82.2 us)
Async XLA Ops:
  7.2 73.0 %all-gather.6.cloned.1.call-start = ((), (), s32[]{:S(2)}) async-start(), calls=%async_computation.5 | async-start | bytes 5750784 | tf_op jit(solution)/shard_map/all_gather | solution.py:1659
  15.9 159.2 %all-gather.8.cloned.1.call-start = ((), (), s32[]{:S(2)}) async-start(), calls=%async_computation.6 | async-start | bytes 5898240 | tf_op jit(solution)/shard_map/all_gather | solution.py:1676
  17.3 3.9 collective-permute-start.1
  18.1 22.6 %collective-permute-start = (bf16[256,1536]{1,0:T(8,128)(2,1)S(1)}, bf16[256,1536]{1,0:T(8,128)(2,1)S(1)}, u32[]{:S(2)}, u32[]{:S(2)}) collective-permute-start(bf16[256,1536]{1,0:T(8,128)(2,1)S(1)} %get-tuple-element.277.p0), channel_id=1, source_target_pairs={{0,1},{1,2},{2,3},{3,0},{4,5},{5,6},{6,7},{7,4},{8,9},{9,10},{10,1... | collective-permute-start | bytes 2359304 | tf_op jit(solution)/shard_map/ppermute | solution.py:1305
  21.2 42.8 %copy-start.21 = (s32[2,1]{0,1:T(1,128)S(1)}, s32[2,1]{0,1:T(1,128)}, u32[]{:S(2)}) copy-start(s32[2,1]{0,1:T(1,128)} %param.15) | copy-start | bytes 28
  40.7 22.4 %collective-permute-start.2 = (bf16[256,1536]{1,0:T(8,128)(2,1)S(1)}, bf16[256,1536]{1,0:T(8,128)(2,1)}, u32[]{:S(2)}, u32[]{:S(2)}) collective-permute-start(bf16[256,1536]{1,0:T(8,128)(2,1)S(1)} %collective-permute-done.p1), channel_id=1, source_target_pairs={{0,1},{1,2},{2,3},{3,0},{4,5},{5,6},{6,7},{7,4},{8,9},{9,10},{10,1... | collective-permute-start | bytes 2359304 | tf_op jit(solution)/shard_map/ppermute | solution.py:1305
  40.7 39.2 %collective-permute-start.5 = (bf16[256,1536]{1,0:T(8,128)(2,1)S(1)}, bf16[256,1536]{1,0:T(8,128)(2,1)}, u32[]{:S(2)}, u32[]{:S(2)}) collective-permute-start(bf16[256,1536]{1,0:T(8,128)(2,1)S(1)} %get-tuple-element.114.p0), channel_id=1, source_target_pairs={{0,1},{1,2},{2,3},{3,0},{4,5},{5,6},{6,7},{7,4},{8,9},{9,10},{10,1... | collective-permute-start | bytes 2359304 | tf_op jit(solution)/shard_map/ppermute | solution.py:1305
  42.1 218.4 %all-gather.10.cloned.1.call-start = ((), (), s32[]{:S(2)}) async-start(), calls=%async_computation.7 | async-start | bytes 5308416 | tf_op jit(solution)/shard_map/all_gather | solution.py:1683
  63.1 33.6 %collective-permute-start.3 = (bf16[256,1536]{1,0:T(8,128)(2,1)}, bf16[256,1536]{1,0:T(8,128)(2,1)S(1)}, u32[]{:S(2)}, u32[]{:S(2)}) collective-permute-start(bf16[256,1536]{1,0:T(8,128)(2,1)} %collective-permute-done.2.p2), channel_id=1, source_target_pairs={{0,1},{1,2},{2,3},{3,0},{4,5},{5,6},{6,7},{7,4},{8,9},{9,10},{10,1... | collective-permute-start | bytes 2359304 | tf_op jit(solution)/shard_map/ppermute | solution.py:1305
  63.1 89.7 %collective-permute-start.4 = (bf16[512,1536]{1,0:T(8,128)(2,1)}, bf16[512,1536]{1,0:T(8,128)(2,1)S(1)}, u32[]{:S(2)}, u32[]{:S(2)}) collective-permute-start(bf16[512,1536]{1,0:T(8,128)(2,1)} %bitcast.125), channel_id=1, source_target_pairs={{0,4},{4,0},{1,5},{5,1},{2,6},{6,2},{3,7},{7,3},{8,12},{12,8},{9,1... | collective-permute-start | bytes 4718600 | tf_op jit(solution)/shard_map/ppermute | solution.py:1546
  80.0 50.9 %collective-permute-start.6 = (bf16[256,1536]{1,0:T(8,128)(2,1)}, bf16[256,1536]{1,0:T(8,128)(2,1)S(1)}, u32[]{:S(2)}, u32[]{:S(2)}) collective-permute-start(bf16[256,1536]{1,0:T(8,128)(2,1)} %collective-permute-done.5.p1), channel_id=1, source_target_pairs={{0,1},{1,2},{2,3},{3,0},{4,5},{5,6},{6,7},{7,4},{8,9},{9,10},{10,1... | collective-permute-start | bytes 2359304 | tf_op jit(solution)/shard_map/ppermute | solution.py:1305
  110.0 39.0 %copy-start.20 = (bf16[384,192]{0,1:T(8,128)(2,1)S(1)}, bf16[384,192]{0,1:T(8,128)(2,1)}, u32[]{:S(2)}) copy-start(bf16[384,192]{0,1:T(8,128)(2,1)} %param.22) | copy-start | bytes 442372
  130.8 18.1 %collective-permute-start.7 = (bf16[256,1536]{1,0:T(8,128)(2,1)S(1)}, bf16[256,1536]{1,0:T(8,128)(2,1)S(1)}, u32[]{:S(2)}, u32[]{:S(2)}) collective-permute-start(bf16[256,1536]{1,0:T(8,128)(2,1)S(1)} %collective-permute-done.6.p2), channel_id=1, source_target_pairs={{0,1},{1,2},{2,3},{3,0},{4,5},{5,6},{6,7},{7,4},{8,9},{9,10},{10,1... | collective-permute-start | bytes 2359304 | tf_op jit(solution)/shard_map/ppermute | solution.py:1305
  149.0 10.9 %collective-permute-start.14 = (bf16[192,384]{1,0:T(8,128)(2,1)S(1)}, bf16[192,384]{1,0:T(8,128)(2,1)S(1)}, u32[]{:S(2)}, u32[]{:S(2)}) collective-permute-start(bf16[192,384]{1,0:T(8,128)(2,1)S(1)} %bitcast.136), channel_id=1, source_target_pairs={{0,1},{1,2},{2,3},{3,0},{4,5},{5,6},{6,7},{7,4},{8,9},{9,10},{10,1... | collective-permute-start | bytes 442376 | tf_op jit(solution)/shard_map/ppermute | solution.py:1305
  149.0 10.9 %collective-permute-start.16 = (bf16[192,384]{1,0:T(8,128)(2,1)S(1)}, bf16[192,384]{1,0:T(8,128)(2,1)S(1)}, u32[]{:S(2)}, u32[]{:S(2)}) collective-permute-start(bf16[192,384]{1,0:T(8,128)(2,1)S(1)} %bitcast.137), channel_id=1, source_target_pairs={{0,3},{1,0},{2,1},{3,2},{4,7},{5,4},{6,5},{7,6},{8,11},{9,8},{10,9... | collective-permute-start | bytes 442376 | tf_op jit(solution)/shard_map/ppermute | solution.py:1305
  152.8 8.6 %collective-permute-start.15 = (bf16[192,384]{1,0:T(8,128)(2,1)S(1)}, bf16[192,384]{1,0:T(8,128)(2,1)S(1)}, u32[]{:S(2)}, u32[]{:S(2)}) collective-permute-start(bf16[192,384]{1,0:T(8,128)(2,1)S(1)} %bitcast.138), channel_id=1, source_target_pairs={{0,2},{1,3},{2,0},{3,1},{4,6},{5,7},{6,4},{7,5},{8,10},{9,11},{10,... | collective-permute-start | bytes 442376 | tf_op jit(solution)/shard_map/ppermute | solution.py:1305
  162.3 162.1 %all-gather.12.cloned.1.call-start = ((), (), s32[]{:S(2)}) async-start(), calls=%async_computation.8 | async-start | bytes 5898240 | tf_op jit(solution)/shard_map/all_gather | solution.py:1676
  162.4 33.6 %collective-permute-start.18 = (bf16[384,1536]{1,0:T(8,128)(2,1)S(1)}, bf16[384,1536]{1,0:T(8,128)(2,1)S(1)}, u32[]{:S(2)}, u32[]{:S(2)}) collective-permute-start(bf16[384,1536]{1,0:T(8,128)(2,1)S(1)} %copy-done.1), channel_id=1, source_target_pairs={{0,1},{1,2},{2,3},{3,0},{4,5},{5,6},{6,7},{7,4},{8,9},{9,10},{10,1... | collective-permute-start | bytes 3538952 | tf_op jit(solution)/shard_map/ppermute | solution.py:1305
  197.0 43.7 %copy-start.8 = (bf16[384,1536]{1,0:T(8,128)(2,1)S(1)}, bf16[384,1536]{1,0:T(8,128)(2,1)}, u32[]{:S(2)}) copy-start(bf16[384,1536]{1,0:T(8,128)(2,1)} %copy-done.7) | copy-start | bytes 3538948
  197.0 182.1 %all-gather.14.cloned.1.call-start = ((), (), s32[]{:S(2)}) async-start(), calls=%async_computation.9 | async-start | bytes 5898240 | tf_op jit(solution)/shard_map/all_gather | solution.py:1676
  198.2 9.5 %collective-permute-start.10 = (bf16[256,384]{1,0:T(8,128)(2,1)S(1)}, bf16[256,384]{1,0:T(8,128)(2,1)S(1)}, u32[]{:S(2)}, u32[]{:S(2)}) collective-permute-start(bf16[256,384]{1,0:T(8,128)(2,1)S(1)} %get-tuple-element.284), channel_id=1, source_target_pairs={{0,3},{1,0},{2,1},{3,2},{4,7},{5,4},{6,5},{7,6},{8,11},{9,8},{10,9... | collective-permute-start | bytes 589832 | tf_op jit(solution)/shard_map/ppermute | solution.py:1305
  202.0 38.6 %collective-permute-start.9 = (bf16[256,384]{1,0:T(8,128)(2,1)S(1)}, bf16[256,384]{1,0:T(8,128)(2,1)S(1)}, u32[]{:S(2)}, u32[]{:S(2)}) collective-permute-start(bf16[256,384]{1,0:T(8,128)(2,1)S(1)} %get-tuple-element.285), channel_id=1, source_target_pairs={{0,2},{1,3},{2,0},{3,1},{4,6},{5,7},{6,4},{7,5},{8,10},{9,11},{10,... | collective-permute-start | bytes 589832 | tf_op jit(solution)/shard_map/ppermute | solution.py:1305
  202.0 39.1 %collective-permute-start.8 = (bf16[256,384]{1,0:T(8,128)(2,1)S(1)}, bf16[256,384]{1,0:T(8,128)(2,1)S(1)}, u32[]{:S(2)}, u32[]{:S(2)}) collective-permute-start(bf16[256,384]{1,0:T(8,128)(2,1)S(1)} %get-tuple-element.286), channel_id=1, source_target_pairs={{0,1},{1,2},{2,3},{3,0},{4,5},{5,6},{6,7},{7,4},{8,9},{9,10},{10,1... | collective-permute-start | bytes 589832 | tf_op jit(solution)/shard_map/ppermute | solution.py:1305
  203.4 37.8 %collective-permute-start.13 = (bf16[256,384]{1,0:T(8,128)(2,1)S(1)}, bf16[256,384]{1,0:T(8,128)(2,1)S(1)}, u32[]{:S(2)}, u32[]{:S(2)}) collective-permute-start(bf16[256,384]{1,0:T(8,128)(2,1)S(1)} %get-tuple-element.280), channel_id=1, source_target_pairs={{0,3},{1,0},{2,1},{3,2},{4,7},{5,4},{6,5},{7,6},{8,11},{9,8},{10,9... | collective-permute-start | bytes 589832 | tf_op jit(solution)/shard_map/ppermute | solution.py:1305
  206.6 53.8 %collective-permute-start.12 = (bf16[256,384]{1,0:T(8,128)(2,1)S(1)}, bf16[256,384]{1,0:T(8,128)(2,1)S(1)}, u32[]{:S(2)}, u32[]{:S(2)}) collective-permute-start(bf16[256,384]{1,0:T(8,128)(2,1)S(1)} %get-tuple-element.281), channel_id=1, source_target_pairs={{0,2},{1,3},{2,0},{3,1},{4,6},{5,7},{6,4},{7,5},{8,10},{9,11},{10,... | collective-permute-start | bytes 589832 | tf_op jit(solution)/shard_map/ppermute | solution.py:1305
  207.8 52.7 %copy-start.26 = (bf16[256,384]{1,0:T(8,128)(2,1)}, bf16[256,384]{1,0:T(8,128)(2,1)S(1)}, u32[]{:S(2)}) copy-start(bf16[256,384]{1,0:T(8,128)(2,1)S(1)} %collective-permute-done.10.refs_3_) | copy-start | bytes 589828
  207.8 52.7 %collective-permute-start.11 = (bf16[256,384]{1,0:T(8,128)(2,1)S(1)}, bf16[256,384]{1,0:T(8,128)(2,1)S(1)}, u32[]{:S(2)}, u32[]{:S(2)}) collective-permute-start(bf16[256,384]{1,0:T(8,128)(2,1)S(1)} %get-tuple-element.282), channel_id=1, source_target_pairs={{0,1},{1,2},{2,3},{3,0},{4,5},{5,6},{6,7},{7,4},{8,9},{9,10},{10,1... | collective-permute-start | bytes 589832 | tf_op jit(solution)/shard_map/ppermute | solution.py:1305
  240.7 30.8 %collective-permute-start.19 = (bf16[384,1536]{1,0:T(8,128)(2,1)S(1)}, bf16[384,1536]{1,0:T(8,128)(2,1)}, u32[]{:S(2)}, u32[]{:S(2)}) collective-permute-start(bf16[384,1536]{1,0:T(8,128)(2,1)S(1)} %copy-done.8), channel_id=1, source_target_pairs={{0,1},{1,2},{2,3},{3,0},{4,5},{5,6},{6,7},{7,4},{8,9},{9,10},{10,1... | collective-permute-start | bytes 3538952 | tf_op jit(solution)/shard_map/ppermute | solution.py:1305
  271.5 31.5 %collective-permute-start.17 = (bf16[512,1536]{1,0:T(8,128)(2,1)}, bf16[512,1536]{1,0:T(8,128)(2,1)S(1)}, u32[]{:S(2)}, u32[]{:S(2)}) collective-permute-start(bf16[512,1536]{1,0:T(8,128)(2,1)} %get-tuple-element.157.refs_0_.own_ref), channel_id=1, source_target_pairs={{0,4},{4,0},{1,5},{5,1},{2,6},{6,2},{3,7},{7,3},{8,12},{12,8},{9,1... | collective-permute-start | bytes 4718600 | tf_op jit(solution)/shard_map/ppermute | solution.py:1546
  271.5 30.4 %collective-permute-start.23 = (bf16[384,1536]{1,0:T(8,128)(2,1)}, bf16[384,1536]{1,0:T(8,128)(2,1)S(1)}, u32[]{:S(2)}, u32[]{:S(2)}) collective-permute-start(bf16[384,1536]{1,0:T(8,128)(2,1)} %collective-permute-done.19.refs_4_.refs_6_), channel_id=1, source_target_pairs={{0,1},{1,2},{2,3},{3,0},{4,5},{5,6},{6,7},{7,4},{8,9},{9,10},{10,1... | collective-permute-start | bytes 3538952 | tf_op jit(solution)/shard_map/ppermute | solution.py:1305
  271.6 80.4 %collective-permute-start.22 = (bf16[384,1536]{1,0:T(8,128)(2,1)}, bf16[384,1536]{1,0:T(8,128)(2,1)}, u32[]{:S(2)}, u32[]{:S(2)}) collective-permute-start(bf16[384,1536]{1,0:T(8,128)(2,1)} %collective-permute-done.19.refs_4_.refs_6_), channel_id=1, source_target_pairs={{0,24},{8,16},{16,8},{24,0},{1,25},{9,17},{17,9},{25,1},{2,26},{10... | collective-permute-start | bytes 3538952 | tf_op jit(solution)/shard_map/ppermute | solution.py:1550
  274.0 78.0 %collective-permute-start.21 = (bf16[384,1536]{1,0:T(8,128)(2,1)}, bf16[384,1536]{1,0:T(8,128)(2,1)}, u32[]{:S(2)}, u32[]{:S(2)}) collective-permute-start(bf16[384,1536]{1,0:T(8,128)(2,1)} %collective-permute-done.19.refs_4_.refs_6_), channel_id=1, source_target_pairs={{0,16},{8,24},{16,0},{24,8},{1,17},{9,25},{17,1},{25,9},{2,18},{10... | collective-permute-start | bytes 3538952 | tf_op jit(solution)/shard_map/ppermute | solution.py:1550
  274.4 77.5 %collective-permute-start.20 = (bf16[384,1536]{1,0:T(8,128)(2,1)}, bf16[384,1536]{1,0:T(8,128)(2,1)}, u32[]{:S(2)}, u32[]{:S(2)}) collective-permute-start(bf16[384,1536]{1,0:T(8,128)(2,1)} %collective-permute-done.19.refs_4_.refs_6_), channel_id=1, source_target_pairs={{0,8},{8,0},{16,24},{24,16},{1,9},{9,1},{17,25},{25,17},{2,10},{10... | collective-permute-start | bytes 3538952 | tf_op jit(solution)/shard_map/ppermute | solution.py:1550
  302.9 141.5 %reduce-scatter.6.cloned.1.call-start = ((), (), s32[]{:S(2)}) async-start(), calls=%async_computation.10 | async-start | bytes 5898240 | tf_op jit(solution)/shard_map/reduce_scatter | solution.py:1773
  351.7 193.6 %reduce-scatter.8.cloned.1.call-start = ((), (), s32[]{:S(2)}) async-start(), calls=%async_computation.11 | async-start | bytes 5898240 | tf_op jit(solution)/shard_map/reduce_scatter | solution.py:1773
  397.6 3.7 collective-permute-start.24
  397.7 285.6 %reduce-scatter.14.cloned.1.call-start = ((), (), s32[]{:S(2)}) async-start(), calls=%async_computation.14 | async-start | bytes 2949120 | tf_op jit(solution)/shard_map/reduce_scatter | solution.py:1832
  418.2 27.6 %collective-permute-start.27 = (bf16[2,256,384]{2,1,0:T(8,128)(2,1)}, bf16[2,256,384]{2,1,0:T(8,128)(2,1)}, u32[]{:S(2)}, u32[]{:S(2)}) collective-permute-start(bf16[2,256,384]{2,1,0:T(8,128)(2,1)} %get-tuple-element.272), channel_id=1, source_target_pairs={{0,1},{1,2},{2,3},{3,0},{4,5},{5,6},{6,7},{7,4},{8,9},{9,10},{10,1... | collective-permute-start | bytes 1179656 | tf_op jit(solution)/shard_map/ppermute | solution.py:1305
  418.2 30.1 %collective-permute-start.26 = (bf16[2,256,384]{2,1,0:T(8,128)(2,1)}, bf16[2,256,384]{2,1,0:T(8,128)(2,1)}, u32[]{:S(2)}, u32[]{:S(2)}) collective-permute-start(bf16[2,256,384]{2,1,0:T(8,128)(2,1)} %get-tuple-element.273), channel_id=1, source_target_pairs={{0,2},{1,3},{2,0},{3,1},{4,6},{5,7},{6,4},{7,5},{8,10},{9,11},{10,... | collective-permute-start | bytes 1179656 | tf_op jit(solution)/shard_map/ppermute | solution.py:1305
  418.2 30.1 %collective-permute-start.25 = (bf16[2,256,384]{2,1,0:T(8,128)(2,1)}, bf16[2,256,384]{2,1,0:T(8,128)(2,1)}, u32[]{:S(2)}, u32[]{:S(2)}) collective-permute-start(bf16[2,256,384]{2,1,0:T(8,128)(2,1)} %get-tuple-element.274), channel_id=1, source_target_pairs={{0,3},{1,0},{2,1},{3,2},{4,7},{5,4},{6,5},{7,6},{8,11},{9,8},{10,9... | collective-permute-start | bytes 1179656 | tf_op jit(solution)/shard_map/ppermute | solution.py:1305
  444.4 96.9 %collective-permute-start.41 = (bf16[4,4,192,384]{3,2,1,0:T(8,128)(2,1)}, bf16[4,4,192,384]{3,2,1,0:T(8,128)(2,1)S(1)}, u32[]{:S(2)}, u32[]{:S(2)}) collective-permute-start(bf16[4,4,192,384]{3,2,1,0:T(8,128)(2,1)} %slice_bitcast_fusion.2), channel_id=1, source_target_pairs={{0,4},{4,0},{1,5},{5,1},{2,6},{6,2},{3,7},{7,3},{8,12},{12,8},{9,1... | collective-permute-start | bytes 7077896 | tf_op jit(solution)/shard_map/ppermute | solution.py:1546
  444.4 30.7 %collective-permute-start.28 = (bf16[384,1536]{1,0:T(8,128)(2,1)}, bf16[384,1536]{1,0:T(8,128)(2,1)S(1)}, u32[]{:S(2)}, u32[]{:S(2)}) collective-permute-start(bf16[384,1536]{1,0:T(8,128)(2,1)} %reduce-scatter.6.cloned.1.call-done), channel_id=1, source_target_pairs={{0,1},{1,2},{2,3},{3,0},{4,5},{5,6},{6,7},{7,4},{8,9},{9,10},{10,1... | collective-permute-start | bytes 3538952 | tf_op jit(solution)/shard_map/ppermute | solution.py:1305
  475.1 66.2 %slice-start = ((s8[4718592]{0:T(1024)(128)(4,1)}), s8[4194304]{0:T(1024)(128)(4,1)S(1)}, s32[]{:S(2)}) async-start(s8[4718592]{0:T(1024)(128)(4,1)} %bitcast.120), calls=%async_computation.15 | async-start | bytes 8388608
  489.1 52.3 %slice-start.1 = ((s8[4718592]{0:T(1024)(128)(4,1)}), s8[524288]{0:T(1024)(128)(4,1)S(1)}, s32[]{:S(2)}) async-start(s8[4718592]{0:T(1024)(128)(4,1)} %bitcast.120), calls=%async_computation.16 | async-start | bytes 1048576
  489.1 45.6 %collective-permute-start.29 = (bf16[256,1536]{1,0:T(8,128)(2,1)}, bf16[256,1536]{1,0:T(8,128)(2,1)}, u32[]{:S(2)}, u32[]{:S(2)}) collective-permute-start(bf16[256,1536]{1,0:T(8,128)(2,1)} %slice_bitcast_fusion.4), channel_id=1, source_target_pairs={{0,3},{1,0},{2,1},{3,2},{4,7},{5,4},{6,5},{7,6},{8,11},{9,8},{10,9... | collective-permute-start | bytes 2359304 | tf_op jit(solution)/shard_map/ppermute | solution.py:1305
  543.6 156.9 %reduce-scatter.10.cloned.1.call-start = ((), (), s32[]{:S(2)}) async-start(), calls=%async_computation.12 | async-start | bytes 5898240 | tf_op jit(solution)/shard_map/reduce_scatter | solution.py:1773
  545.2 21.0 %collective-permute-start.30 = (bf16[256,1536]{1,0:T(8,128)(2,1)S(1)}, bf16[256,1536]{1,0:T(8,128)(2,1)S(1)}, u32[]{:S(2)}, u32[]{:S(2)}) collective-permute-start(bf16[256,1536]{1,0:T(8,128)(2,1)S(1)} %fusion.5), channel_id=1, source_target_pairs={{0,3},{1,0},{2,1},{3,2},{4,7},{5,4},{6,5},{7,6},{8,11},{9,8},{10,9... | collective-permute-start | bytes 2359304 | tf_op jit(solution)/shard_map/ppermute | solution.py:1305
  545.3 202.5 %reduce-scatter.12.cloned.1.call-start = ((), (), s32[]{:S(2)}) async-start(), calls=%async_computation.13 | async-start | bytes 3194880 | tf_op jit(solution)/shard_map/reduce_scatter | solution.py:1911
  547.9 105.2 %collective-permute-start.33 = (bf16[384,1536]{1,0:T(8,128)(2,1)}, bf16[384,1536]{1,0:T(8,128)(2,1)}, u32[]{:S(2)}, u32[]{:S(2)}) collective-permute-start(bf16[384,1536]{1,0:T(8,128)(2,1)} %add_convert_fusion.1), channel_id=1, source_target_pairs={{0,1},{1,2},{2,3},{3,0},{4,5},{5,6},{6,7},{7,4},{8,9},{9,10},{10,1... | collective-permute-start | bytes 3538952 | tf_op jit(solution)/shard_map/ppermute | solution.py:1305
  549.9 103.2 %collective-permute-start.34 = (bf16[768,1536]{1,0:T(8,128)(2,1)}, bf16[768,1536]{1,0:T(8,128)(2,1)}, u32[]{:S(2)}, u32[]{:S(2)}) collective-permute-start(bf16[768,1536]{1,0:T(8,128)(2,1)} %weight_grads.2), channel_id=1, source_target_pairs={{0,16},{16,0},{1,17},{17,1},{2,18},{18,2},{3,19},{19,3},{4,20},{20... | collective-permute-start | bytes 7077896 | tf_op jit(solution)/shard_map/ppermute | solution.py:1546
  567.5 58.5 %collective-permute-start.31 = (bf16[256,1536]{1,0:T(8,128)(2,1)S(1)}, bf16[256,1536]{1,0:T(8,128)(2,1)S(1)}, u32[]{:S(2)}, u32[]{:S(2)}) collective-permute-start(bf16[256,1536]{1,0:T(8,128)(2,1)S(1)} %fusion.4), channel_id=1, source_target_pairs={{0,3},{1,0},{2,1},{3,2},{4,7},{5,4},{6,5},{7,6},{8,11},{9,8},{10,9... | collective-permute-start | bytes 2359304 | tf_op jit(solution)/shard_map/ppermute | solution.py:1305
  603.5 44.7 %collective-permute-start.32 = (bf16[256,1536]{1,0:T(8,128)(2,1)S(1)}, bf16[256,1536]{1,0:T(8,128)(2,1)}, u32[]{:S(2)}, u32[]{:S(2)}) collective-permute-start(bf16[256,1536]{1,0:T(8,128)(2,1)S(1)} %slice_bitcast_fusion.3), channel_id=1, source_target_pairs={{0,3},{1,0},{2,1},{3,2},{4,7},{5,4},{6,5},{7,6},{8,11},{9,8},{10,9... | collective-permute-start | bytes 2359304 | tf_op jit(solution)/shard_map/ppermute | solution.py:1305
  648.2 28.0 %collective-permute-start.40 = (bf16[768,1544]{0,1:T(8,128)(2,1)}, bf16[768,1544]{0,1:T(8,128)(2,1)}, u32[]{:S(2)}, u32[]{:S(2)}) collective-permute-start(bf16[768,1544]{0,1:T(8,128)(2,1)} %copy.84), channel_id=1, source_target_pairs={{0,4},{4,0},{1,5},{5,1},{2,6},{6,2},{3,7},{7,3},{8,12},{12,8},{9,1... | collective-permute-start | bytes 7114760 | tf_op jit(solution)/shard_map/ppermute | solution.py:1546
  649.8 20.6 %collective-permute-start.36 = (bf16[256,1536]{1,0:T(8,128)(2,1)S(1)}, bf16[256,1536]{1,0:T(8,128)(2,1)S(1)}, u32[]{:S(2)}, u32[]{:S(2)}) collective-permute-start(bf16[256,1536]{1,0:T(8,128)(2,1)S(1)} %fusion.3), channel_id=1, source_target_pairs={{0,3},{1,0},{2,1},{3,2},{4,7},{5,4},{6,5},{7,6},{8,11},{9,8},{10,9... | collective-permute-start | bytes 2359304 | tf_op jit(solution)/shard_map/ppermute | solution.py:1305
  652.9 56.1 %collective-permute-start.35 = (bf16[512,1536]{1,0:T(8,128)(2,1)}, bf16[512,1536]{1,0:T(8,128)(2,1)}, u32[]{:S(2)}, u32[]{:S(2)}) collective-permute-start(bf16[512,1536]{1,0:T(8,128)(2,1)} %get-tuple-element.191), channel_id=1, source_target_pairs={{0,4},{4,0},{1,5},{5,1},{2,6},{6,2},{3,7},{7,3},{8,12},{12,8},{9,1... | collective-permute-start | bytes 4718600 | tf_op jit(solution)/shard_map/ppermute | solution.py:1546
  658.4 74.2 %collective-permute-start.38 = (bf16[384,1536]{1,0:T(8,128)(2,1)}, bf16[384,1536]{1,0:T(8,128)(2,1)}, u32[]{:S(2)}, u32[]{:S(2)}) collective-permute-start(bf16[384,1536]{1,0:T(8,128)(2,1)} %weight_grads.3), channel_id=1, source_target_pairs={{0,8},{8,0},{1,9},{9,1},{2,10},{10,2},{3,11},{11,3},{4,12},{12,4},... | collective-permute-start | bytes 3538952 | tf_op jit(solution)/shard_map/ppermute | solution.py:1546
  671.7 68.1 %collective-permute-start.37 = (bf16[256,1536]{1,0:T(8,128)(2,1)S(1)}, bf16[256,1536]{1,0:T(8,128)(2,1)}, u32[]{:S(2)}, u32[]{:S(2)}) collective-permute-start(bf16[256,1536]{1,0:T(8,128)(2,1)S(1)} %fusion.2), channel_id=1, source_target_pairs={{0,3},{1,0},{2,1},{3,2},{4,7},{5,4},{6,5},{7,6},{8,11},{9,8},{10,9... | collective-permute-start | bytes 2359304 | tf_op jit(solution)/shard_map/ppermute | solution.py:1305
  684.3 11.8 %collective-permute-start.42 = (bf16[192,384]{1,0:T(8,128)(2,1)S(1)}, bf16[192,384]{1,0:T(8,128)(2,1)S(1)}, u32[]{:S(2)}, u32[]{:S(2)}) collective-permute-start(bf16[192,384]{1,0:T(8,128)(2,1)S(1)} %slice.219), channel_id=1, source_target_pairs={{0,3},{1,0},{2,1},{3,2},{4,7},{5,4},{6,5},{7,6},{8,11},{9,8},{10,9... | collective-permute-start | bytes 442376 | tf_op jit(solution)/shard_map/ppermute | solution.py:1305
  696.1 8.6 %collective-permute-start.43 = (bf16[192,384]{1,0:T(8,128)(2,1)S(1)}, bf16[192,384]{1,0:T(8,128)(2,1)S(1)}, u32[]{:S(2)}, u32[]{:S(2)}) collective-permute-start(bf16[192,384]{1,0:T(8,128)(2,1)S(1)} %add_convert_fusion.3), channel_id=1, source_target_pairs={{0,3},{1,0},{2,1},{3,2},{4,7},{5,4},{6,5},{7,6},{8,11},{9,8},{10,9... | collective-permute-start | bytes 442376 | tf_op jit(solution)/shard_map/ppermute | solution.py:1305
  702.3 30.2 %collective-permute-start.39 = (bf16[384,1536]{1,0:T(8,128)(2,1)S(1)}, bf16[384,1536]{1,0:T(8,128)(2,1)S(1)}, u32[]{:S(2)}, u32[]{:S(2)}) collective-permute-start(bf16[384,1536]{1,0:T(8,128)(2,1)S(1)} %add_convert_fusion), channel_id=1, source_target_pairs={{0,1},{1,2},{2,3},{3,0},{4,5},{5,6},{6,7},{7,4},{8,9},{9,10},{10,1... | collective-permute-start | bytes 3538952 | tf_op jit(solution)/shard_map/ppermute | solution.py:1305
  704.7 27.1 %collective-permute-start.44 = (bf16[192,384]{1,0:T(8,128)(2,1)S(1)}, bf16[192,384]{1,0:T(8,128)(2,1)S(1)}, u32[]{:S(2)}, u32[]{:S(2)}) collective-permute-start(bf16[192,384]{1,0:T(8,128)(2,1)S(1)} %add_convert_fusion.2), channel_id=1, source_target_pairs={{0,3},{1,0},{2,1},{3,2},{4,7},{5,4},{6,5},{7,6},{8,11},{9,8},{10,9... | collective-permute-start | bytes 442376 | tf_op jit(solution)/shard_map/ppermute | solution.py:1305
  739.8 4.1 collective-permute-start.45
  753.1 5.3 collective-permute-start.46
  758.5 7.7 collective-permute-start.47
  (28 other events, 222.9 us)
Sparse Core Ops, SparseCore 0:
  16.0 43.2 all-gather.5
  61.1 57.0 all-gather.7
  162.4 37.8 all-gather.9
  202.0 57.0 all-gather.11
  303.0 67.9 all-gather.13
  373.8 57.0 reduce-scatter.5
  434.0 57.0 reduce-scatter.7
  543.7 55.8 reduce-scatter.13
  602.6 71.3 reduce-scatter.9
  683.4 39.1 reduce-scatter.11
